TPU v7x, 32 devices: a whole 2x2x4 slice. The times are simulated.
32 devices in a mesh: dom: 16 (over z, y, core), orient: 2 (over x).
Axes of the slice: x: 2, y: 2, z: 4, core: 2. Of those that a mesh axis runs over, the one named last changes fastest.
Arguments:
- particles: bfloat16 [256, 64, 128], P(('dom', 'orient')), may hold values from -48 to 48
- slices: bfloat16 [16, 64, 128], P('orient'), may hold values from -5 to 5
- freq_mask: int32 [64, 64], replicated, may hold values 0 or 1
- slice_class: int32 [16], replicated, may hold values from 0 to 7
- slice_orient: int32 [16], replicated, may hold values from 0 to 31
- class_prior: float32 [8], replicated, may hold values from -1 to 1
- orient_prior: float32 [32], replicated, may hold values from -1 to 1
Outputs:
- back_proj: float32 [16, 64, 128], P('orient', 'dom')
- occupancy: float32 [16], P('orient')
- loglik: float32 [256], P(('dom', 'orient'))
All inputs are finite; a program needn't handle non-finite values.
Results may differ from a plain program's by a relative error of at most 0.0034.
Values may be sent and summed in bfloat16 or wider, within the bound.
No kernel may reach another device: no remote copies, remote signals or barrier semaphores. Data moves between devices by JAX's collectives and lax.ppermute only.
A program may use at most 128 MiB of HBM per device.

v0:
```python
import math

import jax
import jax.numpy as jnp
from jax import lax
from jax.sharding import PartitionSpec as P

TS = 16


HIGH = lax.Precision.HIGHEST


def phase_tables(crop, shifts):
    freq = jnp.arange(crop, dtype=jnp.float32) - crop // 2
    offset = jnp.arange(shifts, dtype=jnp.float32) - shifts // 2
    angle = 2.0 * math.pi / crop * freq[:, None] * offset[None, :]
    return (jnp.cos(angle), jnp.sin(angle))


def score_table(cosine, sine):
    upper = jnp.concatenate([cosine, sine], axis=1)
    lower = jnp.concatenate([-sine, cosine], axis=1)
    return jnp.concatenate([upper, lower], axis=0).astype(jnp.bfloat16)


def spread_table(cosine, sine):
    return jnp.concatenate([cosine.T, -sine.T], axis=1).astype(jnp.bfloat16)


def slice_prior(slice_class, slice_orient, class_prior, orient_prior):
    class_hot = (
        slice_class[:, None] == jnp.arange(class_prior.shape[0], dtype=jnp.int32)[None, :]
    ).astype(jnp.float32)
    orient_hot = (
        slice_orient[:, None] == jnp.arange(orient_prior.shape[0], dtype=jnp.int32)[None, :]
    ).astype(jnp.float32)
    return jnp.sum(class_hot * class_prior[None, :], axis=1) + jnp.sum(
        orient_hot * orient_prior[None, :], axis=1
    )


def score_block(parts, block, weight_mask, forward, cosine, sine, prior):
    half = parts.shape[-1] // 2
    x_re = parts[..., :half].astype(jnp.float32)[:, None]
    x_im = parts[..., half:].astype(jnp.float32)[:, None]
    s_re = block[..., :half].astype(jnp.float32)[None]
    s_im = block[..., half:].astype(jnp.float32)[None]
    cross_re = (x_re * s_re + x_im * s_im) * weight_mask
    cross_im = (x_im * s_re - x_re * s_im) * weight_mask
    cross = jnp.concatenate([cross_re, cross_im], axis=-1).astype(jnp.bfloat16)
    rowcorr = jnp.einsum("abyk,kt->abyt", cross, forward, preferred_element_type=jnp.float32)
    shifts = cosine.shape[1]
    corr = jnp.einsum("yu,abyt->abut", cosine, rowcorr[..., :shifts], precision=HIGH) - jnp.einsum(
        "yu,abyt->abut", sine, rowcorr[..., shifts:], precision=HIGH
    )
    power = jnp.sum((s_re * s_re + s_im * s_im) * weight_mask, axis=(2, 3))
    crop = weight_mask.shape[0]
    return (corr - 0.5 * power[:, :, None, None]) / crop + prior[None, :, None, None]


def back_block(parts, weights, weight_mask, spread, cosine, sine):
    half = parts.shape[-1] // 2
    spread_x = jnp.einsum("abuv,vk->abuk", weights, spread, preferred_element_type=jnp.float32)
    a_re = spread_x[..., :half]
    a_im = spread_x[..., half:]
    g_re = jnp.einsum("yu,abuk->abyk", cosine, a_re, precision=HIGH) + jnp.einsum(
        "yu,abuk->abyk", sine, a_im, precision=HIGH
    )
    g_im = jnp.einsum("yu,abuk->abyk", cosine, a_im, precision=HIGH) - jnp.einsum(
        "yu,abuk->abyk", sine, a_re, precision=HIGH
    )
    x_re = parts[..., :half].astype(jnp.float32)[:, None]
    x_im = parts[..., half:].astype(jnp.float32)[:, None]
    b_re = jnp.sum(g_re * x_re - g_im * x_im, axis=0) * weight_mask
    b_im = jnp.sum(g_re * x_im + g_im * x_re, axis=0) * weight_mask
    return jnp.concatenate([b_re, b_im], axis=-1)


def shards(particles, slices, freq_mask, slice_class, slice_orient, class_prior, orient_prior):
    crop = slices.shape[1]
    share = slices.shape[0]
    cosine, sine = phase_tables(crop, TS)
    forward = score_table(cosine, sine)
    spread = spread_table(cosine, sine)
    weight_mask = freq_mask.astype(jnp.float32)
    prior = slice_prior(slice_class, slice_orient, class_prior, orient_prior)
    scores = score_block(
        particles,
        lax.all_gather(slices, "orient", axis=0, tiled=True),
        weight_mask,
        forward,
        cosine,
        sine,
        prior,
    )
    top = jnp.max(scores, axis=(1, 2, 3))
    loglik = top + jnp.log(jnp.sum(jnp.exp(scores - top[:, None, None, None]), axis=(1, 2, 3)))
    weights = jnp.exp(scores - loglik[:, None, None, None]).astype(jnp.bfloat16)
    mass_part = jnp.sum(weights.astype(jnp.float32), axis=(0, 2, 3))
    mass_all = lax.psum(mass_part, ("dom", "orient"))
    own = lax.axis_index("orient")
    occupancy = lax.dynamic_slice_in_dim(mass_all, own * share, share)
    mine = lax.psum_scatter(
        back_block(particles, weights, weight_mask, spread, cosine, sine),
        "orient",
        scatter_dimension=0,
        tiled=True,
    )
    image = lax.psum_scatter(mine, "dom", scatter_dimension=1, tiled=True)
    return (image, occupancy, loglik)


def solution(mesh):
    placed = (P(("dom", "orient"), None, None), P("orient", None, None), P(), P(), P(), P(), P())
    return jax.shard_map(
        shards,
        mesh=mesh,
        in_specs=placed,
        out_specs=(P("orient", "dom", None), P("orient"), P(("dom", "orient"))),
        check_vma=False,
    )
```

profile of v0, /device:TPU:0, one launch (start us, length us, event | category | flops | bytes accessed | tf_op | source)
XLA Modules:
  0.0 125.8 jit_solution(7963805782147708149)
XLA Ops:
  7.5 0.8 convert_element_type.32
  8.2 7.4 %all_gather.3 = bf16[16,64,128]{2,1,0:T(8,128)(2,1)S(1)} all-gather(bf16[8,64,128]{2,1,0:T(8,128)(2,1)} %param.8), channel_id=1, replica_groups=mesh['dom'=16,'orient'=2] {'orient'}, dimensions={0}, use_global_device_ids=true | all-gather | bytes 393216 | tf_op jit(solution)/shard_map/all_gather | solution.py:90
  15.6 0.2 slice_convert_fusion.1
  15.8 0.3 multiply_reduce_fusion
  16.1 1.1 slice_convert_fusion.3
  17.2 1.4 %multiply_convert_fusion.1 = (bf16[8,16,64,64]{3,2,1,0:T(8,128)(2,1)S(1)}, bf16[8,16,64,64]{3,2,1,0:T(8,128)(2,1)S(1)}) fusion(f32[64,64]{1,0:T(8,128)S(1)} %convert_element_type.32, f32[16,64,64]{2,1,0:T(8,128)S(1)} %get-tuple-element.14, f32[8,64,64]{2,1,0:T(8,128)S(1)} %get-tuple-element.16, f32[16,64,64]{2,1,0:T(8,128)S(1)} %get-tuple-element.13, ...), kind=kLoop, calls=%fused_computation.9 | loop fusion | flops 5242880 | bytes 2899968 | tf_op jit(solution)/shard_map/convert.8
  18.6 2.1 %fusion.4 = f32[8,16,64,32]{2,3,1,0:T(8,128)S(1)} fusion(bf16[8,16,64,64]{3,2,1,0:T(8,128)(2,1)S(1)} %get-tuple-element.12, bf16[8,16,64,64]{3,2,1,0:T(8,128)(2,1)S(1)} %get-tuple-element.11, bf16[64,16]{0,1:T(8,128)(2,1)S(1)} %get-tuple-element.21, bf16[64,16]{0,1:T(8,128)(2,1)S(1)} %get-tuple-element.20, bf16[64,16]{0,1:T(8,128)(2,1)S(1)} %get-tuple-element.19), kind=kOutput, calls=%fused_computation.12 | convolution fusion | flops 71335936 | bytes 3151872 | tf_op jit(solution)/shard_map/abyk,kt->abyt/dot_general | solution.py:52
  20.7 1.1 fusion.12
  21.9 0.2 select_reduce_fusion
  22.1 1.3 %fusion.60 = (f32[8]{0:T(128)S(1)}, f32[8,16,16,16]{3,2,1,0:T(8,128)S(1)}) fusion(f32[16]{0:T(128)S(1)} %add.62, f32[16]{0:T(128)S(1)} %broadcast_multiply_fusion.2, f32[8,16,16,16]{3,2,1,0:T(8,128)S(1)} %fusion.12, f32[16]{0:T(128)S(1)} %iota_add_fusion, f32[64]{0:T(128)S(1)} %add_multiply_fusion, f32[8,16,64,32]{2,3,1,0:T(8,128)S(1)} %fusion.4), kind=kOutput, calls=%fused_computation.87 | convolution fusion | flops 25330680 | bytes 2230304 | tf_op jit(solution)/shard_map/yu,abyt->abut/dot_general | solution.py:54
  23.4 0.3 exponential_reduce_fusion
  23.8 0.5 fusion.42
  24.2 3.6 %fusion.14 = f32[8,16,64,64]{2,3,1,0:T(8,128)S(1)} fusion(f32[8,16,16,128]{3,2,1,0:T(8,128)S(1)} %fusion.42, f32[16]{0:T(128)S(1)} %iota_add_fusion, f32[64]{0:T(128)S(1)} %add_multiply_fusion), kind=kOutput, calls=%fused_computation.26 | convolution fusion | flops 100664320 | bytes 3146048 | tf_op jit(solution)/shard_map/yu,abuk->abyk/dot_general | solution.py:70
  27.9 3.8 %fusion.18 = f32[8,16,64,64]{2,3,1,0:T(8,128)S(1)} fusion(f32[8,16,16,128]{3,2,1,0:T(8,128)S(1)} %fusion.42, f32[16]{0:T(128)S(1)} %iota_add_fusion, f32[64]{0:T(128)S(1)} %add_multiply_fusion), kind=kOutput, calls=%fused_computation.30 | convolution fusion | flops 100664320 | bytes 3146048 | tf_op jit(solution)/shard_map/yu,abuk->abyk/dot_general | solution.py:67
  31.7 3.6 %convolution_add_fusion = f32[8,16,64,64]{2,3,1,0:T(8,128)S(1)} fusion(f32[8,16,64,64]{2,3,1,0:T(8,128)S(1)} %fusion.18, f32[8,16,16,128]{3,2,1,0:T(8,128)S(1)} %fusion.42, f32[16]{0:T(128)S(1)} %iota_add_fusion, f32[64]{0:T(128)S(1)} %add_multiply_fusion), kind=kOutput, calls=%fused_computation.11 | convolution fusion | flops 101188608 | bytes 5243200 | tf_op jit(solution)/shard_map/yu,abuk->abyk/dot_general | solution.py:67
  35.3 5.7 %fusion.1 = (f32[16,64,64]{2,1,0:T(8,128)S(1)}, f32[16,64,64]{2,1,0:T(8,128)S(1)}) fusion(f32[8,16,64,64]{2,3,1,0:T(8,128)S(1)} %convolution_add_fusion, f32[8,64,64]{2,1,0:T(8,128)S(1)} %get-tuple-element.16, f32[8,64,64]{2,1,0:T(8,128)S(1)} %get-tuple-element.15, f32[8,16,64,64]{2,3,1,0:T(8,128)S(1)} %fusion.14, f32[16]{0:T(128)S(1)} %iota_add_fusion, ...), kind=kOutput, calls=%fused_computation.3 | convolution fusion | flops 105251840 | bytes 6029632 | tf_op jit(solution)/shard_map/yu,abuk->abyk/dot_general | solution.py:70
  41.2 1.0 pad_maximum_fusion
  42.2 16.1 %reduce-scatter.3.cloned.1.call-done = f32[8,64,128]{2,1,0:T(8,128)} async-done(((f32[16,64,128]{2,1,0:T(8,128)}), f32[8,64,128]{2,1,0:T(8,128)}) %reduce-scatter.3.cloned.1.call-update) | async-done | bytes 262160 | tf_op jit(solution)/shard_map/reduce_scatter | solution.py:104
  58.4 1.8 %copy.27 = f32[8,64,128]{2,0,1:T(8,128)} copy(f32[8,64,128]{2,1,0:T(8,128)} %reduce-scatter.3.cloned.1.call-done) | data formatting | bytes 524288 | tf_op jit(solution)/shard_map/reduce_scatter | solution.py:104
  60.2 0.4 convert_reduce_fusion
  60.6 39.4 %psum.7 = f32[16]{0:T(128)S(1)} all-reduce(f32[16]{0:T(128)S(1)} %convert_reduce_fusion), channel_id=1, replica_groups=mesh['dom'=16,'orient'=2] {'dom','orient'}, use_global_device_ids=true, to_apply=%region_10.0 | all-reduce | flops 16 | bytes 128 | tf_op jit(solution)/shard_map/psum | solution.py:101
  99.9 0.6 dynamic_slice.3
  100.5 17.1 %reduce-scatter.5.cloned.1.call-done = f32[8,4,128]{2,0,1:T(8,128)} async-done(((f32[8,64,128]{2,0,1:T(8,128)}), f32[8,4,128]{2,0,1:T(8,128)}) %reduce-scatter.5.cloned.1.call-update) | async-done | bytes 16400 | tf_op jit(solution)/shard_map/reduce_scatter | solution.py:110
  117.6 1.3 %copy.28 = f32[8,4,128]{2,1,0:T(4,128)} copy(f32[8,4,128]{2,0,1:T(8,128)} %reduce-scatter.5.cloned.1.call-done) | data formatting | bytes 32768
  (23 shorter events, 0.6 us)
Async XLA Ops:
  7.2 51.2 %reduce-scatter.3.cloned.1.call-start = ((), (), s32[]{:S(2)}) async-start(), calls=%async_computation.2 | async-start | bytes 786432 | tf_op jit(solution)/shard_map/reduce_scatter | solution.py:104
  18.6 3.3 %copy-start.1 = (f32[8]{0:T(128)S(1)}, f32[8]{0:T(128)}, u32[]{:S(2)}) copy-start(f32[8]{0:T(128)} %param.12) | copy-start | bytes 100
  18.6 3.3 %copy-start.2 = (s32[16]{0:T(128)S(1)}, s32[16]{0:T(128)}, u32[]{:S(2)}) copy-start(s32[16]{0:T(128)} %param.10) | copy-start | bytes 196
  18.6 3.3 %copy-start.3 = (f32[32]{0:T(128)S(1)}, f32[32]{0:T(128)}, u32[]{:S(2)}) copy-start(f32[32]{0:T(128)} %param.13) | copy-start | bytes 388
  18.6 3.3 %copy-start.4 = (s32[16]{0:T(128)S(1)}, s32[16]{0:T(128)}, u32[]{:S(2)}) copy-start(s32[16]{0:T(128)} %param.11) | copy-start | bytes 196
  23.8 36.4 %copy-start = (f32[8]{0:T(128)}, f32[8]{0:T(128)S(1)}, u32[]{:S(2)}) copy-start(f32[8]{0:T(128)S(1)} %log_add_fusion) | copy-start | bytes 100
  42.2 75.4 %reduce-scatter.5.cloned.1.call-start = ((), (), s32[]{:S(2)}) async-start(), calls=%async_computation.3 | async-start | bytes 278528 | tf_op jit(solution)/shard_map/reduce_scatter | solution.py:110
Sparse Core Ops, SparseCore 0:
  42.3 15.9 reduce-scatter.2
  62.3 55.2 reduce-scatter.4
where the time goes:
time: 126 us
  blocking collectives  46.7 us (37%)
  waiting for transfers between devices  33.3 us (26%)
  matrix products  21.7 us (17%)
  between operations  14.2 us (11%)
  other arithmetic  6.06 us (5%)
  local copies, waits for them, and re-layouts  3.73 us (3%)
    psum x1, blocking collectives, shards(): mass_all = lax.psum(mass_part, ('dom', 'orient'))  39.4 us
    reduce_scatter x1, waiting for transfers between devices, shards(): image = lax.psum_scatter(mine, 'dom', scatter_dimension=1, tiled=True)  17.1 us
    reduce_scatter x1, waiting for transfers between devices, shards(): lax.psum_scatter(back_block(particles, weights, weight_mask, spread, cosi...  16.1 us
    all_gather x1, blocking collectives, shards(): lax.all_gather(slices, 'orient', axis=0, tiled=True)  7.35 us
    dot_general x1, matrix products, back_block(): jnp.einsum('yu,abuk->abyk', sine, a_re, precision=HIGH)  5.71 us
    dot_general x1, matrix products, back_block(): jnp.einsum('yu,abuk->abyk', cosine, a_re, precision=HIGH)  3.83 us
    dot_general x1, matrix products, back_block(): jnp.einsum('yu,abuk->abyk', sine, a_im, precision=HIGH)  3.63 us
    dot_general x1, matrix products, back_block(): jnp.einsum('yu,abuk->abyk', cosine, a_im, precision=HIGH)  3.61 us
  transfers between devices with their start and end apart: 2, of which 2 were waited for; matrix products, arithmetic and copies ran while one was open for 1% of the time, Pallas kernels for 0%

commit v1 on v0

v1 whole, which is shorter than its diff:
```python
import functools
import math

import jax
import jax.numpy as jnp
import ml_dtypes
import numpy as np
from jax import lax
from jax.experimental import pallas as pl
from jax.experimental.pallas import tpu as pltpu
from jax.sharding import PartitionSpec as P

TS = 16
F32 = jnp.float32
BF16 = jnp.bfloat16
VMEM_LIMIT = 24 * 1024 * 1024


def phase_tables(crop):
    freq = np.arange(crop, dtype=np.float64) - crop // 2
    offset = np.arange(TS, dtype=np.float64) - TS // 2
    angle = 2.0 * math.pi / crop * freq[:, None] * offset[None, :]
    return np.cos(angle).astype(np.float32), np.sin(angle).astype(np.float32)


def high_low(table):
    high = table.astype(ml_dtypes.bfloat16)
    low = (table - high.astype(np.float32)).astype(ml_dtypes.bfloat16)
    return high, low


def score_tables(crop, share):
    cosine, sine = phase_tables(crop)
    rows = np.zeros((share, 2, crop, 2, share, TS), np.float32)
    for j in range(share):
        rows[j, 0, :, 0, j] = cosine
        rows[j, 0, :, 1, j] = sine
        rows[j, 1, :, 0, j] = -sine
        rows[j, 1, :, 1, j] = cosine
    rows = rows.reshape(share * 2 * crop, 2 * share * TS).astype(ml_dtypes.bfloat16)
    high, low = high_low(np.concatenate([cosine.T, -sine.T], axis=1))
    columns = np.concatenate(
        [np.concatenate([high, high], axis=1), np.concatenate([low, np.zeros_like(low)], axis=1)], axis=0
    )
    return rows, columns


def back_tables(crop, share, order):
    cosine, sine = phase_tables(crop)
    rows = np.zeros((share, TS, 2, share, 2, crop), np.float32)
    for place, j in enumerate(order):
        rows[j, :, 0, place, 0] = cosine.T
        rows[j, :, 0, place, 1] = -sine.T
        rows[j, :, 1, place, 0] = -sine.T
        rows[j, :, 1, place, 1] = -cosine.T
    rows = rows.reshape(share * TS, 2 * share * 2 * crop).astype(ml_dtypes.bfloat16)
    high, low = high_low(np.concatenate([cosine, sine], axis=1))
    return rows, np.concatenate([high, high, low], axis=1)


def both_halves(mask_ref):
    mask = mask_ref[...].astype(F32)
    return jnp.concatenate([mask, mask], axis=1)


def score_kernel(
    share,
    own_ref,
    class_ref,
    orient_ref,
    class_prior_ref,
    orient_prior_ref,
    x_ref,
    s_ref,
    mask_ref,
    rows_ref,
    columns_ref,
    logits_ref,
    lse_ref,
    cross,
    first,
    second,
    plain,
    swapped,
):
    count, crop, width = x_ref.shape
    half = width // 2
    mask = both_halves(mask_ref)
    left = lax.broadcasted_iota(jnp.int32, (crop, width), 1) < half
    slot = lax.broadcasted_iota(jnp.int32, (1, share * TS), 1) // TS
    bias = jnp.zeros((1, share * TS), F32)
    start = own_ref[0] * share
    for j in range(share):
        s = s_ref[j].astype(F32) * mask
        turned = pltpu.roll(s, half, 1)
        first[j] = jnp.where(left, s, turned)
        second[j] = jnp.where(left, turned, -s)
        power = jnp.sum(s * s)
        prior = class_prior_ref[class_ref[start + j]] + orient_prior_ref[orient_ref[start + j]]
        bias = jnp.where(slot == j, prior - power * (0.5 / crop), bias)
    for i in range(count):
        x = x_ref[i].astype(F32)
        plain[i] = x
        swapped[i] = pltpu.roll(x, half, 1)
    for at in range(0, crop, 16):
        for j in range(share):
            a, b = first[j, at : at + 16], second[j, at : at + 16]
            for i in range(count):
                value = plain[i, at : at + 16] * a + swapped[i, at : at + 16] * b
                cross[i * crop + at : i * crop + at + 16, j * width : (j + 1) * width] = value.astype(BF16)
    rowcorr = jnp.dot(cross[...], rows_ref[...], preferred_element_type=F32)
    high = rowcorr.astype(BF16)
    low = (rowcorr - high.astype(F32)).astype(BF16)
    lanes = share * TS
    stacked = jnp.concatenate(
        [
            jnp.concatenate(
                [part[i * crop : (i + 1) * crop, k * lanes : (k + 1) * lanes] for part in (high, low) for k in (0, 1)],
                axis=0,
            )
            for i in range(count)
        ],
        axis=1,
    )
    corr = jnp.dot(columns_ref[...], stacked, preferred_element_type=F32)
    corr = (corr[:TS] + corr[TS:]) * (1.0 / crop)
    for i in range(count):
        logits = corr[:, i * lanes : (i + 1) * lanes] + bias
        logits_ref[i] = logits
        top = jnp.max(logits, keepdims=True)
        total = jnp.sum(jnp.exp(logits - top), keepdims=True)
        lse_ref[i : i + 1, :] = jnp.broadcast_to(top + jnp.log(total), (1, lse_ref.shape[1]))


def back_kernel(n, share, pack, *refs):
    logits_refs, x_refs = refs[:n], refs[n : 2 * n]
    lse_ref, mask_ref, rows_ref, columns_ref, out_ref, mass_ref, doubled_re, doubled_im, high, low = refs[2 * n :]
    count, crop, width = x_refs[0].shape
    half = width // 2
    left = lax.broadcasted_iota(jnp.int32, (crop, width), 1) < half
    sign = jnp.where(left[:1], -1.0, 1.0)
    mask = both_halves(mask_ref)
    mass = jnp.zeros((1, share * TS), F32)
    for r in range(n):
        weights = []
        for i in range(count):
            k = r * count + i
            weight = jnp.exp(logits_refs[r][i] - lse_ref[k : k + 1, :]).astype(BF16)
            mass = mass + jnp.sum(weight.astype(F32), axis=0, keepdims=True)
            weights.append(weight)
            x = x_refs[r][i].astype(F32)
            turned = pltpu.roll(x, half, 1)
            doubled_re[k] = jnp.where(left, x, turned)
            doubled_im[k] = jnp.where(left, turned, x)
        spread = jnp.dot(jnp.concatenate(weights, axis=0), rows_ref[...], preferred_element_type=F32)
        rounded = spread.astype(BF16)
        span = slice(r * count * TS, (r + 1) * count * TS)
        high[span] = rounded
        low[span] = (spread - rounded.astype(F32)).astype(BF16)
    mass_ref[...] = jnp.broadcast_to(mass, mass_ref.shape)
    forms = share * width
    wide = pack * width
    columns = columns_ref[...]
    for group in range(share // pack):
        re = jnp.zeros((crop, wide), F32)
        im = jnp.zeros((crop, wide), F32)
        for k in range(n * count):
            rows = slice(k * TS, (k + 1) * TS)
            here = slice(group * wide, (group + 1) * wide)
            there = slice(forms + group * wide, forms + (group + 1) * wide)
            a, b = high[rows, here], high[rows, there]
            terms = jnp.concatenate([a, b, low[rows, here], low[rows, there], a, b], axis=0)
            kernel = jnp.dot(columns, terms, preferred_element_type=F32)
            x_re, x_im = doubled_re[k], doubled_im[k]
            re = re + kernel * jnp.concatenate([x_re] * pack, axis=1)
            im = im + kernel * jnp.concatenate([x_im] * pack, axis=1)
        images = []
        for p in range(pack):
            here = slice(p * width, (p + 1) * width)
            images.append((re[:, here] + pltpu.roll(im[:, here], half, 1) * sign) * mask)
        block = 8 // pack
        for tile in range(crop // 8):
            for b in range(pack):
                rows = slice(tile * 8 + b * block, tile * 8 + (b + 1) * block)
                out_ref[tile * pack + b, group] = jnp.concatenate([image[rows] for image in images], axis=0)


def log_add(a, b):
    top = jnp.maximum(a, b)
    return top + jnp.log(jnp.exp(a - top) + jnp.exp(b - top))


def bits(count):
    return count.bit_length() - 1


def shards(n_dom, n_orient, particles, slices, freq_mask, slice_class, slice_orient, class_prior, orient_prior):
    count, crop, width = particles.shape
    share = slices.shape[0]
    lanes = share * TS
    block = crop // n_dom
    pack = 8 // block
    smem = pl.BlockSpec(memory_space=pltpu.SMEM)
    vmem = pl.BlockSpec(memory_space=pltpu.VMEM)
    own = lax.axis_index("orient")
    me = lax.axis_index("dom")
    score_rows, score_columns = score_tables(crop, share)
    groups = share // pack
    order = [p * groups + g for g in range(groups) for p in range(pack)]
    back_rows, back_columns = back_tables(crop, share, order)

    def swap(value, axis, size, step):
        return lax.ppermute(value, axis, [(i, i ^ step) for i in range(size)])

    flops = 2 * count * crop * share * width * 2 * lanes
    score = pl.pallas_call(
        functools.partial(score_kernel, share),
        out_shape=(
            jax.ShapeDtypeStruct((count, TS, lanes), F32),
            jax.ShapeDtypeStruct((count, 128), F32),
        ),
        in_specs=[smem] * 5 + [vmem] * 5,
        out_specs=(vmem, vmem),
        scratch_shapes=[
            pltpu.VMEM((count * crop, share * width), BF16),
            pltpu.VMEM((share, crop, width), F32),
            pltpu.VMEM((share, crop, width), F32),
            pltpu.VMEM((count, crop, width), F32),
            pltpu.VMEM((count, crop, width), F32),
        ],
        compiler_params=pltpu.CompilerParams(vmem_limit_bytes=VMEM_LIMIT),
        cost_estimate=pl.CostEstimate(flops=flops, bytes_accessed=1 << 20, transcendentals=count * TS * lanes),
        name="score",
    )

    def scores(parts):
        return score(
            own[None].astype(jnp.int32), slice_class, slice_orient, class_prior, orient_prior,
            parts, slices, freq_mask, jnp.asarray(score_rows), jnp.asarray(score_columns),
        )

    slots = [particles] + [swap(particles, "orient", n_orient, r) for r in range(1, n_orient)]
    scored = [scores(parts) for parts in slots]
    lse = jnp.stack([s[1] for s in scored])
    for b in range(bits(n_orient)):
        theirs = swap(lse, "orient", n_orient, 1 << b)
        lse = log_add(lse, jnp.stack([theirs[r ^ (1 << b)] for r in range(n_orient)]))
    loglik = lse[0, :, 0]

    total = n_orient * count
    terms, mass = pl.pallas_call(
        functools.partial(back_kernel, n_orient, share, pack),
        out_shape=(
            jax.ShapeDtypeStruct((n_dom, groups, 8, width), F32),
            jax.ShapeDtypeStruct((8, lanes), F32),
        ),
        in_specs=[vmem] * (2 * n_orient + 4),
        out_specs=(vmem, vmem),
        scratch_shapes=[
            pltpu.VMEM((total, crop, width), F32),
            pltpu.VMEM((total, crop, width), F32),
            pltpu.VMEM((total * TS, 2 * share * width), BF16),
            pltpu.VMEM((total * TS, 2 * share * width), BF16),
        ],
        compiler_params=pltpu.CompilerParams(vmem_limit_bytes=VMEM_LIMIT),
        name="back",
    )(
        *[s[0] for s in scored], *slots, lse.reshape(total, 128), freq_mask,
        jnp.asarray(back_rows), jnp.asarray(back_columns),
    )

    mass = jnp.sum(mass[0].reshape(share, TS), axis=1)
    mass = jnp.pad(mass[None, :], ((0, 0), (0, 128 - share)))
    for b in range(bits(n_dom)):
        halves = terms.reshape(terms.shape[0] // 2, 2, *terms.shape[1:])
        bit = (me >> b) & 1
        keep = lax.dynamic_index_in_dim(halves, bit, 1, keepdims=False)
        send = lax.dynamic_index_in_dim(halves, 1 - bit, 1, keepdims=False).astype(BF16)
        high = mass.astype(BF16)
        middle = (mass - high.astype(F32)).astype(BF16)
        low = (mass - high.astype(F32) - middle.astype(F32)).astype(BF16)
        tail = jnp.concatenate([high, middle, low, jnp.zeros((13, 128), BF16)], axis=0).reshape(2, 8, 128)
        got = swap(jnp.concatenate([send.reshape(-1, 8, width), tail], axis=0), "dom", n_dom, 1 << b).astype(F32)
        terms = keep + got[:-2].reshape(keep.shape)
        mass = mass + got[-2, 0:1] + got[-2, 1:2] + got[-2, 2:3]
    image = terms[0].reshape(groups, pack, block, width).transpose(1, 0, 2, 3).reshape(share, block, width)
    return image, mass[0, :share], loglik


def solution(mesh):
    placed = (P(("dom", "orient"), None, None), P("orient", None, None), P(), P(), P(), P(), P())
    return jax.shard_map(
        functools.partial(shards, mesh.shape["dom"], mesh.shape["orient"]),
        mesh=mesh,
        in_specs=placed,
        out_specs=(P("orient", "dom", None), P("orient"), P(("dom", "orient"))),
        check_vma=False,
    )
```

time: 126 us -> 35.2 us (0.28)
  blocking collectives: 46.7 us -> 0 us
  waiting for transfers between devices: 33.3 us -> 10.8 us
  matrix products: 21.7 us -> 0 us
  between operations: 14.2 us -> 0.92 us
  starting transfers between devices: 0.08 us -> 8.92 us
  Pallas kernels: 0 us -> 6.6 us
  other arithmetic: 6.06 us -> 1.26 us
  local copies, waits for them, and re-layouts: 3.73 us -> 6.42 us
    psum x1 -> x0, blocking collectives: 39.4 us -> none  [shards(): mass_all = lax.psum(mass_part, ('dom', 'orient'))]
    reduce_scatter x2 -> x0, waiting for transfers between devices: 33.2 us -> none  [the longest x1 17.1 us: shards(): image = lax.psum_scatter(mine, 'dom', scatter_dimension=1, tiled=True)]
    dot_general x8 -> x0, matrix products: 21.7 us -> none  [the longest x1 5.71 us: back_block(): jnp.einsum('yu,abuk->abyk', sine, a_re, precision=HIGH)]
    ppermute x0 -> x6, waiting for transfers between devices: none -> 10.8 us  [swap(): return lax.ppermute(value, axis, [(i, i ^ step) for i in range(size)])]
    ppermute x0 -> x6, starting transfers between devices: none -> 8.92 us  [swap(): return lax.ppermute(value, axis, [(i, i ^ step) for i in range(size)])]
    all_gather x1 -> x0, blocking collectives: 7.35 us -> none  [shards(): lax.all_gather(slices, 'orient', axis=0, tiled=True)]
    pallas_call x0 -> x3, Pallas kernels: none -> 6.6 us  [the longest x2 5.24 us: scores(): score(own[None].astype(jnp.int32), slice_class, slice_orient, class_prior...]
    unnamed x11 -> x30, local copies, waits for them, and re-layouts: 1.35 us -> 5 us
  transfers between devices with their start and end apart: 2 -> 6, of which waited for: 2 -> 5; matrix products, arithmetic and copies ran while one was open for 1% -> 2% of each run, Pallas kernels for 0% -> 7%
where the time goes in v1:
time: 35.2 us; the launch traced here: 34.9 us
  waiting for transfers between devices  10.8 us (31%)
  starting transfers between devices  8.92 us (25%)
  Pallas kernels  6.6 us (19%)
  local copies, waits for them, and re-layouts  6.42 us (18%)
  other arithmetic  1.26 us (4%)
  between operations  0.92 us (3%)
    ppermute x6, waiting for transfers between devices, swap(): return lax.ppermute(value, axis, [(i, i ^ step) for i in range(size)])  10.8 us
    ppermute x6, starting transfers between devices, swap(): return lax.ppermute(value, axis, [(i, i ^ step) for i in range(size)])  8.92 us
    pallas_call x2, Pallas kernels, scores(): score(own[None].astype(jnp.int32), slice_class, slice_orient, class_prior...  5.24 us
    unnamed x30, local copies, waits for them, and re-layouts  5 us
    pallas_call x1, Pallas kernels, shards(): pl.pallas_call(functools.partial(back_kernel, n_orient, share, pack), out...  1.35 us
  transfers between devices with their start and end apart: 6, of which 5 were waited for; matrix products, arithmetic and copies ran while one was open for 2% of the time, Pallas kernels for 7%

profile of v1, /device:TPU:0, one launch (start us, length us, event | category | flops | bytes accessed | tf_op | source)
XLA Modules:
  0.0 34.9 jit_solution(1685411824415040462)
XLA Ops:
  0.6 3.0 %collective-permute-start = (bf16[8,64,128]{2,1,0:T(8,128)(2,1)}, bf16[8,64,128]{2,1,0:T(8,128)(2,1)S(1)}, u32[]{:S(2)}, u32[]{:S(2)}) collective-permute-start(bf16[8,64,128]{2,1,0:T(8,128)(2,1)} %refs_2_.1), channel_id=1, source_target_pairs={{0,1},{1,0},{2,3},{3,2},{4,5},{5,4},{6,7},{7,6},{8,9},{9,8},{10,11... | collective-permute-start | bytes 393224 | tf_op jit(solution)/shard_map/ppermute | solution.py:213
  3.7 0.6 %copy-done.11 = f32[32]{0:T(128)S(1)} copy-done((f32[32]{0:T(128)S(1)}, f32[32]{0:T(128)}, u32[]{:S(2)}) %copy-start.11) | copy-done | bytes 152
  4.4 0.9 %copy-done.1 = bf16[8,64,128]{2,1,0:T(8,128)(2,1)S(1)} copy-done((bf16[8,64,128]{2,1,0:T(8,128)(2,1)S(1)}, bf16[8,64,128]{2,1,0:T(8,128)(2,1)}, u32[]{:S(2)}) %copy-start.1) | copy-done | bytes 131096
  5.3 0.8 %copy-done.3 = s32[64,64]{1,0:T(8,128)S(1)} copy-done((s32[64,64]{1,0:T(8,128)S(1)}, s32[64,64]{1,0:T(8,128)}, u32[]{:S(2)}) %copy-start.3) | copy-done | bytes 16408
  6.0 0.9 %copy-done.6 = bf16[8,64,128]{2,1,0:T(8,128)(2,1)S(1)} copy-done((bf16[8,64,128]{2,1,0:T(8,128)(2,1)S(1)}, bf16[8,64,128]{2,1,0:T(8,128)(2,1)}, u32[]{:S(2)}) %copy-start.6) | copy-done | bytes 131096
  6.9 1.0 %copy-done.12 = bf16[1024,256]{1,0:T(8,128)(2,1)S(1)} copy-done((bf16[1024,256]{1,0:T(8,128)(2,1)S(1)}, bf16[1024,256]{1,0:T(8,128)(2,1)}, u32[]{:S(2)}) %copy-start.12) | copy-done | bytes 524312
  8.0 2.6 %score.2 = (f32[8,16,128]{2,1,0:T(8,128)S(1)}, f32[8,128]{1,0:T(8,128)S(1)}) custom-call(s32[1]{0:T(128)} %bitcast.own_ref, s32[16]{0:T(128)S(1)} %copy-done.8, s32[16]{0:T(128)S(1)} %copy-done.9, f32[8]{0:T(128)S(1)} %copy-done.10, f32[32]{0:T(128)S(1)} %copy-done.11, bf16[8,64,128]{2,1,0:T(8,128)(2,1)S(1)} %copy-done.1, bf16[8,64,128]{2,1,0:T(8,128)(2,1)S(1)} %copy-done.6, ...), custom_call_target="tpu_custom_call" | custom-call | flops 268435456 | bytes 1048576 | tf_op jit(solution)/shard_map/score/pallas_call | solution.py:237
  10.7 2.6 %score.3 = (f32[8,16,128]{2,1,0:T(8,128)S(1)}, f32[8,128]{1,0:T(8,128)S(1)}) custom-call(s32[1]{0:T(128)} %bitcast.own_ref, s32[16]{0:T(128)S(1)} %copy-done.8, s32[16]{0:T(128)S(1)} %copy-done.9, f32[8]{0:T(128)S(1)} %copy-done.10, f32[32]{0:T(128)S(1)} %copy-done.11, bf16[8,64,128]{2,1,0:T(8,128)(2,1)S(1)} %collective-permute-done.x_ref.refs_3_, ...), custom_call_target="tpu_custom_call" | custom-call | flops 268435456 | bytes 1048576 | tf_op jit(solution)/shard_map/score/pallas_call | solution.py:237
  13.3 0.1 collective-permute-start.1
  13.5 3.5 %collective-permute-done.1 = f32[2,8,128]{2,1,0:T(8,128)S(1)} collective-permute-done((f32[2,8,128]{2,1,0:T(8,128)S(1)}, f32[2,8,128]{2,1,0:T(8,128)S(1)}, u32[]{:S(2)}, u32[]{:S(2)}) %collective-permute-start.1) | collective-permute-done | bytes 8224 | tf_op jit(solution)/shard_map/ppermute | solution.py:213
  17.1 0.7 %copy-done.5 = bf16[64,96]{1,0:T(8,128)(2,1)S(1)} copy-done((bf16[64,96]{1,0:T(8,128)(2,1)S(1)}, bf16[64,96]{1,0:T(8,128)(2,1)}, u32[]{:S(2)}) %copy-start.5) | copy-done | bytes 12312
  17.7 1.4 %back.1 = (f32[16,4,8,128]{3,2,1,0:T(8,128)S(1)}, f32[8,128]{1,0:T(8,128)S(1)}) custom-call(f32[8,16,128]{2,1,0:T(8,128)S(1)} %get-tuple-element.9.refs_0_, f32[8,16,128]{2,1,0:T(8,128)S(1)} %get-tuple-element.10.refs_1_, bf16[8,64,128]{2,1,0:T(8,128)(2,1)S(1)} %copy-done.2, bf16[8,64,128]{2,1,0:T(8,128)(2,1)S(1)} %collective-permute-done.x_ref.refs_3_, ...), custom_call_target="tpu_custom_call" | custom-call | tf_op jit(solution)/shard_map/back/pallas_call | solution.py:251
  19.1 0.1 reshape_squeeze.6
  19.2 0.1 reduce_sum.9
  19.6 1.2 %collective-permute-done.2 = bf16[34,8,128]{2,1,0:T(8,128)(2,1)S(1)} collective-permute-done((bf16[34,8,128]{2,1,0:T(8,128)(2,1)S(1)}, bf16[34,8,128]{2,1,0:T(8,128)(2,1)S(1)}, u32[]{:S(2)}, u32[]{:S(2)}) %collective-permute-start.2) | collective-permute-done | bytes 69664 | tf_op jit(solution)/shard_map/ppermute | solution.py:213
  21.0 1.6 %collective-permute-start.3 = (bf16[18,8,128]{2,1,0:T(8,128)(2,1)S(1)}, bf16[18,8,128]{2,1,0:T(8,128)(2,1)S(1)}, u32[]{:S(2)}, u32[]{:S(2)}) collective-permute-start(bf16[18,8,128]{2,1,0:T(8,128)(2,1)S(1)} %pad_maximum_fusion.1), channel_id=1, source_target_pairs={{0,4},{2,6},{4,0},{6,2},{8,12},{10,14},{12,8},{14,10},{16,20},{18,... | collective-permute-start | bytes 110600 | tf_op jit(solution)/shard_map/ppermute | solution.py:213
  22.6 2.4 %collective-permute-done.3 = bf16[18,8,128]{2,1,0:T(8,128)(2,1)S(1)} collective-permute-done((bf16[18,8,128]{2,1,0:T(8,128)(2,1)S(1)}, bf16[18,8,128]{2,1,0:T(8,128)(2,1)S(1)}, u32[]{:S(2)}, u32[]{:S(2)}) %collective-permute-start.3) | collective-permute-done | bytes 36896 | tf_op jit(solution)/shard_map/ppermute | solution.py:213
  25.2 1.6 %collective-permute-start.4 = (bf16[10,8,128]{2,1,0:T(8,128)(2,1)S(1)}, bf16[10,8,128]{2,1,0:T(8,128)(2,1)S(1)}, u32[]{:S(2)}, u32[]{:S(2)}) collective-permute-start(bf16[10,8,128]{2,1,0:T(8,128)(2,1)S(1)} %pad_maximum_fusion.2), channel_id=1, source_target_pairs={{0,8},{2,10},{4,12},{6,14},{8,0},{10,2},{12,4},{14,6},{16,24},{18,... | collective-permute-start | bytes 61448 | tf_op jit(solution)/shard_map/ppermute | solution.py:213
  26.8 2.2 %collective-permute-done.4 = bf16[10,8,128]{2,1,0:T(8,128)(2,1)S(1)} collective-permute-done((bf16[10,8,128]{2,1,0:T(8,128)(2,1)S(1)}, bf16[10,8,128]{2,1,0:T(8,128)(2,1)S(1)}, u32[]{:S(2)}, u32[]{:S(2)}) %collective-permute-start.4) | collective-permute-done | bytes 20512 | tf_op jit(solution)/shard_map/ppermute | solution.py:213
  29.1 2.6 %collective-permute-start.5 = (bf16[6,8,128]{2,1,0:T(8,128)(2,1)S(1)}, bf16[6,8,128]{2,1,0:T(8,128)(2,1)S(1)}, u32[]{:S(2)}, u32[]{:S(2)}) collective-permute-start(bf16[6,8,128]{2,1,0:T(8,128)(2,1)S(1)} %pad_maximum_fusion.3), channel_id=1, source_target_pairs={{0,16},{2,18},{4,20},{6,22},{8,24},{10,26},{12,28},{14,30},{16,0},... | collective-permute-start | bytes 36872 | tf_op jit(solution)/shard_map/ppermute | solution.py:213
  31.7 0.6 %add_reduce_fusion = f32[8]{0:T(128)} fusion(f32[1,8,128]{2,1,0:T(8,128)S(1)} %bitcast.142, f32[1,8,128]{2,1,0:T(8,128)S(1)} %bitcast.139, f32[1,8,128]{2,1,0:T(8,128)S(1)} %get-tuple-element.22, f32[1,8,128]{2,1,0:T(8,128)S(1)} %get-tuple-element.21), kind=kLoop, calls=%fused_computation.34 | loop fusion | flops 56 | bytes 16416 | tf_op jit(solution)/shard_map/slice | solution.py:248
  32.4 1.4 %collective-permute-done.5 = bf16[6,8,128]{2,1,0:T(8,128)(2,1)S(1)} collective-permute-done((bf16[6,8,128]{2,1,0:T(8,128)(2,1)S(1)}, bf16[6,8,128]{2,1,0:T(8,128)(2,1)S(1)}, u32[]{:S(2)}, u32[]{:S(2)}) %collective-permute-start.5) | collective-permute-done | bytes 12320 | tf_op jit(solution)/shard_map/ppermute | solution.py:213
  33.8 0.5 %slice_bitcast_fusion.12 = f32[8]{0:T(128)} fusion(f32[1,128]{1,0:T(1,128)S(1)} %fusion.11), kind=kLoop, calls=%fused_computation.63 | loop fusion | bytes 64 | tf_op jit(solution)/shard_map/squeeze | solution.py:287
  34.3 0.6 %copy.18 = f32[4,2,4,128]{3,2,0,1:T(4,128)} copy(f32[4,2,4,128]{3,2,1,0:T(4,128)S(1)} %bitcast.150) | data formatting | bytes 32768 | tf_op jit(solution)/shard_map/reshape;squeeze | solution.py:286
  (66 shorter events, 0.9 us)
Async XLA Ops:
  0.6 3.0 %copy-start.14 = (bf16[32,256]{1,0:T(8,128)(2,1)S(1)}, bf16[32,256]{1,0:T(8,128)(2,1)}, u32[]{:S(2)}) copy-start(bf16[32,256]{1,0:T(8,128)(2,1)} %constant.58.clone.columns_ref) | copy-start | bytes 49156
  0.6 10.0 %collective-permute-start = (bf16[8,64,128]{2,1,0:T(8,128)(2,1)}, bf16[8,64,128]{2,1,0:T(8,128)(2,1)S(1)}, u32[]{:S(2)}, u32[]{:S(2)}) collective-permute-start(bf16[8,64,128]{2,1,0:T(8,128)(2,1)} %refs_2_.1), channel_id=1, source_target_pairs={{0,1},{1,0},{2,3},{3,2},{4,5},{5,4},{6,7},{7,6},{8,9},{9,8},{10,11... | collective-permute-start | bytes 393224 | tf_op jit(solution)/shard_map/ppermute | solution.py:213
  3.6 0.7 %copy-start.11 = (f32[32]{0:T(128)S(1)}, f32[32]{0:T(128)}, u32[]{:S(2)}) copy-start(f32[32]{0:T(128)} %orient_prior_ref.3) | copy-start | bytes 388
  3.7 0.7 %copy-start.8 = (s32[16]{0:T(128)S(1)}, s32[16]{0:T(128)}, u32[]{:S(2)}) copy-start(s32[16]{0:T(128)} %class_ref.3) | copy-start | bytes 196
  3.7 0.7 %copy-start.9 = (s32[16]{0:T(128)S(1)}, s32[16]{0:T(128)}, u32[]{:S(2)}) copy-start(s32[16]{0:T(128)} %orient_ref.3) | copy-start | bytes 196
  3.7 0.7 %copy-start.10 = (f32[8]{0:T(128)S(1)}, f32[8]{0:T(128)}, u32[]{:S(2)}) copy-start(f32[8]{0:T(128)} %class_prior_ref.3) | copy-start | bytes 100
  4.4 0.9 %copy-start.1 = (bf16[8,64,128]{2,1,0:T(8,128)(2,1)S(1)}, bf16[8,64,128]{2,1,0:T(8,128)(2,1)}, u32[]{:S(2)}) copy-start(bf16[8,64,128]{2,1,0:T(8,128)(2,1)} %refs_2_.1) | copy-start | bytes 393220
  5.3 0.8 %copy-start.3 = (s32[64,64]{1,0:T(8,128)S(1)}, s32[64,64]{1,0:T(8,128)}, u32[]{:S(2)}) copy-start(s32[64,64]{1,0:T(8,128)} %refs_5_.1) | copy-start | bytes 49156
  6.0 0.9 %copy-start.6 = (bf16[8,64,128]{2,1,0:T(8,128)(2,1)S(1)}, bf16[8,64,128]{2,1,0:T(8,128)(2,1)}, u32[]{:S(2)}) copy-start(bf16[8,64,128]{2,1,0:T(8,128)(2,1)} %s_ref.3) | copy-start | bytes 393220
  6.9 1.0 %copy-start.12 = (bf16[1024,256]{1,0:T(8,128)(2,1)S(1)}, bf16[1024,256]{1,0:T(8,128)(2,1)}, u32[]{:S(2)}) copy-start(bf16[1024,256]{1,0:T(8,128)(2,1)} %constant.57.clone.rows_ref) | copy-start | bytes 1572868
  8.0 2.7 %copy-start.4 = (s32[64,64]{1,0:T(8,128)S(1)}, s32[64,64]{1,0:T(8,128)}, u32[]{:S(2)}) copy-start(s32[64,64]{1,0:T(8,128)} %refs_5_.1) | copy-start | bytes 49156
  8.0 2.7 %copy-start.7 = (bf16[8,64,128]{2,1,0:T(8,128)(2,1)S(1)}, bf16[8,64,128]{2,1,0:T(8,128)(2,1)}, u32[]{:S(2)}) copy-start(bf16[8,64,128]{2,1,0:T(8,128)(2,1)} %s_ref.3) | copy-start | bytes 393220
  8.0 2.7 %copy-start.13 = (bf16[1024,256]{1,0:T(8,128)(2,1)S(1)}, bf16[1024,256]{1,0:T(8,128)(2,1)}, u32[]{:S(2)}) copy-start(bf16[1024,256]{1,0:T(8,128)(2,1)} %constant.57.clone.rows_ref) | copy-start | bytes 1572868
  10.6 6.5 %copy-start = (bf16[128,2048]{1,0:T(8,128)(2,1)S(1)}, bf16[128,2048]{1,0:T(8,128)(2,1)}, u32[]{:S(2)}) copy-start(bf16[128,2048]{1,0:T(8,128)(2,1)} %constant.59.clone.refs_6_) | copy-start | bytes 1572868
  10.6 6.4 %copy-start.2 = (bf16[8,64,128]{2,1,0:T(8,128)(2,1)S(1)}, bf16[8,64,128]{2,1,0:T(8,128)(2,1)}, u32[]{:S(2)}) copy-start(bf16[8,64,128]{2,1,0:T(8,128)(2,1)} %refs_2_.1) | copy-start | bytes 393220
  13.3 3.7 %collective-permute-start.1 = (f32[2,8,128]{2,1,0:T(8,128)S(1)}, f32[2,8,128]{2,1,0:T(8,128)S(1)}, u32[]{:S(2)}, u32[]{:S(2)}) collective-permute-start(f32[2,8,128]{2,1,0:T(8,128)S(1)} %pad_maximum_fusion.4), channel_id=1, source_target_pairs={{0,1},{1,0},{2,3},{3,2},{4,5},{5,4},{6,7},{7,6},{8,9},{9,8},{10,11... | collective-permute-start | bytes 24584 | tf_op jit(solution)/shard_map/ppermute | solution.py:213
  17.0 0.7 %copy-start.5 = (bf16[64,96]{1,0:T(8,128)(2,1)S(1)}, bf16[64,96]{1,0:T(8,128)(2,1)}, u32[]{:S(2)}) copy-start(bf16[64,96]{1,0:T(8,128)(2,1)} %constant.60.clone.refs_7_) | copy-start | bytes 36868
  19.5 1.3 %collective-permute-start.2 = (bf16[34,8,128]{2,1,0:T(8,128)(2,1)S(1)}, bf16[34,8,128]{2,1,0:T(8,128)(2,1)S(1)}, u32[]{:S(2)}, u32[]{:S(2)}) collective-permute-start(bf16[34,8,128]{2,1,0:T(8,128)(2,1)S(1)} %pad_maximum_fusion), channel_id=1, source_target_pairs={{0,2},{2,0},{4,6},{6,4},{8,10},{10,8},{12,14},{14,12},{16,18},{18,... | collective-permute-start | bytes 208904 | tf_op jit(solution)/shard_map/ppermute | solution.py:213
  21.0 4.0 %collective-permute-start.3 = (bf16[18,8,128]{2,1,0:T(8,128)(2,1)S(1)}, bf16[18,8,128]{2,1,0:T(8,128)(2,1)S(1)}, u32[]{:S(2)}, u32[]{:S(2)}) collective-permute-start(bf16[18,8,128]{2,1,0:T(8,128)(2,1)S(1)} %pad_maximum_fusion.1), channel_id=1, source_target_pairs={{0,4},{2,6},{4,0},{6,2},{8,12},{10,14},{12,8},{14,10},{16,20},{18,... | collective-permute-start | bytes 110600 | tf_op jit(solution)/shard_map/ppermute | solution.py:213
  25.2 3.8 %collective-permute-start.4 = (bf16[10,8,128]{2,1,0:T(8,128)(2,1)S(1)}, bf16[10,8,128]{2,1,0:T(8,128)(2,1)S(1)}, u32[]{:S(2)}, u32[]{:S(2)}) collective-permute-start(bf16[10,8,128]{2,1,0:T(8,128)(2,1)S(1)} %pad_maximum_fusion.2), channel_id=1, source_target_pairs={{0,8},{2,10},{4,12},{6,14},{8,0},{10,2},{12,4},{14,6},{16,24},{18,... | collective-permute-start | bytes 61448 | tf_op jit(solution)/shard_map/ppermute | solution.py:213
  29.1 4.6 %collective-permute-start.5 = (bf16[6,8,128]{2,1,0:T(8,128)(2,1)S(1)}, bf16[6,8,128]{2,1,0:T(8,128)(2,1)S(1)}, u32[]{:S(2)}, u32[]{:S(2)}) collective-permute-start(bf16[6,8,128]{2,1,0:T(8,128)(2,1)S(1)} %pad_maximum_fusion.3), channel_id=1, source_target_pairs={{0,16},{2,18},{4,20},{6,22},{8,24},{10,26},{12,28},{14,30},{16,0},... | collective-permute-start | bytes 36872 | tf_op jit(solution)/shard_map/ppermute | solution.py:213

commit v2 on v1

v2 whole, which is shorter than its diff:
```python
import functools
import math

import jax
import jax.numpy as jnp
import ml_dtypes
import numpy as np
from jax import lax
from jax.experimental import pallas as pl
from jax.experimental.pallas import tpu as pltpu
from jax.sharding import PartitionSpec as P

TS = 16
F32 = jnp.float32
BF16 = jnp.bfloat16
VMEM_LIMIT = 24 * 1024 * 1024


def phase_tables(crop):
    freq = np.arange(crop, dtype=np.float64) - crop // 2
    offset = np.arange(TS, dtype=np.float64) - TS // 2
    angle = 2.0 * math.pi / crop * freq[:, None] * offset[None, :]
    return np.cos(angle).astype(np.float32), np.sin(angle).astype(np.float32)


def high_low(table):
    high = table.astype(ml_dtypes.bfloat16)
    low = (table - high.astype(np.float32)).astype(ml_dtypes.bfloat16)
    return high, low


def score_tables(crop, share):
    cosine, sine = phase_tables(crop)
    rows = np.zeros((share, 2, crop, 2, share, TS), np.float32)
    for j in range(share):
        rows[j, 0, :, 0, j] = cosine
        rows[j, 0, :, 1, j] = sine
        rows[j, 1, :, 0, j] = -sine
        rows[j, 1, :, 1, j] = cosine
    rows = rows.reshape(share * 2 * crop, 2 * share * TS).astype(ml_dtypes.bfloat16)
    high, low = high_low(np.concatenate([cosine.T, -sine.T], axis=1))
    columns = np.concatenate(
        [np.concatenate([high, high], axis=1), np.concatenate([low, np.zeros_like(low)], axis=1)], axis=0
    )
    return rows, columns


def back_tables(crop, share, order):
    cosine, sine = phase_tables(crop)
    rows = np.zeros((share, TS, 2, share, 2, crop), np.float32)
    for place, j in enumerate(order):
        rows[j, :, 0, place, 0] = cosine.T
        rows[j, :, 0, place, 1] = -sine.T
        rows[j, :, 1, place, 0] = -sine.T
        rows[j, :, 1, place, 1] = -cosine.T
    rows = rows.reshape(share * TS, 2 * share * 2 * crop).astype(ml_dtypes.bfloat16)
    high, low = high_low(np.concatenate([cosine, sine], axis=1))
    return rows, np.concatenate([high, high, low], axis=1)


def score_block(plain, swapped, first_ref, second_ref, bias, rows_ref, columns_ref, cross, logits_ref, lse_ref):
    count, crop, width = plain.shape
    share = first_ref.shape[0]
    lanes = share * TS
    for at in range(0, crop, 16):
        for j in range(share):
            a, b = first_ref[j, at : at + 16], second_ref[j, at : at + 16]
            for i in range(count):
                value = plain[i, at : at + 16] * a + swapped[i, at : at + 16] * b
                cross[i * crop + at : i * crop + at + 16, j * width : (j + 1) * width] = value.astype(BF16)
    rowcorr = jnp.dot(cross[...], rows_ref[...], preferred_element_type=F32)
    high = rowcorr.astype(BF16)
    low = (rowcorr - high.astype(F32)).astype(BF16)
    stacked = jnp.concatenate(
        [
            jnp.concatenate(
                [part[i * crop : (i + 1) * crop, k * lanes : (k + 1) * lanes] for part in (high, low) for k in (0, 1)],
                axis=0,
            )
            for i in range(count)
        ],
        axis=1,
    )
    corr = jnp.dot(columns_ref[...], stacked, preferred_element_type=F32)
    corr = (corr[:TS] + corr[TS:]) * (1.0 / crop)
    logits = [corr[:, i * lanes : (i + 1) * lanes] + bias for i in range(count)]
    for i in range(count):
        logits_ref[i] = logits[i]
    tops = jnp.concatenate([jnp.max(value, axis=0, keepdims=True) for value in logits], axis=0)
    top = jnp.max(tops, axis=1, keepdims=True)
    sums = [jnp.sum(jnp.exp(logits[i] - top[i : i + 1]), axis=0, keepdims=True) for i in range(count)]
    total = jnp.sum(jnp.concatenate(sums, axis=0), axis=1, keepdims=True)
    lse_ref[...] = jnp.broadcast_to(top + jnp.log(total), lse_ref.shape)


def split_particles(x_ref, plain, swapped):
    for i in range(x_ref.shape[0]):
        x = x_ref[i].astype(F32)
        plain[i] = x
        swapped[i] = pltpu.roll(x, x.shape[1] // 2, 1)


def first_kernel(*refs):
    sources, (logits_ref, lse_ref, first, second, bias_ref), kept = refs[:11], refs[11:16], refs[16:22]
    s_ref, class_ref, orient_ref, class_prior_ref, orient_prior_ref, cross, plain, swapped, sems = refs[22:]
    x_ref, mask_ref, rows_ref, columns_ref, back_rows_ref, back_columns_ref = kept
    targets = (
        x_ref, s_ref, mask_ref, rows_ref, columns_ref, class_ref, orient_ref, class_prior_ref, orient_prior_ref,
        back_rows_ref, back_columns_ref,
    )
    copies = [pltpu.make_async_copy(a, b, sems.at[k]) for k, (a, b) in enumerate(zip(sources, targets))]
    for copy in copies:
        copy.start()
    share, crop, width = s_ref.shape
    half = width // 2
    left = lax.broadcasted_iota(jnp.int32, (crop, width), 1) < half
    for copy in copies[:3]:
        copy.wait()
    mask = mask_ref[...].astype(F32)
    mask = jnp.concatenate([mask, mask], axis=1)
    powers = []
    for j in range(share):
        s = s_ref[j].astype(F32) * mask
        turned = pltpu.roll(s, half, 1)
        first[j] = jnp.where(left, s, turned)
        second[j] = jnp.where(left, turned, -s)
        powers.append(jnp.sum(s * s, axis=0, keepdims=True))
    power = jnp.sum(jnp.concatenate(powers, axis=0), axis=1, keepdims=True)
    split_particles(x_ref, plain, swapped)
    for copy in copies[3:]:
        copy.wait()
    slot = lax.broadcasted_iota(jnp.int32, (1, share * TS), 1) // TS
    bias = jnp.zeros((1, share * TS), F32)
    start = lax.axis_index("orient") * share
    for j in range(share):
        prior = class_prior_ref[class_ref[start + j]] + orient_prior_ref[orient_ref[start + j]]
        bias = jnp.where(slot == j, prior - power[j : j + 1] * (0.5 / crop), bias)
    bias_ref[...] = jnp.broadcast_to(bias, bias_ref.shape)
    score_block(plain, swapped, first, second, bias, rows_ref, columns_ref, cross, logits_ref, lse_ref)


def score_kernel(
    x_ref, first, second, bias_ref, rows_ref, columns_ref, logits_ref, lse_ref, cross, plain, swapped
):
    split_particles(x_ref, plain, swapped)
    score_block(plain, swapped, first, second, bias_ref[:1], rows_ref, columns_ref, cross, logits_ref, lse_ref)


def log_add(a, b):
    top = jnp.maximum(a, b)
    return top + jnp.log(jnp.exp(a - top) + jnp.exp(b - top))


def to_lanes(column):
    wide = jnp.broadcast_to(column, (column.shape[0], 128))
    row = lax.broadcasted_iota(jnp.int32, wide.shape, 0)
    lane = lax.broadcasted_iota(jnp.int32, wide.shape, 1)
    return jnp.sum(jnp.where(row == lane, wide, 0.0), axis=0, keepdims=True)


def put_mass(send_ref, at, mass):
    row = lax.broadcasted_iota(jnp.int32, (8, 128), 0)
    if send_ref.dtype == F32:
        send_ref[at : at + 8] = jnp.broadcast_to(mass, (8, 128))
    else:
        high = mass.astype(BF16).astype(F32)
        middle = (mass - high).astype(BF16).astype(F32)
        low = mass - high - middle
        terms = jnp.where(row == 0, high, jnp.where(row == 1, middle, jnp.where(row == 2, low, 0.0)))
        send_ref[at : at + 16] = jnp.concatenate([terms, jnp.zeros((8, 128), F32)], axis=0).astype(BF16)


def get_mass(got_ref, at):
    if got_ref.dtype == F32:
        return got_ref[at : at + 1]
    terms = got_ref[at : at + 16].astype(F32)
    return terms[0:1] + terms[1:2] + terms[2:3]


def back_kernel(share, pack, start, last, *refs):
    refs = list(refs)
    logits_ref, lse_a_ref, lse_b_ref, x_ref, rows_ref, columns_ref = refs[:6]
    del refs[:6]
    if not start:
        re_in, im_in, mass_in = refs[:3]
        del refs[:3]
    if last:
        mask_ref, keep_ref, send_ref, mass_ref, loglik_ref = refs[:5]
        del refs[:5]
    else:
        re_ref, im_ref, mass_ref = refs[:3]
        del refs[:3]
    doubled_re, doubled_im, high, low = refs
    count, crop, width = x_ref.shape
    half = width // 2
    left = lax.broadcasted_iota(jnp.int32, (crop, width), 1) < half
    loglik = log_add(lse_a_ref[...], lse_b_ref[...])
    mass = jnp.zeros((TS, share * TS), F32)
    weights = []
    for i in range(count):
        weight = jnp.exp(logits_ref[i] - loglik[i : i + 1, :]).astype(BF16)
        mass = mass + weight.astype(F32)
        weights.append(weight)
        x = x_ref[i].astype(F32)
        turned = pltpu.roll(x, half, 1)
        doubled_re[i] = jnp.where(left, x, turned)
        doubled_im[i] = jnp.where(left, turned, x)
    mass = jnp.sum(mass, axis=0, keepdims=True)
    if not start:
        mass = mass + mass_in[:1]
    spread = jnp.dot(jnp.concatenate(weights, axis=0), rows_ref[...], preferred_element_type=F32)
    rounded = spread.astype(BF16)
    high[...] = rounded
    low[...] = (spread - rounded.astype(F32)).astype(BF16)
    forms = share * width
    wide = pack * width
    groups = share // pack
    columns = columns_ref[...]
    if last:
        mask = mask_ref[...].astype(F32)
        mask = jnp.concatenate([mask, mask], axis=1)
        sign = jnp.where(left[:1], -1.0, 1.0)
        odd = (lax.axis_index("dom") & 1) == 1
    for group in range(groups):
        re = jnp.zeros((crop, wide), F32) if start else re_in[group]
        im = jnp.zeros((crop, wide), F32) if start else im_in[group]
        for k in range(count):
            rows = slice(k * TS, (k + 1) * TS)
            here = slice(group * wide, (group + 1) * wide)
            there = slice(forms + group * wide, forms + (group + 1) * wide)
            a, b = high[rows, here], high[rows, there]
            terms = jnp.concatenate([a, b, low[rows, here], low[rows, there], a, b], axis=0)
            kernel = jnp.dot(columns, terms, preferred_element_type=F32)
            re = re + kernel * jnp.concatenate([doubled_re[k]] * pack, axis=1)
            im = im + kernel * jnp.concatenate([doubled_im[k]] * pack, axis=1)
        if not last:
            re_ref[group] = re
            im_ref[group] = im
            continue
        images = []
        for p in range(pack):
            here = slice(p * width, (p + 1) * width)
            images.append((re[:, here] + pltpu.roll(im[:, here], half, 1) * sign) * mask)
        block = 8 // pack
        tiles = [
            jnp.concatenate([image[at : at + block] for image in images], axis=0) for at in range(0, crop, block)
        ]
        for pair in range(len(tiles) // 2):
            at = (pair * groups + group) * 8
            keep_ref[at : at + 8] = jnp.where(odd, tiles[2 * pair + 1], tiles[2 * pair])
            send_ref[at : at + 8] = jnp.where(odd, tiles[2 * pair], tiles[2 * pair + 1])
    if last:
        row = lax.broadcasted_iota(jnp.int32, (share, share * TS), 0)
        lane = lax.broadcasted_iota(jnp.int32, (share, share * TS), 1)
        each = jnp.sum(jnp.where(row == lane // TS, mass, 0.0), axis=1, keepdims=True)
        mass = to_lanes(each)
        put_mass(send_ref, keep_ref.shape[0], mass)
        loglik_ref[...] = to_lanes(loglik[:, :1])[0, :count]
    mass_ref[...] = jnp.broadcast_to(mass, mass_ref.shape)


def halve_kernel(groups, bit, keep_ref, got_ref, mass_in, left_ref, send_ref, mass_ref):
    rows = keep_ref.shape[0]
    unit = groups * 8
    side = (lax.axis_index("dom") >> bit) & 1
    for pair in range(rows // unit // 2):
        at = pair * unit
        mine = pl.ds(pl.multiple_of((2 * pair + side) * unit, unit), unit)
        theirs = pl.ds(pl.multiple_of((2 * pair + 1 - side) * unit, unit), unit)
        left_ref[at : at + unit] = keep_ref[mine] + got_ref[mine].astype(F32)
        send_ref[at : at + unit] = (keep_ref[theirs] + got_ref[theirs].astype(F32)).astype(send_ref.dtype)
    mass = mass_in[:1] + get_mass(got_ref, rows)
    put_mass(send_ref, rows // 2, mass)
    mass_ref[...] = jnp.broadcast_to(mass, mass_ref.shape)


def last_kernel(groups, pack, keep_ref, got_ref, mass_in, image_ref, occupancy_ref):
    block = image_ref.shape[1]
    rows = keep_ref.shape[0]
    total = keep_ref[...] + got_ref[:rows].astype(F32)
    for g in range(groups):
        for p in range(pack):
            image_ref[p * groups + g] = total[g * 8 + p * block : g * 8 + (p + 1) * block]
    mass = mass_in[:1] + get_mass(got_ref, rows)
    occupancy_ref[...] = mass[0, : occupancy_ref.shape[0]]


def bits(count):
    return count.bit_length() - 1


def shards(n_dom, n_orient, particles, slices, freq_mask, slice_class, slice_orient, class_prior, orient_prior):
    count, crop, width = particles.shape
    share = slices.shape[0]
    lanes = share * TS
    block = crop // n_dom
    pack = 8 // block
    groups = share // pack
    vmem = pl.BlockSpec(memory_space=pltpu.VMEM)
    hbm = pl.BlockSpec(memory_space=pltpu.HBM)
    shape = jax.ShapeDtypeStruct
    params = pltpu.CompilerParams(vmem_limit_bytes=VMEM_LIMIT)
    order = [p * groups + g for g in range(groups) for p in range(pack)]
    tables = [jnp.asarray(t) for t in (*score_tables(crop, share), *back_tables(crop, share, order))]

    def call(kernel, outs, args, scratch, specs=None, flops=0, name=None):
        return pl.pallas_call(
            kernel,
            out_shape=tuple(outs),
            in_specs=specs or [vmem] * len(args),
            out_specs=(vmem,) * len(outs),
            scratch_shapes=scratch,
            compiler_params=params,
            cost_estimate=pl.CostEstimate(flops=flops, bytes_accessed=1 << 20, transcendentals=0),
            name=name,
        )(*args)

    def swap(value, axis, size, step):
        return lax.ppermute(value, axis, [(i, i ^ step) for i in range(size)])

    flops = 2 * count * crop * share * width * 2 * lanes
    scored_shapes = [shape((count, TS, lanes), F32), shape((count, 128), F32)]
    turned = pltpu.VMEM((count, crop, width), F32)
    score_scratch = [pltpu.VMEM((count * crop, share * width), BF16), turned, turned]
    slices_shape = shape(slices.shape, F32)
    score_rows, score_columns, back_rows, back_columns = tables

    slots = [particles] + [swap(particles, "orient", n_orient, r) for r in range(1, n_orient)]
    kept = (particles, freq_mask, *tables)
    logits, lse, first, second, bias, mine, mask, *tables = call(
        first_kernel,
        [*scored_shapes, slices_shape, slices_shape, shape((8, lanes), F32)]
        + [shape(value.shape, value.dtype) for value in kept],
        tuple(
            pltpu.with_memory_space_constraint(value, pltpu.HBM)
            for value in (
                particles, slices, freq_mask, score_rows, score_columns, slice_class, slice_orient, class_prior,
                orient_prior, back_rows, back_columns,
            )
        ),
        [
            pltpu.VMEM(slices.shape, slices.dtype),
            *[pltpu.SMEM(v.shape, v.dtype) for v in (slice_class, slice_orient, class_prior, orient_prior)],
            *score_scratch,
            pltpu.SemaphoreType.DMA((11,)),
        ],
        specs=[hbm] * 11, flops=flops, name="first",
    )
    score_rows, score_columns, back_rows, back_columns = tables
    slots[0] = mine
    scored = [(logits, lse)] + [
        call(
            score_kernel, scored_shapes, (parts, first, second, bias, score_rows, score_columns), score_scratch,
            flops=flops, name="score",
        )
        for parts in slots[1:]
    ]
    lses = [s[1] for s in scored]
    for b in range(bits(n_orient)):
        theirs = [swap(lses[r ^ (1 << b)], "orient", n_orient, 1 << b) for r in range(n_orient)]
        if b < bits(n_orient) - 1:
            lses = [log_add(x, y) for x, y in zip(lses, theirs)]

    rows = crop // block * groups * 8
    steps = bits(n_dom)

    def sent(step, height):
        dtype = F32 if step in (0, steps - 1) else BF16
        return shape((height + (8 if dtype == F32 else 16), width), dtype)

    sums = shape((groups, crop, pack * width), F32)
    mass_shape = shape((8, lanes), F32)
    back_scratch = [turned, turned] + [pltpu.VMEM((count * TS, 2 * share * width), BF16)] * 2
    partial = ()
    for r in range(1, n_orient):
        partial = call(
            functools.partial(back_kernel, share, pack, r == 1, False),
            [sums, sums, mass_shape],
            (scored[r][0], lses[r], theirs[r], slots[r], back_rows, back_columns, *partial),
            back_scratch, flops=flops, name="back",
        )
    keep, send, mass, loglik = call(
        functools.partial(back_kernel, share, pack, False, True),
        [shape((rows // 2, width), F32), sent(0, rows // 2), shape((8, 128), F32), shape((count,), F32)],
        (scored[0][0], lses[0], theirs[0], slots[0], back_rows, back_columns, *partial, mask),
        back_scratch, flops=flops, name="last_back",
    )
    for b in range(steps - 1):
        got = swap(send, "dom", n_dom, 1 << b)
        height = keep.shape[0] // 2
        keep, send, mass = call(
            functools.partial(halve_kernel, groups, b + 1),
            [shape((height, width), F32), sent(b + 1, height), shape((8, 128), F32)],
            (keep, got, mass), [], name="halve",
        )
    got = swap(send, "dom", n_dom, n_dom // 2)
    image, occupancy = call(
        functools.partial(last_kernel, groups, pack),
        [shape((share, block, width), F32), shape((share,), F32)],
        (keep, got, mass), [], name="last",
    )
    return image, occupancy, loglik


def solution(mesh):
    placed = (P(("dom", "orient"), None, None), P("orient", None, None), P(), P(), P(), P(), P())
    return jax.shard_map(
        functools.partial(shards, mesh.shape["dom"], mesh.shape["orient"]),
        mesh=mesh,
        in_specs=placed,
        out_specs=(P("orient", "dom", None), P("orient"), P(("dom", "orient"))),
        check_vma=False,
    )
```

time: 35.2 us -> 28.2 us (0.80)
  local copies, waits for them, and re-layouts: 6.42 us -> 0 us
  starting transfers between devices: 8.92 us -> 11.5 us
  other arithmetic: 1.26 us -> 0 us
  waiting for transfers between devices: 10.8 us -> 9.58 us
    unnamed x30 -> x0, local copies, waits for them, and re-layouts: 5 us -> none
    ppermute x6 -> x7, starting transfers between devices: 8.92 us -> 11.5 us  [swap(): return lax.ppermute(value, axis, [(i, i ^ step) for i in range(size)])]
    ppermute x6 -> x7, waiting for transfers between devices: 10.8 us -> 9.58 us  [swap(): return lax.ppermute(value, axis, [(i, i ^ step) for i in range(size)])]
    another operation x3 -> x0, local copies, waits for them, and re-layouts: 0.69 us -> none  [the longest x1 0.61 us: shards(): terms[0].reshape(groups, pack, block, width).transpose(1, 0, 2, 3)]
    slice x1 -> x0, other arithmetic: 0.64 us -> none  [shards(): loglik = lse[0, :, 0]]
    squeeze x1 -> x0, local copies, waits for them, and re-layouts: 0.51 us -> none  [shards(): return (image, mass[0, :share], loglik)]
    pallas_call x3 -> x8, Pallas kernels: 6.6 us -> 6.29 us  [call(): pl.pallas_call(kernel, out_shape=tuple(outs), in_specs=specs or [vmem] *...]
  transfers between devices with their start and end apart: 6 -> 7, of which waited for: 5 -> 6; matrix products, arithmetic and copies ran while one was open for 2% -> 0% of each run, Pallas kernels for 7% -> 15%
where the time goes in v2:
time: 28.2 us; the launch traced here: 28 us
  starting transfers between devices  11.5 us (41%)
  waiting for transfers between devices  9.58 us (34%)
  Pallas kernels  6.29 us (22%)
  between operations  0.66 us (2%)
    ppermute x7, starting transfers between devices, swap(): return lax.ppermute(value, axis, [(i, i ^ step) for i in range(size)])  11.5 us
    ppermute x7, waiting for transfers between devices, swap(): return lax.ppermute(value, axis, [(i, i ^ step) for i in range(size)])  9.58 us
    pallas_call x8, Pallas kernels, call(): pl.pallas_call(kernel, out_shape=tuple(outs), in_specs=specs or [vmem] *...  6.29 us
  transfers between devices with their start and end apart: 7, of which 6 were waited for; matrix products, arithmetic and copies ran while one was open for 0% of the time, Pallas kernels for 15%

profile of v2, /device:TPU:0, one launch (start us, length us, event | category | flops | bytes accessed | tf_op | source)
XLA Modules:
  0.0 28.0 jit_solution(9194622289446807842)
XLA Ops:
  0.6 3.0 %collective-permute-start = (bf16[8,64,128]{2,1,0:T(8,128)(2,1)}, bf16[8,64,128]{2,1,0:T(8,128)(2,1)S(1)}, u32[]{:S(2)}, u32[]{:S(2)}) collective-permute-start(bf16[8,64,128]{2,1,0:T(8,128)(2,1)} %refs_0_.1), channel_id=1, source_target_pairs={{0,1},{1,0},{2,3},{3,2},{4,5},{5,4},{6,7},{7,6},{8,9},{9,8},{10,11... | collective-permute-start | bytes 393224 | tf_op jit(solution)/shard_map/ppermute | solution.py:319
  3.6 2.5 %first.1 = (f32[8,16,128]{2,1,0:T(8,128)S(1)}, f32[8,128]{1,0:T(8,128)S(1)}, f32[8,64,128]{2,1,0:T(8,128)S(1)}, f32[8,64,128]{2,1,0:T(8,128)S(1)}, f32[8,128]{1,...) custom-call(bf16[8,64,128]{2,1,0:T(8,128)(2,1)} %refs_0_.1, ...), custom_call_target="tpu_custom_call" | custom-call | flops 268435456 | bytes 1048576 | tf_op jit(solution)/shard_map/first/pallas_call | solution.py:307
  6.1 0.1 collective-permute-start.2
  6.2 1.1 %collective-permute-done.x_ref.refs_3_ = bf16[8,64,128]{2,1,0:T(8,128)(2,1)S(1)} collective-permute-done((bf16[8,64,128]{2,1,0:T(8,128)(2,1)}, bf16[8,64,128]{2,1,0:T(8,128)(2,1)S(1)}, u32[]{:S(2)}, u32[]{:S(2)}) %collective-permute-start) | collective-permute-done | bytes 131104 | tf_op jit(solution)/shard_map/ppermute | solution.py:319
  7.3 1.1 %score.1 = (f32[8,16,128]{2,1,0:T(8,128)S(1)}, f32[8,128]{1,0:T(8,128)S(1)}) custom-call(bf16[8,64,128]{2,1,0:T(8,128)(2,1)S(1)} %collective-permute-done.x_ref.refs_3_, f32[8,64,128]{2,1,0:T(8,128)S(1)} %get-tuple-element.36.first, f32[8,64,128]{2,1,0:T(8,128)S(1)} %get-tuple-element.37.second, f32[8,128]{1,0:T(8,128)S(1)} %get-tuple-element.38.bias_ref, ...), custom_call_target="tpu_custom_call" | custom-call | flops 268435456 | bytes 1048576 | tf_op jit(solution)/shard_map/score/pallas_call | solution.py:307
  8.5 1.8 %collective-permute-start.1 = (f32[8,128]{1,0:T(8,128)S(1)}, f32[8,128]{1,0:T(8,128)S(1)}, u32[]{:S(2)}, u32[]{:S(2)}) collective-permute-start(f32[8,128]{1,0:T(8,128)S(1)} %get-tuple-element.41.refs_1_), channel_id=1, source_target_pairs={{0,1},{1,0},{2,3},{3,2},{4,5},{5,4},{6,7},{7,6},{8,9},{9,8},{10,11... | collective-permute-start | bytes 12296 | tf_op jit(solution)/shard_map/ppermute | solution.py:319
  10.3 0.0 collective-permute-done.2.refs_2_
  10.3 0.7 %back.1 = (f32[4,64,256]{2,1,0:T(8,128)S(1)}, f32[4,64,256]{2,1,0:T(8,128)S(1)}, f32[8,128]{1,0:T(8,128)S(1)}) custom-call(f32[8,16,128]{2,1,0:T(8,128)S(1)} %get-tuple-element.45.refs_0_, f32[8,128]{1,0:T(8,128)S(1)} %get-tuple-element.41.refs_1_, f32[8,128]{1,0:T(8,128)S(1)} %collective-permute-done.2.refs_2_, ...), custom_call_target="tpu_custom_call" | custom-call | flops 268435456 | bytes 1048576 | tf_op jit(solution)/shard_map/back/pallas_call | solution.py:307
  11.0 1.1 %collective-permute-done.1.refs_2_ = f32[8,128]{1,0:T(8,128)S(1)} collective-permute-done((f32[8,128]{1,0:T(8,128)S(1)}, f32[8,128]{1,0:T(8,128)S(1)}, u32[]{:S(2)}, u32[]{:S(2)}) %collective-permute-start.1) | collective-permute-done | bytes 4128 | tf_op jit(solution)/shard_map/ppermute | solution.py:319
  12.1 1.3 %last_back.1 = (f32[256,128]{1,0:T(8,128)S(1)}, f32[264,128]{1,0:T(8,128)S(1)}, f32[8,128]{1,0:T(8,128)S(1)}, f32[8]{0:T(128)}) custom-call(f32[8,16,128]{2,1,0:T(8,128)S(1)} %get-tuple-element.34.refs_0_, f32[8,128]{1,0:T(8,128)S(1)} %get-tuple-element.35.refs_1_, f32[8,128]{1,0:T(8,128)S(1)} %collective-permute-done.1.refs_2_, ...), custom_call_target="tpu_custom_call" | custom-call | flops 268435456 | bytes 1048576 | tf_op jit(solution)/shard_map/last_back/pallas_call | solution.py:307
  13.4 0.0 collective-permute-start.3
  13.4 1.4 %collective-permute-done.3.got_ref = f32[264,128]{1,0:T(8,128)S(1)} collective-permute-done((f32[264,128]{1,0:T(8,128)S(1)}, f32[264,128]{1,0:T(8,128)S(1)}, u32[]{:S(2)}, u32[]{:S(2)}) %collective-permute-start.3) | collective-permute-done | bytes 135200 | tf_op jit(solution)/shard_map/ppermute | solution.py:319
  14.8 1.8 %collective-permute-start.4 = (bf16[144,128]{1,0:T(8,128)(2,1)S(1)}, bf16[144,128]{1,0:T(8,128)(2,1)S(1)}, u32[]{:S(2)}, u32[]{:S(2)}) collective-permute-start(bf16[144,128]{1,0:T(8,128)(2,1)S(1)} %get-tuple-element.54), channel_id=1, source_target_pairs={{0,4},{2,6},{4,0},{6,2},{8,12},{10,14},{12,8},{14,10},{16,20},{18,... | collective-permute-start | bytes 110600 | tf_op jit(solution)/shard_map/ppermute | solution.py:319
  16.6 2.2 %collective-permute-done.4.got_ref = bf16[144,128]{1,0:T(8,128)(2,1)S(1)} collective-permute-done((bf16[144,128]{1,0:T(8,128)(2,1)S(1)}, bf16[144,128]{1,0:T(8,128)(2,1)S(1)}, u32[]{:S(2)}, u32[]{:S(2)}) %collective-permute-start.4) | collective-permute-done | bytes 36896 | tf_op jit(solution)/shard_map/ppermute | solution.py:319
  18.8 1.9 %collective-permute-start.5 = (bf16[80,128]{1,0:T(8,128)(2,1)S(1)}, bf16[80,128]{1,0:T(8,128)(2,1)S(1)}, u32[]{:S(2)}, u32[]{:S(2)}) collective-permute-start(bf16[80,128]{1,0:T(8,128)(2,1)S(1)} %get-tuple-element.57), channel_id=1, source_target_pairs={{0,8},{2,10},{4,12},{6,14},{8,0},{10,2},{12,4},{14,6},{16,24},{18,... | collective-permute-start | bytes 61448 | tf_op jit(solution)/shard_map/ppermute | solution.py:319
  20.7 2.0 %collective-permute-done.5.got_ref = bf16[80,128]{1,0:T(8,128)(2,1)S(1)} collective-permute-done((bf16[80,128]{1,0:T(8,128)(2,1)S(1)}, bf16[80,128]{1,0:T(8,128)(2,1)S(1)}, u32[]{:S(2)}, u32[]{:S(2)}) %collective-permute-start.5) | collective-permute-done | bytes 20512 | tf_op jit(solution)/shard_map/ppermute | solution.py:319
  22.7 2.9 %collective-permute-start.6 = (f32[40,128]{1,0:T(8,128)S(1)}, f32[40,128]{1,0:T(8,128)S(1)}, u32[]{:S(2)}, u32[]{:S(2)}) collective-permute-start(f32[40,128]{1,0:T(8,128)S(1)} %get-tuple-element.60), channel_id=1, source_target_pairs={{0,16},{2,18},{4,20},{6,22},{8,24},{10,26},{12,28},{14,30},{16,0},... | collective-permute-start | bytes 61448 | tf_op jit(solution)/shard_map/ppermute | solution.py:319
  25.6 1.9 %collective-permute-done.6.got_ref = f32[40,128]{1,0:T(8,128)S(1)} collective-permute-done((f32[40,128]{1,0:T(8,128)S(1)}, f32[40,128]{1,0:T(8,128)S(1)}, u32[]{:S(2)}, u32[]{:S(2)}) %collective-permute-start.6) | collective-permute-done | bytes 20512 | tf_op jit(solution)/shard_map/ppermute | solution.py:319
  27.4 0.6 %last.1 = (f32[8,4,128]{2,1,0:T(4,128)}, f32[8]{0:T(128)}) custom-call(f32[32,128]{1,0:T(8,128)S(1)} %get-tuple-element.59.keep_ref, f32[40,128]{1,0:T(8,128)S(1)} %collective-permute-done.6.got_ref, f32[8,128]{1,0:T(8,128)S(1)} %get-tuple-element.61.mass_in), custom_call_target="tpu_custom_call" | custom-call | bytes 1048576 | tf_op jit(solution)/shard_map/last/pallas_call | solution.py:307
  (3 shorter events, 0.1 us)
Async XLA Ops:
  0.6 6.7 %collective-permute-start = (bf16[8,64,128]{2,1,0:T(8,128)(2,1)}, bf16[8,64,128]{2,1,0:T(8,128)(2,1)S(1)}, u32[]{:S(2)}, u32[]{:S(2)}) collective-permute-start(bf16[8,64,128]{2,1,0:T(8,128)(2,1)} %refs_0_.1), channel_id=1, source_target_pairs={{0,1},{1,0},{2,3},{3,2},{4,5},{5,4},{6,7},{7,6},{8,9},{9,8},{10,11... | collective-permute-start | bytes 393224 | tf_op jit(solution)/shard_map/ppermute | solution.py:319
  6.1 4.1 %collective-permute-start.2 = (f32[8,128]{1,0:T(8,128)S(1)}, f32[8,128]{1,0:T(8,128)S(1)}, u32[]{:S(2)}, u32[]{:S(2)}) collective-permute-start(f32[8,128]{1,0:T(8,128)S(1)} %get-tuple-element.35.refs_1_), channel_id=1, source_target_pairs={{0,1},{1,0},{2,3},{3,2},{4,5},{5,4},{6,7},{7,6},{8,9},{9,8},{10,11... | collective-permute-start | bytes 12296 | tf_op jit(solution)/shard_map/ppermute | solution.py:319
  8.5 3.6 %collective-permute-start.1 = (f32[8,128]{1,0:T(8,128)S(1)}, f32[8,128]{1,0:T(8,128)S(1)}, u32[]{:S(2)}, u32[]{:S(2)}) collective-permute-start(f32[8,128]{1,0:T(8,128)S(1)} %get-tuple-element.41.refs_1_), channel_id=1, source_target_pairs={{0,1},{1,0},{2,3},{3,2},{4,5},{5,4},{6,7},{7,6},{8,9},{9,8},{10,11... | collective-permute-start | bytes 12296 | tf_op jit(solution)/shard_map/ppermute | solution.py:319
  13.4 1.4 %collective-permute-start.3 = (f32[264,128]{1,0:T(8,128)S(1)}, f32[264,128]{1,0:T(8,128)S(1)}, u32[]{:S(2)}, u32[]{:S(2)}) collective-permute-start(f32[264,128]{1,0:T(8,128)S(1)} %get-tuple-element.51), channel_id=1, source_target_pairs={{0,2},{2,0},{4,6},{6,4},{8,10},{10,8},{12,14},{14,12},{16,18},{18,... | collective-permute-start | bytes 405512 | tf_op jit(solution)/shard_map/ppermute | solution.py:319
  14.8 4.0 %collective-permute-start.4 = (bf16[144,128]{1,0:T(8,128)(2,1)S(1)}, bf16[144,128]{1,0:T(8,128)(2,1)S(1)}, u32[]{:S(2)}, u32[]{:S(2)}) collective-permute-start(bf16[144,128]{1,0:T(8,128)(2,1)S(1)} %get-tuple-element.54), channel_id=1, source_target_pairs={{0,4},{2,6},{4,0},{6,2},{8,12},{10,14},{12,8},{14,10},{16,20},{18,... | collective-permute-start | bytes 110600 | tf_op jit(solution)/shard_map/ppermute | solution.py:319
  18.8 3.8 %collective-permute-start.5 = (bf16[80,128]{1,0:T(8,128)(2,1)S(1)}, bf16[80,128]{1,0:T(8,128)(2,1)S(1)}, u32[]{:S(2)}, u32[]{:S(2)}) collective-permute-start(bf16[80,128]{1,0:T(8,128)(2,1)S(1)} %get-tuple-element.57), channel_id=1, source_target_pairs={{0,8},{2,10},{4,12},{6,14},{8,0},{10,2},{12,4},{14,6},{16,24},{18,... | collective-permute-start | bytes 61448 | tf_op jit(solution)/shard_map/ppermute | solution.py:319
  22.7 4.7 %collective-permute-start.6 = (f32[40,128]{1,0:T(8,128)S(1)}, f32[40,128]{1,0:T(8,128)S(1)}, u32[]{:S(2)}, u32[]{:S(2)}) collective-permute-start(f32[40,128]{1,0:T(8,128)S(1)} %get-tuple-element.60), channel_id=1, source_target_pairs={{0,16},{2,18},{4,20},{6,22},{8,24},{10,26},{12,28},{14,30},{16,0},... | collective-permute-start | bytes 61448 | tf_op jit(solution)/shard_map/ppermute | solution.py:319

commit v3 on v2

--- a/solution.py
+++ b/solution.py
@@ -58,17 +58,17 @@
     return rows, np.concatenate([high, high, low], axis=1)
 
 
-def score_block(plain, swapped, first_ref, second_ref, bias, rows_ref, columns_ref, cross, logits_ref, lse_ref):
-    count, crop, width = plain.shape
+def score_block(x_ref, first_ref, second_ref, bias, rows_ref, columns_ref, logits_ref, lse_ref):
+    count, crop, width = x_ref.shape
     share = first_ref.shape[0]
     lanes = share * TS
-    for at in range(0, crop, 16):
-        for j in range(share):
-            a, b = first_ref[j, at : at + 16], second_ref[j, at : at + 16]
-            for i in range(count):
-                value = plain[i, at : at + 16] * a + swapped[i, at : at + 16] * b
-                cross[i * crop + at : i * crop + at + 16, j * width : (j + 1) * width] = value.astype(BF16)
-    rowcorr = jnp.dot(cross[...], rows_ref[...], preferred_element_type=F32)
+    cross = []
+    for i in range(count):
+        x = x_ref[i].astype(F32)
+        turned = pltpu.roll(x, width // 2, 1)
+        terms = [(x * first_ref[j] + turned * second_ref[j]).astype(BF16) for j in range(share)]
+        cross.append(jnp.concatenate(terms, axis=1))
+    rowcorr = jnp.dot(jnp.concatenate(cross, axis=0), rows_ref[...], preferred_element_type=F32)
     high = rowcorr.astype(BF16)
     low = (rowcorr - high.astype(F32)).astype(BF16)
     stacked = jnp.concatenate(
@@ -93,29 +93,10 @@
     lse_ref[...] = jnp.broadcast_to(top + jnp.log(total), lse_ref.shape)
 
 
-def split_particles(x_ref, plain, swapped):
-    for i in range(x_ref.shape[0]):
-        x = x_ref[i].astype(F32)
-        plain[i] = x
-        swapped[i] = pltpu.roll(x, x.shape[1] // 2, 1)
-
-
-def first_kernel(*refs):
-    sources, (logits_ref, lse_ref, first, second, bias_ref), kept = refs[:11], refs[11:16], refs[16:22]
-    s_ref, class_ref, orient_ref, class_prior_ref, orient_prior_ref, cross, plain, swapped, sems = refs[22:]
-    x_ref, mask_ref, rows_ref, columns_ref, back_rows_ref, back_columns_ref = kept
-    targets = (
-        x_ref, s_ref, mask_ref, rows_ref, columns_ref, class_ref, orient_ref, class_prior_ref, orient_prior_ref,
-        back_rows_ref, back_columns_ref,
-    )
-    copies = [pltpu.make_async_copy(a, b, sems.at[k]) for k, (a, b) in enumerate(zip(sources, targets))]
-    for copy in copies:
-        copy.start()
+def prepare_slices(s_ref, mask_ref, first, second):
     share, crop, width = s_ref.shape
     half = width // 2
     left = lax.broadcasted_iota(jnp.int32, (crop, width), 1) < half
-    for copy in copies[:3]:
-        copy.wait()
     mask = mask_ref[...].astype(F32)
     mask = jnp.concatenate([mask, mask], axis=1)
     powers = []
@@ -125,30 +106,60 @@
         first[j] = jnp.where(left, s, turned)
         second[j] = jnp.where(left, turned, -s)
         powers.append(jnp.sum(s * s, axis=0, keepdims=True))
-    power = jnp.sum(jnp.concatenate(powers, axis=0), axis=1, keepdims=True)
-    split_particles(x_ref, plain, swapped)
-    for copy in copies[3:]:
+    power = jnp.sum(jnp.concatenate(powers, axis=0), axis=1, keepdims=True) * (0.5 / crop)
+    slot = lax.broadcasted_iota(jnp.int32, (1, share * TS), 1) // TS
+    spread = jnp.zeros((1, share * TS), F32)
+    for j in range(share):
+        spread = jnp.where(slot == j, power[j : j + 1], spread)
+    return spread
+
+
+def first_kernel(*refs):
+    sources, (logits_ref, lse_ref, first, second, bias_ref), kept = refs[:11], refs[11:16], refs[16:22]
+    s_ref, class_ref, orient_ref, class_prior_ref, orient_prior_ref, sems = refs[22:]
+    x_ref, mask_ref, rows_ref, columns_ref, back_rows_ref, back_columns_ref = kept
+    targets = (
+        class_ref, orient_ref, class_prior_ref, orient_prior_ref, x_ref, s_ref, mask_ref, rows_ref, columns_ref,
+        back_rows_ref, back_columns_ref,
+    )
+    copies = [pltpu.make_async_copy(a, b, sems.at[k]) for k, (a, b) in enumerate(zip(sources, targets))]
+    for copy in copies:
+        copy.start()
+    share = s_ref.shape[0]
+    for copy in copies[:4]:
         copy.wait()
     slot = lax.broadcasted_iota(jnp.int32, (1, share * TS), 1) // TS
-    bias = jnp.zeros((1, share * TS), F32)
+    prior = jnp.zeros((1, share * TS), F32)
     start = lax.axis_index("orient") * share
     for j in range(share):
-        prior = class_prior_ref[class_ref[start + j]] + orient_prior_ref[orient_ref[start + j]]
-        bias = jnp.where(slot == j, prior - power[j : j + 1] * (0.5 / crop), bias)
+        value = class_prior_ref[class_ref[start + j]] + orient_prior_ref[orient_ref[start + j]]
+        prior = jnp.where(slot == j, value, prior)
+    for copy in copies[4:7]:
+        copy.wait()
+    power = prepare_slices(s_ref, mask_ref, first, second)
+    for copy in copies[7:9]:
+        copy.wait()
+    bias = prior - power
     bias_ref[...] = jnp.broadcast_to(bias, bias_ref.shape)
-    score_block(plain, swapped, first, second, bias, rows_ref, columns_ref, cross, logits_ref, lse_ref)
-
-
-def score_kernel(
-    x_ref, first, second, bias_ref, rows_ref, columns_ref, logits_ref, lse_ref, cross, plain, swapped
-):
-    split_particles(x_ref, plain, swapped)
-    score_block(plain, swapped, first, second, bias_ref[:1], rows_ref, columns_ref, cross, logits_ref, lse_ref)
+    score_block(x_ref, first, second, bias, rows_ref, columns_ref, logits_ref, lse_ref)
+    for copy in copies[9:]:
+        copy.wait()
+
+
+def score_kernel(x_ref, first, second, bias_ref, rows_ref, columns_ref, logits_ref, lse_ref):
+    score_block(x_ref, first, second, bias_ref[:1], rows_ref, columns_ref, logits_ref, lse_ref)
 
 
 def log_add(a, b):
     top = jnp.maximum(a, b)
     return top + jnp.log(jnp.exp(a - top) + jnp.exp(b - top))
+
+
+def parity(index, limit):
+    total = index & 1
+    for b in range(1, bits(limit)):
+        total = total ^ ((index >> b) & 1)
+    return total
 
 
 def to_lanes(column):
@@ -177,10 +188,11 @@
     return terms[0:1] + terms[1:2] + terms[2:3]
 
 
-def back_kernel(share, pack, start, last, *refs):
+def back_kernel(share, pack, n_lse, start, last, *refs):
     refs = list(refs)
-    logits_ref, lse_a_ref, lse_b_ref, x_ref, rows_ref, columns_ref = refs[:6]
-    del refs[:6]
+    logits_ref, x_ref, rows_ref, columns_ref = refs[:4]
+    lse_refs = refs[4 : 4 + n_lse]
+    del refs[: 4 + n_lse]
     if not start:
         re_in, im_in, mass_in = refs[:3]
         del refs[:3]
@@ -194,7 +206,7 @@
     count, crop, width = x_ref.shape
     half = width // 2
     left = lax.broadcasted_iota(jnp.int32, (crop, width), 1) < half
-    loglik = log_add(lse_a_ref[...], lse_b_ref[...])
+    loglik = functools.reduce(log_add, [ref[...] for ref in lse_refs])
     mass = jnp.zeros((TS, share * TS), F32)
     weights = []
     for i in range(count):
@@ -220,7 +232,7 @@
         mask = mask_ref[...].astype(F32)
         mask = jnp.concatenate([mask, mask], axis=1)
         sign = jnp.where(left[:1], -1.0, 1.0)
-        odd = (lax.axis_index("dom") & 1) == 1
+        odd = parity(lax.axis_index("dom"), crop * pack // 8)
     for group in range(groups):
         re = jnp.zeros((crop, wide), F32) if start else re_in[group]
         im = jnp.zeros((crop, wide), F32) if start else im_in[group]
@@ -247,15 +259,18 @@
         ]
         for pair in range(len(tiles) // 2):
             at = (pair * groups + group) * 8
-            keep_ref[at : at + 8] = jnp.where(odd, tiles[2 * pair + 1], tiles[2 * pair])
-            send_ref[at : at + 8] = jnp.where(odd, tiles[2 * pair], tiles[2 * pair + 1])
+            even, other = tiles[2 * pair], tiles[2 * pair + 1]
+            if parity(pair, crop):
+                even, other = other, even
+            keep_ref[at : at + 8] = jnp.where(odd == 1, other, even)
+            send_ref[at : at + 8] = jnp.where(odd == 1, even, other)
     if last:
         row = lax.broadcasted_iota(jnp.int32, (share, share * TS), 0)
         lane = lax.broadcasted_iota(jnp.int32, (share, share * TS), 1)
         each = jnp.sum(jnp.where(row == lane // TS, mass, 0.0), axis=1, keepdims=True)
         mass = to_lanes(each)
         put_mass(send_ref, keep_ref.shape[0], mass)
-        loglik_ref[...] = to_lanes(loglik[:, :1])[0, :count]
+        loglik_ref[...] = jnp.broadcast_to(to_lanes(loglik[:, :1]), loglik_ref.shape)
     mass_ref[...] = jnp.broadcast_to(mass, mass_ref.shape)
 
 
@@ -274,7 +289,7 @@
     mass_ref[...] = jnp.broadcast_to(mass, mass_ref.shape)
 
 
-def last_kernel(groups, pack, keep_ref, got_ref, mass_in, image_ref, occupancy_ref):
+def last_kernel(groups, pack, keep_ref, got_ref, mass_in, loglik_in, image_ref, occupancy_ref, loglik_ref):
     block = image_ref.shape[1]
     rows = keep_ref.shape[0]
     total = keep_ref[...] + got_ref[:rows].astype(F32)
@@ -283,6 +298,7 @@
             image_ref[p * groups + g] = total[g * 8 + p * block : g * 8 + (p + 1) * block]
     mass = mass_in[:1] + get_mass(got_ref, rows)
     occupancy_ref[...] = mass[0, : occupancy_ref.shape[0]]
+    loglik_ref[...] = loglik_in[0, : loglik_ref.shape[0]]
 
 
 def bits(count):
@@ -315,33 +331,32 @@
             name=name,
         )(*args)
 
-    def swap(value, axis, size, step):
-        return lax.ppermute(value, axis, [(i, i ^ step) for i in range(size)])
+    def swap(value, r):
+        core = parity(r, n_orient)
+        pairs = [(d * n_orient + o, (d ^ core) * n_orient + (o ^ r)) for d in range(n_dom) for o in range(n_orient)]
+        return lax.ppermute(value, ("dom", "orient"), pairs)
 
     flops = 2 * count * crop * share * width * 2 * lanes
-    scored_shapes = [shape((count, TS, lanes), F32), shape((count, 128), F32)]
-    turned = pltpu.VMEM((count, crop, width), F32)
-    score_scratch = [pltpu.VMEM((count * crop, share * width), BF16), turned, turned]
+    logits_shape, lse_shape = shape((count, TS, lanes), F32), shape((count, 128), F32)
     slices_shape = shape(slices.shape, F32)
     score_rows, score_columns, back_rows, back_columns = tables
 
-    slots = [particles] + [swap(particles, "orient", n_orient, r) for r in range(1, n_orient)]
+    slots = [particles] + [swap(particles, r) for r in range(1, n_orient)]
     kept = (particles, freq_mask, *tables)
     logits, lse, first, second, bias, mine, mask, *tables = call(
         first_kernel,
-        [*scored_shapes, slices_shape, slices_shape, shape((8, lanes), F32)]
+        [logits_shape, lse_shape, slices_shape, slices_shape, shape((8, lanes), F32)]
         + [shape(value.shape, value.dtype) for value in kept],
         tuple(
             pltpu.with_memory_space_constraint(value, pltpu.HBM)
             for value in (
-                particles, slices, freq_mask, score_rows, score_columns, slice_class, slice_orient, class_prior,
-                orient_prior, back_rows, back_columns,
+                slice_class, slice_orient, class_prior, orient_prior, particles, slices, freq_mask, score_rows,
+                score_columns, back_rows, back_columns,
             )
         ),
         [
             pltpu.VMEM(slices.shape, slices.dtype),
             *[pltpu.SMEM(v.shape, v.dtype) for v in (slice_class, slice_orient, class_prior, orient_prior)],
-            *score_scratch,
             pltpu.SemaphoreType.DMA((11,)),
         ],
         specs=[hbm] * 11, flops=flops, name="first",
@@ -350,16 +365,15 @@
     slots[0] = mine
     scored = [(logits, lse)] + [
         call(
-            score_kernel, scored_shapes, (parts, first, second, bias, score_rows, score_columns), score_scratch,
+            score_kernel, [logits_shape, lse_shape], (parts, first, second, bias, score_rows, score_columns), [],
             flops=flops, name="score",
         )
         for parts in slots[1:]
     ]
-    lses = [s[1] for s in scored]
+    terms = [[s[1]] for s in scored]
     for b in range(bits(n_orient)):
-        theirs = [swap(lses[r ^ (1 << b)], "orient", n_orient, 1 << b) for r in range(n_orient)]
-        if b < bits(n_orient) - 1:
-            lses = [log_add(x, y) for x, y in zip(lses, theirs)]
+        sums = [functools.reduce(log_add, t) for t in terms]
+        terms = [[sums[r], swap(sums[r ^ (1 << b)], 1 << b)] for r in range(n_orient)]
 
     rows = crop // block * groups * 8
     steps = bits(n_dom)
@@ -370,34 +384,39 @@
 
     sums = shape((groups, crop, pack * width), F32)
     mass_shape = shape((8, lanes), F32)
+    turned = pltpu.VMEM((count, crop, width), F32)
     back_scratch = [turned, turned] + [pltpu.VMEM((count * TS, 2 * share * width), BF16)] * 2
     partial = ()
     for r in range(1, n_orient):
         partial = call(
-            functools.partial(back_kernel, share, pack, r == 1, False),
+            functools.partial(back_kernel, share, pack, len(terms[r]), r == 1, False),
             [sums, sums, mass_shape],
-            (scored[r][0], lses[r], theirs[r], slots[r], back_rows, back_columns, *partial),
+            (scored[r][0], slots[r], back_rows, back_columns, *terms[r], *partial),
             back_scratch, flops=flops, name="back",
         )
     keep, send, mass, loglik = call(
-        functools.partial(back_kernel, share, pack, False, True),
-        [shape((rows // 2, width), F32), sent(0, rows // 2), shape((8, 128), F32), shape((count,), F32)],
-        (scored[0][0], lses[0], theirs[0], slots[0], back_rows, back_columns, *partial, mask),
+        functools.partial(back_kernel, share, pack, len(terms[0]), False, True),
+        [shape((rows // 2, width), F32), sent(0, rows // 2), shape((8, 128), F32), shape((8, 128), F32)],
+        (scored[0][0], slots[0], back_rows, back_columns, *terms[0], *partial, mask),
         back_scratch, flops=flops, name="last_back",
     )
+    def exchange(value, b):
+        step = 1 << b | 1
+        return lax.ppermute(value, "dom", [(i, i ^ step) for i in range(n_dom)])
+
     for b in range(steps - 1):
-        got = swap(send, "dom", n_dom, 1 << b)
+        got = exchange(send, b)
         height = keep.shape[0] // 2
         keep, send, mass = call(
             functools.partial(halve_kernel, groups, b + 1),
             [shape((height, width), F32), sent(b + 1, height), shape((8, 128), F32)],
             (keep, got, mass), [], name="halve",
         )
-    got = swap(send, "dom", n_dom, n_dom // 2)
-    image, occupancy = call(
+    got = exchange(send, steps - 1)
+    image, occupancy, loglik = call(
         functools.partial(last_kernel, groups, pack),
-        [shape((share, block, width), F32), shape((share,), F32)],
-        (keep, got, mass), [], name="last",
+        [shape((share, block, width), F32), shape((share,), F32), shape((count,), F32)],
+        (keep, got, mass, loglik), [], name="last",
     )
     return image, occupancy, loglik
 

time: 28.2 us -> 25.9 us (0.918)
  waiting for transfers between devices: 9.58 us -> 8.17 us
  Pallas kernels: 6.29 us -> 5.4 us
    ppermute x7, waiting for transfers between devices: 9.58 us -> 8.17 us  [the longest x4 5.68 us: exchange(): return lax.ppermute(value, 'dom', [(i, i ^ step) for i in range(n_dom)])]
    pallas_call x8, Pallas kernels: 6.29 us -> 5.4 us  [call(): pl.pallas_call(kernel, out_shape=tuple(outs), in_specs=specs or [vmem] *...]
where the time goes in v3:
time: 25.9 us; the launch traced here: 25.7 us
  starting transfers between devices  11.5 us (44%)
  waiting for transfers between devices  8.17 us (32%)
  Pallas kernels  5.4 us (21%)
  between operations  0.67 us (3%)
    ppermute x4, starting transfers between devices, exchange(): return lax.ppermute(value, 'dom', [(i, i ^ step) for i in range(n_dom)])  6.84 us
    ppermute x4, waiting for transfers between devices, exchange(): return lax.ppermute(value, 'dom', [(i, i ^ step) for i in range(n_dom)])  5.68 us
    pallas_call x8, Pallas kernels, call(): pl.pallas_call(kernel, out_shape=tuple(outs), in_specs=specs or [vmem] *...  5.4 us
    ppermute x3, starting transfers between devices, swap(): return lax.ppermute(value, ('dom', 'orient'), pairs)  4.64 us
    ppermute x3, waiting for transfers between devices, swap(): return lax.ppermute(value, ('dom', 'orient'), pairs)  2.49 us
  transfers between devices with their start and end apart: 7, of which 6 were waited for; matrix products, arithmetic and copies ran while one was open for 0% of the time, Pallas kernels for 15%

profile of v3, /device:TPU:0, one launch (start us, length us, event | category | flops | bytes accessed | tf_op | source)
XLA Modules:
  0.0 25.7 jit_solution(6257339429524802597)
XLA Ops:
  0.6 2.4 %collective-permute-start = (bf16[8,64,128]{2,1,0:T(8,128)(2,1)}, bf16[8,64,128]{2,1,0:T(8,128)(2,1)S(1)}, u32[]{:S(2)}, u32[]{:S(2)}) collective-permute-start(bf16[8,64,128]{2,1,0:T(8,128)(2,1)} %refs_4_.1), channel_id=1, source_target_pairs={{0,3},{1,2},{2,1},{3,0},{4,7},{5,6},{6,5},{7,4},{8,11},{9,10},{10,... | collective-permute-start | bytes 393224 | tf_op jit(solution)/shard_map/ppermute | solution.py:337
  3.1 2.2 %first.1 = (f32[8,16,128]{2,1,0:T(8,128)S(1)}, f32[8,128]{1,0:T(8,128)S(1)}, f32[8,64,128]{2,1,0:T(8,128)S(1)}, f32[8,64,128]{2,1,0:T(8,128)S(1)}, f32[8,128]{1,...) custom-call(s32[16]{0:T(128)} %refs_0_.1, ...), custom_call_target="tpu_custom_call" | custom-call | flops 268435456 | bytes 1048576 | tf_op jit(solution)/shard_map/first/pallas_call | solution.py:323
  5.3 0.1 collective-permute-start.2
  5.4 1.9 %collective-permute-done.x_ref.refs_1_ = bf16[8,64,128]{2,1,0:T(8,128)(2,1)S(1)} collective-permute-done((bf16[8,64,128]{2,1,0:T(8,128)(2,1)}, bf16[8,64,128]{2,1,0:T(8,128)(2,1)S(1)}, u32[]{:S(2)}, u32[]{:S(2)}) %collective-permute-start) | collective-permute-done | bytes 131104 | tf_op jit(solution)/shard_map/ppermute | solution.py:337
  7.3 0.9 %score.1 = (f32[8,16,128]{2,1,0:T(8,128)S(1)}, f32[8,128]{1,0:T(8,128)S(1)}) custom-call(bf16[8,64,128]{2,1,0:T(8,128)(2,1)S(1)} %collective-permute-done.x_ref.refs_1_, f32[8,64,128]{2,1,0:T(8,128)S(1)} %get-tuple-element.37.first, f32[8,64,128]{2,1,0:T(8,128)S(1)} %get-tuple-element.38.second, f32[8,128]{1,0:T(8,128)S(1)} %get-tuple-element.39.bias_ref, ...), custom_call_target="tpu_custom_call" | custom-call | flops 268435456 | bytes 1048576 | tf_op jit(solution)/shard_map/score/pallas_call | solution.py:323
  8.2 2.1 %collective-permute-start.1 = (f32[8,128]{1,0:T(8,128)S(1)}, f32[8,128]{1,0:T(8,128)S(1)}, u32[]{:S(2)}, u32[]{:S(2)}) collective-permute-start(f32[8,128]{1,0:T(8,128)S(1)} %get-tuple-element.42.refs_4_), channel_id=1, source_target_pairs={{0,3},{1,2},{2,1},{3,0},{4,7},{5,6},{6,5},{7,4},{8,11},{9,10},{10,... | collective-permute-start | bytes 12296 | tf_op jit(solution)/shard_map/ppermute | solution.py:337
  10.3 0.0 collective-permute-done.2.refs_5_
  10.3 0.7 %back.1 = (f32[4,64,256]{2,1,0:T(8,128)S(1)}, f32[4,64,256]{2,1,0:T(8,128)S(1)}, f32[8,128]{1,0:T(8,128)S(1)}) custom-call(f32[8,16,128]{2,1,0:T(8,128)S(1)} %get-tuple-element.43.refs_0_, bf16[8,64,128]{2,1,0:T(8,128)(2,1)S(1)} %collective-permute-done.x_ref.refs_1_, bf16[128,2048]{1,0:T(8,128)(2,1)S(1)} %get-tuple-element.34.refs_2_, ...), custom_call_target="tpu_custom_call" | custom-call | flops 268435456 | bytes 1048576 | tf_op jit(solution)/shard_map/back/pallas_call | solution.py:323
  11.0 0.6 %collective-permute-done.1.refs_5_ = f32[8,128]{1,0:T(8,128)S(1)} collective-permute-done((f32[8,128]{1,0:T(8,128)S(1)}, f32[8,128]{1,0:T(8,128)S(1)}, u32[]{:S(2)}, u32[]{:S(2)}) %collective-permute-start.1) | collective-permute-done | bytes 4128 | tf_op jit(solution)/shard_map/ppermute | solution.py:337
  11.7 0.8 %last_back.1 = (f32[256,128]{1,0:T(8,128)S(1)}, f32[264,128]{1,0:T(8,128)S(1)}, f32[8,128]{1,0:T(8,128)S(1)}, f32[8,128]{1,0:T(8,128)S(1)}) custom-call(f32[8,16,128]{2,1,0:T(8,128)S(1)} %get-tuple-element.32.refs_0_, bf16[8,64,128]{2,1,0:T(8,128)(2,1)S(1)} %get-tuple-element.33.refs_1_, bf16[128,2048]{1,0:T(8,128)(2,1)S(1)} %get-tuple-element.34.refs_2_, ...), custom_call_target="tpu_custom_call" | custom-call | flops 268435456 | bytes 1048576 | tf_op jit(solution)/shard_map/last_back/pallas_call | solution.py:323
  12.5 0.4 %collective-permute-start.3 = (f32[264,128]{1,0:T(8,128)S(1)}, f32[264,128]{1,0:T(8,128)S(1)}, u32[]{:S(2)}, u32[]{:S(2)}) collective-permute-start(f32[264,128]{1,0:T(8,128)S(1)} %get-tuple-element.49), channel_id=1, source_target_pairs={{0,2},{2,0},{4,6},{6,4},{8,10},{10,8},{12,14},{14,12},{16,18},{18,... | collective-permute-start | bytes 405512 | tf_op jit(solution)/shard_map/ppermute | solution.py:405
  12.9 1.0 %collective-permute-done.3.got_ref = f32[264,128]{1,0:T(8,128)S(1)} collective-permute-done((f32[264,128]{1,0:T(8,128)S(1)}, f32[264,128]{1,0:T(8,128)S(1)}, u32[]{:S(2)}, u32[]{:S(2)}) %collective-permute-start.3) | collective-permute-done | bytes 135200 | tf_op jit(solution)/shard_map/ppermute | solution.py:405
  14.0 1.8 %collective-permute-start.4 = (bf16[144,128]{1,0:T(8,128)(2,1)S(1)}, bf16[144,128]{1,0:T(8,128)(2,1)S(1)}, u32[]{:S(2)}, u32[]{:S(2)}) collective-permute-start(bf16[144,128]{1,0:T(8,128)(2,1)S(1)} %get-tuple-element.52), channel_id=1, source_target_pairs={{0,6},{2,4},{4,2},{6,0},{8,14},{10,12},{12,10},{14,8},{16,22},{18,... | collective-permute-start | bytes 110600 | tf_op jit(solution)/shard_map/ppermute | solution.py:405
  15.7 1.7 %collective-permute-done.4.got_ref = bf16[144,128]{1,0:T(8,128)(2,1)S(1)} collective-permute-done((bf16[144,128]{1,0:T(8,128)(2,1)S(1)}, bf16[144,128]{1,0:T(8,128)(2,1)S(1)}, u32[]{:S(2)}, u32[]{:S(2)}) %collective-permute-start.4) | collective-permute-done | bytes 36896 | tf_op jit(solution)/shard_map/ppermute | solution.py:405
  17.4 1.9 %collective-permute-start.5 = (bf16[80,128]{1,0:T(8,128)(2,1)S(1)}, bf16[80,128]{1,0:T(8,128)(2,1)S(1)}, u32[]{:S(2)}, u32[]{:S(2)}) collective-permute-start(bf16[80,128]{1,0:T(8,128)(2,1)S(1)} %get-tuple-element.55), channel_id=1, source_target_pairs={{0,10},{2,8},{4,14},{6,12},{8,2},{10,0},{12,6},{14,4},{16,26},{18,... | collective-permute-start | bytes 61448 | tf_op jit(solution)/shard_map/ppermute | solution.py:405
  19.3 1.5 %collective-permute-done.5.got_ref = bf16[80,128]{1,0:T(8,128)(2,1)S(1)} collective-permute-done((bf16[80,128]{1,0:T(8,128)(2,1)S(1)}, bf16[80,128]{1,0:T(8,128)(2,1)S(1)}, u32[]{:S(2)}, u32[]{:S(2)}) %collective-permute-start.5) | collective-permute-done | bytes 20512 | tf_op jit(solution)/shard_map/ppermute | solution.py:405
  20.8 2.8 %collective-permute-start.6 = (f32[40,128]{1,0:T(8,128)S(1)}, f32[40,128]{1,0:T(8,128)S(1)}, u32[]{:S(2)}, u32[]{:S(2)}) collective-permute-start(f32[40,128]{1,0:T(8,128)S(1)} %get-tuple-element.58), channel_id=1, source_target_pairs={{0,18},{2,16},{4,22},{6,20},{8,26},{10,24},{12,30},{14,28},{16,2},... | collective-permute-start | bytes 61448 | tf_op jit(solution)/shard_map/ppermute | solution.py:405
  23.6 1.5 %collective-permute-done.6.got_ref = f32[40,128]{1,0:T(8,128)S(1)} collective-permute-done((f32[40,128]{1,0:T(8,128)S(1)}, f32[40,128]{1,0:T(8,128)S(1)}, u32[]{:S(2)}, u32[]{:S(2)}) %collective-permute-start.6) | collective-permute-done | bytes 20512 | tf_op jit(solution)/shard_map/ppermute | solution.py:405
  25.1 0.6 %last.1 = (f32[8,4,128]{2,1,0:T(4,128)}, f32[8]{0:T(128)}, f32[8]{0:T(128)}) custom-call(f32[32,128]{1,0:T(8,128)S(1)} %get-tuple-element.57.keep_ref, f32[40,128]{1,0:T(8,128)S(1)} %collective-permute-done.6.got_ref, f32[8,128]{1,0:T(8,128)S(1)} %get-tuple-element.59.mass_in, f32[8,128]{1,0:T(8,128)S(1)} %get-tuple-element.60.loglik_in), custom_call_target="tpu_custom_call" | custom-call | bytes 1048576 | tf_op jit(solution)/shard_map/last/pallas_call | solution.py:323
  (3 shorter events, 0.1 us)
Async XLA Ops:
  0.6 6.6 %collective-permute-start = (bf16[8,64,128]{2,1,0:T(8,128)(2,1)}, bf16[8,64,128]{2,1,0:T(8,128)(2,1)S(1)}, u32[]{:S(2)}, u32[]{:S(2)}) collective-permute-start(bf16[8,64,128]{2,1,0:T(8,128)(2,1)} %refs_4_.1), channel_id=1, source_target_pairs={{0,3},{1,2},{2,1},{3,0},{4,7},{5,6},{6,5},{7,4},{8,11},{9,10},{10,... | collective-permute-start | bytes 393224 | tf_op jit(solution)/shard_map/ppermute | solution.py:337
  5.3 5.0 %collective-permute-start.2 = (f32[8,128]{1,0:T(8,128)S(1)}, f32[8,128]{1,0:T(8,128)S(1)}, u32[]{:S(2)}, u32[]{:S(2)}) collective-permute-start(f32[8,128]{1,0:T(8,128)S(1)} %get-tuple-element.36.refs_4_), channel_id=1, source_target_pairs={{0,3},{1,2},{2,1},{3,0},{4,7},{5,6},{6,5},{7,4},{8,11},{9,10},{10,... | collective-permute-start | bytes 12296 | tf_op jit(solution)/shard_map/ppermute | solution.py:337
  8.2 3.4 %collective-permute-start.1 = (f32[8,128]{1,0:T(8,128)S(1)}, f32[8,128]{1,0:T(8,128)S(1)}, u32[]{:S(2)}, u32[]{:S(2)}) collective-permute-start(f32[8,128]{1,0:T(8,128)S(1)} %get-tuple-element.42.refs_4_), channel_id=1, source_target_pairs={{0,3},{1,2},{2,1},{3,0},{4,7},{5,6},{6,5},{7,4},{8,11},{9,10},{10,... | collective-permute-start | bytes 12296 | tf_op jit(solution)/shard_map/ppermute | solution.py:337
  12.5 1.4 %collective-permute-start.3 = (f32[264,128]{1,0:T(8,128)S(1)}, f32[264,128]{1,0:T(8,128)S(1)}, u32[]{:S(2)}, u32[]{:S(2)}) collective-permute-start(f32[264,128]{1,0:T(8,128)S(1)} %get-tuple-element.49), channel_id=1, source_target_pairs={{0,2},{2,0},{4,6},{6,4},{8,10},{10,8},{12,14},{14,12},{16,18},{18,... | collective-permute-start | bytes 405512 | tf_op jit(solution)/shard_map/ppermute | solution.py:405
  14.0 3.4 %collective-permute-start.4 = (bf16[144,128]{1,0:T(8,128)(2,1)S(1)}, bf16[144,128]{1,0:T(8,128)(2,1)S(1)}, u32[]{:S(2)}, u32[]{:S(2)}) collective-permute-start(bf16[144,128]{1,0:T(8,128)(2,1)S(1)} %get-tuple-element.52), channel_id=1, source_target_pairs={{0,6},{2,4},{4,2},{6,0},{8,14},{10,12},{12,10},{14,8},{16,22},{18,... | collective-permute-start | bytes 110600 | tf_op jit(solution)/shard_map/ppermute | solution.py:405
  17.4 3.4 %collective-permute-start.5 = (bf16[80,128]{1,0:T(8,128)(2,1)S(1)}, bf16[80,128]{1,0:T(8,128)(2,1)S(1)}, u32[]{:S(2)}, u32[]{:S(2)}) collective-permute-start(bf16[80,128]{1,0:T(8,128)(2,1)S(1)} %get-tuple-element.55), channel_id=1, source_target_pairs={{0,10},{2,8},{4,14},{6,12},{8,2},{10,0},{12,6},{14,4},{16,26},{18,... | collective-permute-start | bytes 61448 | tf_op jit(solution)/shard_map/ppermute | solution.py:405
  20.8 4.3 %collective-permute-start.6 = (f32[40,128]{1,0:T(8,128)S(1)}, f32[40,128]{1,0:T(8,128)S(1)}, u32[]{:S(2)}, u32[]{:S(2)}) collective-permute-start(f32[40,128]{1,0:T(8,128)S(1)} %get-tuple-element.58), channel_id=1, source_target_pairs={{0,18},{2,16},{4,22},{6,20},{8,26},{10,24},{12,30},{14,28},{16,2},... | collective-permute-start | bytes 61448 | tf_op jit(solution)/shard_map/ppermute | solution.py:405

commit v4 on v3

--- a/solution.py
+++ b/solution.py
@@ -188,89 +188,145 @@
     return terms[0:1] + terms[1:2] + terms[2:3]
 
 
-def back_kernel(share, pack, n_lse, start, last, *refs):
+def double_particles(x_ref, doubled_re, doubled_im):
+    count, crop, width = x_ref.shape
+    left = lax.broadcasted_iota(jnp.int32, (crop, width), 1) < width // 2
+    for i in range(count):
+        x = x_ref[i].astype(F32)
+        turned = pltpu.roll(x, width // 2, 1)
+        doubled_re[i] = jnp.where(left, x, turned)
+        doubled_im[i] = jnp.where(left, turned, x)
+
+
+def put_spread(spread, high, low):
+    rounded = spread.astype(BF16)
+    high[...] = rounded
+    low[...] = (spread - rounded.astype(F32)).astype(BF16)
+
+
+def kernel_of(high, low, columns, k, group, wide):
+    rows = slice(k * TS, (k + 1) * TS)
+    here = slice(group * wide, (group + 1) * wide)
+    there = slice(high.shape[1] // 2 + group * wide, high.shape[1] // 2 + (group + 1) * wide)
+    a, b = high[rows, here], high[rows, there]
+    terms = jnp.concatenate([a, b, low[rows, here], low[rows, there], a, b], axis=0)
+    return jnp.dot(columns, terms, preferred_element_type=F32)
+
+
+def put_images(re, im, mask, odd, pack, group, groups, out_ref, at):
+    crop, width = mask.shape
+    half = width // 2
+    signed = jnp.where(lax.broadcasted_iota(jnp.int32, (1, width), 1) < half, -mask, mask)
+    images = []
+    for p in range(pack):
+        here = slice(p * width, (p + 1) * width)
+        images.append(re[:, here] * mask + pltpu.roll(im[:, here], half, 1) * signed)
+    block = 8 // pack
+    tiles = [jnp.concatenate([image[r : r + block] for image in images], axis=0) for r in range(0, crop, block)]
+    pairs = len(tiles) // 2
+    for pair in range(pairs):
+        even, other = tiles[2 * pair], tiles[2 * pair + 1]
+        if parity(pair, crop):
+            even, other = other, even
+        kept, given = at + (pair * groups + group) * 8, at + ((pairs + pair) * groups + group) * 8
+        out_ref[kept : kept + 8] = jnp.where(odd == 1, other, even)
+        out_ref[given : given + 8] = jnp.where(odd == 1, even, other)
+
+
+def twice_mask(mask_ref):
+    mask = mask_ref[...].astype(F32)
+    return jnp.concatenate([mask, mask], axis=1)
+
+
+def own_kernel(
+    share, pack, logits_ref, lse_ref, x_ref, mask_ref, rows_ref, columns_ref, out_ref, doubled_re, doubled_im, high, low
+):
+    count, crop, width = x_ref.shape
+    double_particles(x_ref, doubled_re, doubled_im)
+    weights = jnp.concatenate([jnp.exp(logits_ref[i] - lse_ref[i : i + 1, :]) for i in range(count)], axis=0)
+    rounded = weights.astype(BF16)
+    rest = (weights - rounded.astype(F32)).astype(BF16)
+    rows = rows_ref[...]
+    put_spread(
+        jnp.dot(rounded, rows, preferred_element_type=F32) + jnp.dot(rest, rows, preferred_element_type=F32), high, low
+    )
+    columns = columns_ref[...]
+    mask = twice_mask(mask_ref)
+    odd = parity(lax.axis_index("dom"), crop * pack // 8)
+    height = crop * share
+    for group in range(share // pack):
+        for k in range(count):
+            kernel = kernel_of(high, low, columns, k, group, pack * width)
+            re = kernel * jnp.concatenate([doubled_re[k]] * pack, axis=1)
+            im = kernel * jnp.concatenate([doubled_im[k]] * pack, axis=1)
+            put_images(re, im, mask, odd, pack, group, share // pack, out_ref, k * height)
+
+
+def back_kernel(share, pack, start, n_lse, *refs):
     refs = list(refs)
-    logits_ref, x_ref, rows_ref, columns_ref = refs[:4]
-    lse_refs = refs[4 : 4 + n_lse]
-    del refs[: 4 + n_lse]
+    logits_ref, x_ref, mask_ref, rows_ref, columns_ref = refs[:5]
+    lse_refs = refs[5 : 5 + n_lse]
+    del refs[: 5 + n_lse]
     if not start:
-        re_in, im_in, mass_in = refs[:3]
-        del refs[:3]
-    if last:
-        mask_ref, keep_ref, send_ref, mass_ref, loglik_ref = refs[:5]
-        del refs[:5]
-    else:
-        re_ref, im_ref, mass_ref = refs[:3]
-        del refs[:3]
-    doubled_re, doubled_im, high, low = refs
+        out_in, mass_in = refs[:2]
+        del refs[:2]
+    out_ref, mass_ref, doubled_re, doubled_im, high, low = refs
     count, crop, width = x_ref.shape
-    half = width // 2
-    left = lax.broadcasted_iota(jnp.int32, (crop, width), 1) < half
     loglik = functools.reduce(log_add, [ref[...] for ref in lse_refs])
+    double_particles(x_ref, doubled_re, doubled_im)
     mass = jnp.zeros((TS, share * TS), F32)
     weights = []
     for i in range(count):
         weight = jnp.exp(logits_ref[i] - loglik[i : i + 1, :]).astype(BF16)
         mass = mass + weight.astype(F32)
         weights.append(weight)
-        x = x_ref[i].astype(F32)
-        turned = pltpu.roll(x, half, 1)
-        doubled_re[i] = jnp.where(left, x, turned)
-        doubled_im[i] = jnp.where(left, turned, x)
     mass = jnp.sum(mass, axis=0, keepdims=True)
     if not start:
         mass = mass + mass_in[:1]
-    spread = jnp.dot(jnp.concatenate(weights, axis=0), rows_ref[...], preferred_element_type=F32)
-    rounded = spread.astype(BF16)
-    high[...] = rounded
-    low[...] = (spread - rounded.astype(F32)).astype(BF16)
-    forms = share * width
+    mass_ref[...] = jnp.broadcast_to(mass, mass_ref.shape)
+    put_spread(jnp.dot(jnp.concatenate(weights, axis=0), rows_ref[...], preferred_element_type=F32), high, low)
     wide = pack * width
-    groups = share // pack
     columns = columns_ref[...]
-    if last:
-        mask = mask_ref[...].astype(F32)
-        mask = jnp.concatenate([mask, mask], axis=1)
-        sign = jnp.where(left[:1], -1.0, 1.0)
-        odd = parity(lax.axis_index("dom"), crop * pack // 8)
-    for group in range(groups):
-        re = jnp.zeros((crop, wide), F32) if start else re_in[group]
-        im = jnp.zeros((crop, wide), F32) if start else im_in[group]
+    mask = twice_mask(mask_ref)
+    odd = parity(lax.axis_index("dom"), crop * pack // 8)
+    for group in range(share // pack):
+        re = jnp.zeros((crop, wide), F32)
+        im = jnp.zeros((crop, wide), F32)
         for k in range(count):
-            rows = slice(k * TS, (k + 1) * TS)
-            here = slice(group * wide, (group + 1) * wide)
-            there = slice(forms + group * wide, forms + (group + 1) * wide)
-            a, b = high[rows, here], high[rows, there]
-            terms = jnp.concatenate([a, b, low[rows, here], low[rows, there], a, b], axis=0)
-            kernel = jnp.dot(columns, terms, preferred_element_type=F32)
+            kernel = kernel_of(high, low, columns, k, group, wide)
             re = re + kernel * jnp.concatenate([doubled_re[k]] * pack, axis=1)
             im = im + kernel * jnp.concatenate([doubled_im[k]] * pack, axis=1)
-        if not last:
-            re_ref[group] = re
-            im_ref[group] = im
-            continue
-        images = []
-        for p in range(pack):
-            here = slice(p * width, (p + 1) * width)
-            images.append((re[:, here] + pltpu.roll(im[:, here], half, 1) * sign) * mask)
-        block = 8 // pack
-        tiles = [
-            jnp.concatenate([image[at : at + block] for image in images], axis=0) for at in range(0, crop, block)
-        ]
-        for pair in range(len(tiles) // 2):
-            at = (pair * groups + group) * 8
-            even, other = tiles[2 * pair], tiles[2 * pair + 1]
-            if parity(pair, crop):
-                even, other = other, even
-            keep_ref[at : at + 8] = jnp.where(odd == 1, other, even)
-            send_ref[at : at + 8] = jnp.where(odd == 1, even, other)
-    if last:
-        row = lax.broadcasted_iota(jnp.int32, (share, share * TS), 0)
-        lane = lax.broadcasted_iota(jnp.int32, (share, share * TS), 1)
-        each = jnp.sum(jnp.where(row == lane // TS, mass, 0.0), axis=1, keepdims=True)
-        mass = to_lanes(each)
-        put_mass(send_ref, keep_ref.shape[0], mass)
-        loglik_ref[...] = jnp.broadcast_to(to_lanes(loglik[:, :1]), loglik_ref.shape)
+        put_images(re, im, mask, odd, pack, group, share // pack, out_ref, 0)
+    if not start:
+        out_ref[...] = out_ref[...] + out_in[...]
+
+
+def last_back_kernel(share, n_lse, logits_ref, lse_ref, own_ref, sum_ref, mass_in, *refs):
+    lse_refs = refs[:n_lse]
+    keep_ref, send_ref, mass_ref, loglik_ref = refs[n_lse:]
+    count = logits_ref.shape[0]
+    loglik = functools.reduce(log_add, [ref[...] for ref in lse_refs])
+    factor = jnp.exp(lse_ref[...] - loglik)
+    mass = jnp.zeros((TS, share * TS), F32)
+    for i in range(count):
+        mass = mass + jnp.exp(logits_ref[i] - loglik[i : i + 1, :]).astype(BF16).astype(F32)
+    mass = jnp.sum(mass, axis=0, keepdims=True) + mass_in[:1]
+    row = lax.broadcasted_iota(jnp.int32, (share, share * TS), 0)
+    lane = lax.broadcasted_iota(jnp.int32, (share, share * TS), 1)
+    mass = to_lanes(jnp.sum(jnp.where(row == lane // TS, mass, 0.0), axis=1, keepdims=True))
+    height = sum_ref.shape[0]
+    half = height // 2
+    factors = [jnp.broadcast_to(factor[i : i + 1, :], (8, factor.shape[1])) for i in range(count)]
+    for at in range(0, height, 8):
+        total = sum_ref[at : at + 8]
+        for i in range(count):
+            total = total + own_ref[i * height + at : i * height + at + 8] * factors[i]
+        if at < half:
+            keep_ref[at : at + 8] = total
+        else:
+            send_ref[at - half : at - half + 8] = total
+    put_mass(send_ref, half, mass)
+    loglik_ref[...] = jnp.broadcast_to(to_lanes(loglik[:, :1]), loglik_ref.shape)
     mass_ref[...] = jnp.broadcast_to(mass, mass_ref.shape)
 
 
@@ -289,16 +345,27 @@
     mass_ref[...] = jnp.broadcast_to(mass, mass_ref.shape)
 
 
-def last_kernel(groups, pack, keep_ref, got_ref, mass_in, loglik_in, image_ref, occupancy_ref, loglik_ref):
+def last_kernel(
+    groups, pack, keep_ref, got_ref, mass_in, loglik_in, image_out, occupancy_out, loglik_out,
+    image_ref, occupancy_ref, loglik_ref, sems,
+):
+    loglik_ref[...] = loglik_in[0, : loglik_ref.shape[0]]
+    copies = [pltpu.make_async_copy(loglik_ref, loglik_out, sems.at[0])]
+    copies[0].start()
     block = image_ref.shape[1]
     rows = keep_ref.shape[0]
     total = keep_ref[...] + got_ref[:rows].astype(F32)
     for g in range(groups):
         for p in range(pack):
             image_ref[p * groups + g] = total[g * 8 + p * block : g * 8 + (p + 1) * block]
+    copies.append(pltpu.make_async_copy(image_ref, image_out, sems.at[1]))
+    copies[1].start()
     mass = mass_in[:1] + get_mass(got_ref, rows)
     occupancy_ref[...] = mass[0, : occupancy_ref.shape[0]]
-    loglik_ref[...] = loglik_in[0, : loglik_ref.shape[0]]
+    copies.append(pltpu.make_async_copy(occupancy_ref, occupancy_out, sems.at[2]))
+    copies[2].start()
+    for copy in copies:
+        copy.wait()
 
 
 def bits(count):
@@ -319,12 +386,12 @@
     order = [p * groups + g for g in range(groups) for p in range(pack)]
     tables = [jnp.asarray(t) for t in (*score_tables(crop, share), *back_tables(crop, share, order))]
 
-    def call(kernel, outs, args, scratch, specs=None, flops=0, name=None):
+    def call(kernel, outs, args, scratch, specs=None, outs_in=vmem, flops=0, name=None):
         return pl.pallas_call(
             kernel,
             out_shape=tuple(outs),
             in_specs=specs or [vmem] * len(args),
-            out_specs=(vmem,) * len(outs),
+            out_specs=(outs_in,) * len(outs),
             scratch_shapes=scratch,
             compiler_params=params,
             cost_estimate=pl.CostEstimate(flops=flops, bytes_accessed=1 << 20, transcendentals=0),
@@ -382,24 +449,27 @@
         dtype = F32 if step in (0, steps - 1) else BF16
         return shape((height + (8 if dtype == F32 else 16), width), dtype)
 
-    sums = shape((groups, crop, pack * width), F32)
     mass_shape = shape((8, lanes), F32)
     turned = pltpu.VMEM((count, crop, width), F32)
     back_scratch = [turned, turned] + [pltpu.VMEM((count * TS, 2 * share * width), BF16)] * 2
+    owns, = call(
+        functools.partial(own_kernel, share, pack), [shape((count * rows, width), F32)],
+        (*scored[0], slots[0], mask, back_rows, back_columns), back_scratch, flops=flops, name="own",
+    )
     partial = ()
     for r in range(1, n_orient):
         partial = call(
-            functools.partial(back_kernel, share, pack, len(terms[r]), r == 1, False),
-            [sums, sums, mass_shape],
-            (scored[r][0], slots[r], back_rows, back_columns, *terms[r], *partial),
+            functools.partial(back_kernel, share, pack, r == 1, len(terms[r])),
+            [shape((rows, width), F32), mass_shape],
+            (scored[r][0], slots[r], mask, back_rows, back_columns, *terms[r], *partial),
             back_scratch, flops=flops, name="back",
         )
     keep, send, mass, loglik = call(
-        functools.partial(back_kernel, share, pack, len(terms[0]), False, True),
+        functools.partial(last_back_kernel, share, len(terms[0])),
         [shape((rows // 2, width), F32), sent(0, rows // 2), shape((8, 128), F32), shape((8, 128), F32)],
-        (scored[0][0], slots[0], back_rows, back_columns, *terms[0], *partial, mask),
-        back_scratch, flops=flops, name="last_back",
-    )
+        (*scored[0], owns, *partial, *terms[0]), [], flops=flops, name="last_back",
+    )
+
     def exchange(value, b):
         step = 1 << b | 1
         return lax.ppermute(value, "dom", [(i, i ^ step) for i in range(n_dom)])
@@ -416,7 +486,12 @@
     image, occupancy, loglik = call(
         functools.partial(last_kernel, groups, pack),
         [shape((share, block, width), F32), shape((share,), F32), shape((count,), F32)],
-        (keep, got, mass, loglik), [], name="last",
+        (keep, got, mass, loglik),
+        [
+            pltpu.VMEM((share, block, width), F32), pltpu.VMEM((share,), F32), pltpu.VMEM((count,), F32),
+            pltpu.SemaphoreType.DMA((3,)),
+        ],
+        outs_in=hbm, name="last",
     )
     return image, occupancy, loglik
 

time: 25.9 us -> 25.3 us (0.977)
  waiting for transfers between devices: 8.17 us -> 6.76 us
  Pallas kernels: 5.4 us -> 6.17 us
    ppermute x3, waiting for transfers between devices: 2.49 us -> 1.09 us  [swap(): return lax.ppermute(value, ('dom', 'orient'), pairs)]
    pallas_call x8 -> x9, Pallas kernels: 5.4 us -> 6.17 us  [call(): pl.pallas_call(kernel, out_shape=tuple(outs), in_specs=specs or [vmem] *...]
  transfers between devices with their start and end apart: 7 -> 7, of which waited for: 6 -> 6; matrix products, arithmetic and copies ran while one was open for 0% -> 0% of each run, Pallas kernels for 15% -> 21%
where the time goes in v4:
time: 25.3 us; the launch traced here: 25.1 us
  starting transfers between devices  11.5 us (45%)
  waiting for transfers between devices  6.76 us (27%)
  Pallas kernels  6.17 us (24%)
  between operations  0.67 us (3%)
    ppermute x4, starting transfers between devices, exchange(): return lax.ppermute(value, 'dom', [(i, i ^ step) for i in range(n_dom)])  6.85 us
    pallas_call x9, Pallas kernels, call(): pl.pallas_call(kernel, out_shape=tuple(outs), in_specs=specs or [vmem] *...  6.17 us
    ppermute x4, waiting for transfers between devices, exchange(): return lax.ppermute(value, 'dom', [(i, i ^ step) for i in range(n_dom)])  5.68 us
    ppermute x3, starting transfers between devices, swap(): return lax.ppermute(value, ('dom', 'orient'), pairs)  4.64 us
    ppermute x3, waiting for transfers between devices, swap(): return lax.ppermute(value, ('dom', 'orient'), pairs)  1.09 us
  transfers between devices with their start and end apart: 7, of which 6 were waited for; matrix products, arithmetic and copies ran while one was open for 0% of the time, Pallas kernels for 21%

profile of v4, /device:TPU:0, one launch (start us, length us, event | category | flops | bytes accessed | tf_op | source)
XLA Modules:
  0.0 25.1 jit_solution(306914444271257175)
XLA Ops:
  0.6 2.4 %collective-permute-start = (bf16[8,64,128]{2,1,0:T(8,128)(2,1)}, bf16[8,64,128]{2,1,0:T(8,128)(2,1)S(1)}, u32[]{:S(2)}, u32[]{:S(2)}) collective-permute-start(bf16[8,64,128]{2,1,0:T(8,128)(2,1)} %refs_4_.1), channel_id=1, source_target_pairs={{0,3},{1,2},{2,1},{3,0},{4,7},{5,6},{6,5},{7,4},{8,11},{9,10},{10,... | collective-permute-start | bytes 393224 | tf_op jit(solution)/shard_map/ppermute | solution.py:404
  3.1 2.2 %first.1 = (f32[8,16,128]{2,1,0:T(8,128)S(1)}, f32[8,128]{1,0:T(8,128)S(1)}, f32[8,64,128]{2,1,0:T(8,128)S(1)}, f32[8,64,128]{2,1,0:T(8,128)S(1)}, f32[8,128]{1,...) custom-call(s32[16]{0:T(128)} %refs_0_.1, ...), custom_call_target="tpu_custom_call" | custom-call | flops 268435456 | bytes 1048576 | tf_op jit(solution)/shard_map/first/pallas_call | solution.py:390
  5.3 0.1 collective-permute-start.1
  5.4 1.3 %own.1.own_ref = f32[4096,128]{1,0:T(8,128)S(1)} custom-call(f32[8,16,128]{2,1,0:T(8,128)S(1)} %get-tuple-element.31.logits_ref, f32[8,128]{1,0:T(8,128)S(1)} %get-tuple-element.32.lse_ref.refs_0_, bf16[8,64,128]{2,1,0:T(8,128)(2,1)S(1)} %get-tuple-element.33.x_ref, s32[64,64]{1,0:T(8,128)S(1)} %get-tuple-element.34.mask_ref.refs_2_, ...), custom_call_target="tpu_custom_call" | custom-call | flops 268435456 | bytes 1048576 | tf_op jit(solution)/shard_map/own/pallas_call | solution.py:390
  6.7 0.6 %collective-permute-done.x_ref.refs_1_ = bf16[8,64,128]{2,1,0:T(8,128)(2,1)S(1)} collective-permute-done((bf16[8,64,128]{2,1,0:T(8,128)(2,1)}, bf16[8,64,128]{2,1,0:T(8,128)(2,1)S(1)}, u32[]{:S(2)}, u32[]{:S(2)}) %collective-permute-start) | collective-permute-done | bytes 131104 | tf_op jit(solution)/shard_map/ppermute | solution.py:404
  7.3 0.9 %score.1 = (f32[8,16,128]{2,1,0:T(8,128)S(1)}, f32[8,128]{1,0:T(8,128)S(1)}) custom-call(bf16[8,64,128]{2,1,0:T(8,128)(2,1)S(1)} %collective-permute-done.x_ref.refs_1_, f32[8,64,128]{2,1,0:T(8,128)S(1)} %get-tuple-element.37.first, f32[8,64,128]{2,1,0:T(8,128)S(1)} %get-tuple-element.38.second, f32[8,128]{1,0:T(8,128)S(1)} %get-tuple-element.39.bias_ref, ...), custom_call_target="tpu_custom_call" | custom-call | flops 268435456 | bytes 1048576 | tf_op jit(solution)/shard_map/score/pallas_call | solution.py:390
  8.2 2.1 %collective-permute-start.2 = (f32[8,128]{1,0:T(8,128)S(1)}, f32[8,128]{1,0:T(8,128)S(1)}, u32[]{:S(2)}, u32[]{:S(2)}) collective-permute-start(f32[8,128]{1,0:T(8,128)S(1)} %get-tuple-element.43.refs_5_), channel_id=1, source_target_pairs={{0,3},{1,2},{2,1},{3,0},{4,7},{5,6},{6,5},{7,4},{8,11},{9,10},{10,... | collective-permute-start | bytes 12296 | tf_op jit(solution)/shard_map/ppermute | solution.py:404
  10.3 0.0 collective-permute-done.1.refs_6_
  10.3 0.8 %back.1 = (f32[512,128]{1,0:T(8,128)S(1)}, f32[8,128]{1,0:T(8,128)S(1)}) custom-call(f32[8,16,128]{2,1,0:T(8,128)S(1)} %get-tuple-element.42.refs_0_, bf16[8,64,128]{2,1,0:T(8,128)(2,1)S(1)} %collective-permute-done.x_ref.refs_1_, s32[64,64]{1,0:T(8,128)S(1)} %get-tuple-element.34.mask_ref.refs_2_, bf16[128,2048]{1,0:T(8,128)(2,1)S(1)} %get-tuple-element.35.rows_ref.refs_3_, ...), custom_call_target="tpu_custom_call" | custom-call | flops 268435456 | bytes 1048576 | tf_op jit(solution)/shard_map/back/pallas_call | solution.py:390
  11.1 0.5 %collective-permute-done.2.refs_1_ = f32[8,128]{1,0:T(8,128)S(1)} collective-permute-done((f32[8,128]{1,0:T(8,128)S(1)}, f32[8,128]{1,0:T(8,128)S(1)}, u32[]{:S(2)}, u32[]{:S(2)}) %collective-permute-start.2) | collective-permute-done | bytes 4128 | tf_op jit(solution)/shard_map/ppermute | solution.py:404
  11.6 0.2 last_back.1
  11.8 0.4 %collective-permute-start.3 = (f32[264,128]{1,0:T(8,128)S(1)}, f32[264,128]{1,0:T(8,128)S(1)}, u32[]{:S(2)}, u32[]{:S(2)}) collective-permute-start(f32[264,128]{1,0:T(8,128)S(1)} %get-tuple-element.47), channel_id=1, source_target_pairs={{0,2},{2,0},{4,6},{6,4},{8,10},{10,8},{12,14},{14,12},{16,18},{18,... | collective-permute-start | bytes 405512 | tf_op jit(solution)/shard_map/ppermute | solution.py:475
  12.2 1.0 %collective-permute-done.3.got_ref = f32[264,128]{1,0:T(8,128)S(1)} collective-permute-done((f32[264,128]{1,0:T(8,128)S(1)}, f32[264,128]{1,0:T(8,128)S(1)}, u32[]{:S(2)}, u32[]{:S(2)}) %collective-permute-start.3) | collective-permute-done | bytes 135200 | tf_op jit(solution)/shard_map/ppermute | solution.py:475
  13.3 1.8 %collective-permute-start.4 = (bf16[144,128]{1,0:T(8,128)(2,1)S(1)}, bf16[144,128]{1,0:T(8,128)(2,1)S(1)}, u32[]{:S(2)}, u32[]{:S(2)}) collective-permute-start(bf16[144,128]{1,0:T(8,128)(2,1)S(1)} %get-tuple-element.50), channel_id=1, source_target_pairs={{0,6},{2,4},{4,2},{6,0},{8,14},{10,12},{12,10},{14,8},{16,22},{18,... | collective-permute-start | bytes 110600 | tf_op jit(solution)/shard_map/ppermute | solution.py:475
  15.1 1.7 %collective-permute-done.4.got_ref = bf16[144,128]{1,0:T(8,128)(2,1)S(1)} collective-permute-done((bf16[144,128]{1,0:T(8,128)(2,1)S(1)}, bf16[144,128]{1,0:T(8,128)(2,1)S(1)}, u32[]{:S(2)}, u32[]{:S(2)}) %collective-permute-start.4) | collective-permute-done | bytes 36896 | tf_op jit(solution)/shard_map/ppermute | solution.py:475
  16.8 1.9 %collective-permute-start.5 = (bf16[80,128]{1,0:T(8,128)(2,1)S(1)}, bf16[80,128]{1,0:T(8,128)(2,1)S(1)}, u32[]{:S(2)}, u32[]{:S(2)}) collective-permute-start(bf16[80,128]{1,0:T(8,128)(2,1)S(1)} %get-tuple-element.53), channel_id=1, source_target_pairs={{0,10},{2,8},{4,14},{6,12},{8,2},{10,0},{12,6},{14,4},{16,26},{18,... | collective-permute-start | bytes 61448 | tf_op jit(solution)/shard_map/ppermute | solution.py:475
  18.7 1.5 %collective-permute-done.5.got_ref = bf16[80,128]{1,0:T(8,128)(2,1)S(1)} collective-permute-done((bf16[80,128]{1,0:T(8,128)(2,1)S(1)}, bf16[80,128]{1,0:T(8,128)(2,1)S(1)}, u32[]{:S(2)}, u32[]{:S(2)}) %collective-permute-start.5) | collective-permute-done | bytes 20512 | tf_op jit(solution)/shard_map/ppermute | solution.py:475
  20.2 2.8 %collective-permute-start.6 = (f32[40,128]{1,0:T(8,128)S(1)}, f32[40,128]{1,0:T(8,128)S(1)}, u32[]{:S(2)}, u32[]{:S(2)}) collective-permute-start(f32[40,128]{1,0:T(8,128)S(1)} %get-tuple-element.56), channel_id=1, source_target_pairs={{0,18},{2,16},{4,22},{6,20},{8,26},{10,24},{12,30},{14,28},{16,2},... | collective-permute-start | bytes 61448 | tf_op jit(solution)/shard_map/ppermute | solution.py:475
  23.0 1.5 %collective-permute-done.6.got_ref = f32[40,128]{1,0:T(8,128)S(1)} collective-permute-done((f32[40,128]{1,0:T(8,128)S(1)}, f32[40,128]{1,0:T(8,128)S(1)}, u32[]{:S(2)}, u32[]{:S(2)}) %collective-permute-start.6) | collective-permute-done | bytes 20512 | tf_op jit(solution)/shard_map/ppermute | solution.py:475
  24.4 0.6 %last.1 = (f32[8,4,128]{2,1,0:T(4,128)}, f32[8]{0:T(128)}, f32[8]{0:T(128)}) custom-call(f32[32,128]{1,0:T(8,128)S(1)} %get-tuple-element.55.keep_ref, f32[40,128]{1,0:T(8,128)S(1)} %collective-permute-done.6.got_ref, f32[8,128]{1,0:T(8,128)S(1)} %get-tuple-element.57.mass_in, f32[8,128]{1,0:T(8,128)S(1)} %get-tuple-element.58.loglik_in), custom_call_target="tpu_custom_call" | custom-call | bytes 1048576 | tf_op jit(solution)/shard_map/last/pallas_call | solution.py:390
  (3 shorter events, 0.1 us)
Async XLA Ops:
  0.6 6.6 %collective-permute-start = (bf16[8,64,128]{2,1,0:T(8,128)(2,1)}, bf16[8,64,128]{2,1,0:T(8,128)(2,1)S(1)}, u32[]{:S(2)}, u32[]{:S(2)}) collective-permute-start(bf16[8,64,128]{2,1,0:T(8,128)(2,1)} %refs_4_.1), channel_id=1, source_target_pairs={{0,3},{1,2},{2,1},{3,0},{4,7},{5,6},{6,5},{7,4},{8,11},{9,10},{10,... | collective-permute-start | bytes 393224 | tf_op jit(solution)/shard_map/ppermute | solution.py:404
  5.3 5.0 %collective-permute-start.1 = (f32[8,128]{1,0:T(8,128)S(1)}, f32[8,128]{1,0:T(8,128)S(1)}, u32[]{:S(2)}, u32[]{:S(2)}) collective-permute-start(f32[8,128]{1,0:T(8,128)S(1)} %get-tuple-element.32.lse_ref.refs_0_), channel_id=1, source_target_pairs={{0,3},{1,2},{2,1},{3,0},{4,7},{5,6},{6,5},{7,4},{8,11},{9,10},{10,... | collective-permute-start | bytes 12296 | tf_op jit(solution)/shard_map/ppermute | solution.py:404
  8.2 3.4 %collective-permute-start.2 = (f32[8,128]{1,0:T(8,128)S(1)}, f32[8,128]{1,0:T(8,128)S(1)}, u32[]{:S(2)}, u32[]{:S(2)}) collective-permute-start(f32[8,128]{1,0:T(8,128)S(1)} %get-tuple-element.43.refs_5_), channel_id=1, source_target_pairs={{0,3},{1,2},{2,1},{3,0},{4,7},{5,6},{6,5},{7,4},{8,11},{9,10},{10,... | collective-permute-start | bytes 12296 | tf_op jit(solution)/shard_map/ppermute | solution.py:404
  11.8 1.4 %collective-permute-start.3 = (f32[264,128]{1,0:T(8,128)S(1)}, f32[264,128]{1,0:T(8,128)S(1)}, u32[]{:S(2)}, u32[]{:S(2)}) collective-permute-start(f32[264,128]{1,0:T(8,128)S(1)} %get-tuple-element.47), channel_id=1, source_target_pairs={{0,2},{2,0},{4,6},{6,4},{8,10},{10,8},{12,14},{14,12},{16,18},{18,... | collective-permute-start | bytes 405512 | tf_op jit(solution)/shard_map/ppermute | solution.py:475
  13.3 3.4 %collective-permute-start.4 = (bf16[144,128]{1,0:T(8,128)(2,1)S(1)}, bf16[144,128]{1,0:T(8,128)(2,1)S(1)}, u32[]{:S(2)}, u32[]{:S(2)}) collective-permute-start(bf16[144,128]{1,0:T(8,128)(2,1)S(1)} %get-tuple-element.50), channel_id=1, source_target_pairs={{0,6},{2,4},{4,2},{6,0},{8,14},{10,12},{12,10},{14,8},{16,22},{18,... | collective-permute-start | bytes 110600 | tf_op jit(solution)/shard_map/ppermute | solution.py:475
  16.8 3.4 %collective-permute-start.5 = (bf16[80,128]{1,0:T(8,128)(2,1)S(1)}, bf16[80,128]{1,0:T(8,128)(2,1)S(1)}, u32[]{:S(2)}, u32[]{:S(2)}) collective-permute-start(bf16[80,128]{1,0:T(8,128)(2,1)S(1)} %get-tuple-element.53), channel_id=1, source_target_pairs={{0,10},{2,8},{4,14},{6,12},{8,2},{10,0},{12,6},{14,4},{16,26},{18,... | collective-permute-start | bytes 61448 | tf_op jit(solution)/shard_map/ppermute | solution.py:475
  20.2 4.3 %collective-permute-start.6 = (f32[40,128]{1,0:T(8,128)S(1)}, f32[40,128]{1,0:T(8,128)S(1)}, u32[]{:S(2)}, u32[]{:S(2)}) collective-permute-start(f32[40,128]{1,0:T(8,128)S(1)} %get-tuple-element.56), channel_id=1, source_target_pairs={{0,18},{2,16},{4,22},{6,20},{8,26},{10,24},{12,30},{14,28},{16,2},... | collective-permute-start | bytes 61448 | tf_op jit(solution)/shard_map/ppermute | solution.py:475

commit v5 on v4

--- a/solution.py
+++ b/solution.py
@@ -330,17 +330,36 @@
     mass_ref[...] = jnp.broadcast_to(mass, mass_ref.shape)
 
 
-def halve_kernel(groups, bit, keep_ref, got_ref, mass_in, left_ref, send_ref, mass_ref):
+def quarter_kernel(unit, keep_ref, got_ref, mass_in, left_ref, *refs):
+    sends, mass_ref = refs[:-1], refs[-1]
     rows = keep_ref.shape[0]
-    unit = groups * 8
+    own = (lax.axis_index("dom") >> 1) & 3
+    mass = mass_in[:1] + get_mass(got_ref, rows)
+    for turn, out_ref in enumerate((left_ref, *sends)):
+        for rest in range(rows // unit // 4):
+            at = rest * unit
+            here = pl.ds(pl.multiple_of((4 * rest + (own ^ turn)) * unit, unit), unit)
+            out_ref[at : at + unit] = (keep_ref[here] + got_ref[here].astype(F32)).astype(out_ref.dtype)
+        if turn:
+            put_mass(out_ref, rows // 4, mass)
+    mass_ref[...] = jnp.broadcast_to(mass, mass_ref.shape)
+
+
+def halve_kernel(unit, bit, keep_ref, mass_in, *refs):
+    gots, (left_ref, send_ref, mass_ref) = refs[:-3], refs[-3:]
+    rows = keep_ref.shape[0]
     side = (lax.axis_index("dom") >> bit) & 1
+    mass = mass_in[:1]
+    for got_ref in gots:
+        mass = mass + get_mass(got_ref, rows)
     for pair in range(rows // unit // 2):
         at = pair * unit
-        mine = pl.ds(pl.multiple_of((2 * pair + side) * unit, unit), unit)
-        theirs = pl.ds(pl.multiple_of((2 * pair + 1 - side) * unit, unit), unit)
-        left_ref[at : at + unit] = keep_ref[mine] + got_ref[mine].astype(F32)
-        send_ref[at : at + unit] = (keep_ref[theirs] + got_ref[theirs].astype(F32)).astype(send_ref.dtype)
-    mass = mass_in[:1] + get_mass(got_ref, rows)
+        for half, out_ref in ((side, left_ref), (1 - side, send_ref)):
+            here = pl.ds(pl.multiple_of((2 * pair + half) * unit, unit), unit)
+            total = keep_ref[here]
+            for got_ref in gots:
+                total = total + got_ref[here].astype(F32)
+            out_ref[at : at + unit] = total.astype(out_ref.dtype)
     put_mass(send_ref, rows // 2, mass)
     mass_ref[...] = jnp.broadcast_to(mass, mass_ref.shape)
 
@@ -470,19 +489,27 @@
         (*scored[0], owns, *partial, *terms[0]), [], flops=flops, name="last_back",
     )
 
-    def exchange(value, b):
-        step = 1 << b | 1
+    def exchange(value, turned):
+        step = turned | parity(turned >> 1, n_dom)
         return lax.ppermute(value, "dom", [(i, i ^ step) for i in range(n_dom)])
 
-    for b in range(steps - 1):
-        got = exchange(send, b)
+    got = exchange(send, 1)
+    height = keep.shape[0] // 4
+    keep, *sends, mass = call(
+        functools.partial(quarter_kernel, groups * 8),
+        [shape((height, width), F32)] + [sent(1, height)] * 3 + [shape((8, 128), F32)],
+        (keep, got, mass), [], name="quarter",
+    )
+    gots = [exchange(sends[turn - 1], turn << 1) for turn in (1, 3, 2)]
+    for b in range(3, steps):
         height = keep.shape[0] // 2
         keep, send, mass = call(
-            functools.partial(halve_kernel, groups, b + 1),
-            [shape((height, width), F32), sent(b + 1, height), shape((8, 128), F32)],
-            (keep, got, mass), [], name="halve",
+            functools.partial(halve_kernel, groups * 8, b),
+            [shape((height, width), F32), sent(b, height), shape((8, 128), F32)],
+            (keep, mass, *gots), [], name="halve",
         )
-    got = exchange(send, steps - 1)
+        gots = [exchange(send, 1 << b)]
+    got, = gots
     image, occupancy, loglik = call(
         functools.partial(last_kernel, groups, pack),
         [shape((share, block, width), F32), shape((share,), F32), shape((count,), F32)],

time: 25.3 us -> 24.8 us (0.980)
  starting transfers between devices: 11.5 us -> 10.7 us
  waiting for transfers between devices: 6.76 us -> 7.11 us
    ppermute x4 -> x5, starting transfers between devices: 6.85 us -> 6.08 us  [exchange(): return lax.ppermute(value, 'dom', [(i, i ^ step) for i in range(n_dom)])]
    ppermute x4 -> x5, waiting for transfers between devices: 5.68 us -> 6.02 us  [exchange(): return lax.ppermute(value, 'dom', [(i, i ^ step) for i in range(n_dom)])]
    pallas_call x9 -> x8, Pallas kernels: 6.17 us -> 6.14 us  [call(): pl.pallas_call(kernel, out_shape=tuple(outs), in_specs=specs or [vmem] *...]
  transfers between devices with their start and end apart: 7 -> 8, of which waited for: 6 -> 6; matrix products, arithmetic and copies ran while one was open for 0% -> 0% of each run, Pallas kernels for 21% -> 21%
where the time goes in v5:
time: 24.8 us; the launch traced here: 24.6 us
  starting transfers between devices  10.7 us (43%)
  waiting for transfers between devices  7.11 us (29%)
  Pallas kernels  6.14 us (25%)
  between operations  0.68 us (3%)
    pallas_call x8, Pallas kernels, call(): pl.pallas_call(kernel, out_shape=tuple(outs), in_specs=specs or [vmem] *...  6.14 us
    ppermute x5, starting transfers between devices, exchange(): return lax.ppermute(value, 'dom', [(i, i ^ step) for i in range(n_dom)])  6.08 us
    ppermute x5, waiting for transfers between devices, exchange(): return lax.ppermute(value, 'dom', [(i, i ^ step) for i in range(n_dom)])  6.02 us
    ppermute x3, starting transfers between devices, swap(): return lax.ppermute(value, ('dom', 'orient'), pairs)  4.64 us
    ppermute x3, waiting for transfers between devices, swap(): return lax.ppermute(value, ('dom', 'orient'), pairs)  1.09 us
  transfers between devices with their start and end apart: 8, of which 6 were waited for; matrix products, arithmetic and copies ran while one was open for 0% of the time, Pallas kernels for 21%

profile of v5, /device:TPU:0, one launch (start us, length us, event | category | flops | bytes accessed | tf_op | source)
XLA Modules:
  0.0 24.6 jit_solution(4133709754404645062)
XLA Ops:
  0.6 2.4 %collective-permute-start = (bf16[8,64,128]{2,1,0:T(8,128)(2,1)}, bf16[8,64,128]{2,1,0:T(8,128)(2,1)S(1)}, u32[]{:S(2)}, u32[]{:S(2)}) collective-permute-start(bf16[8,64,128]{2,1,0:T(8,128)(2,1)} %refs_4_.1), channel_id=1, source_target_pairs={{0,3},{1,2},{2,1},{3,0},{4,7},{5,6},{6,5},{7,4},{8,11},{9,10},{10,... | collective-permute-start | bytes 393224 | tf_op jit(solution)/shard_map/ppermute | solution.py:423
  3.1 2.2 %first.1 = (f32[8,16,128]{2,1,0:T(8,128)S(1)}, f32[8,128]{1,0:T(8,128)S(1)}, f32[8,64,128]{2,1,0:T(8,128)S(1)}, f32[8,64,128]{2,1,0:T(8,128)S(1)}, f32[8,128]{1,...) custom-call(s32[16]{0:T(128)} %refs_0_.1, ...), custom_call_target="tpu_custom_call" | custom-call | flops 268435456 | bytes 1048576 | tf_op jit(solution)/shard_map/first/pallas_call | solution.py:409
  5.3 0.1 collective-permute-start.1
  5.4 1.3 %own.1.own_ref = f32[4096,128]{1,0:T(8,128)S(1)} custom-call(f32[8,16,128]{2,1,0:T(8,128)S(1)} %get-tuple-element.30.logits_ref, f32[8,128]{1,0:T(8,128)S(1)} %get-tuple-element.31.lse_ref.refs_0_, bf16[8,64,128]{2,1,0:T(8,128)(2,1)S(1)} %get-tuple-element.32.x_ref, s32[64,64]{1,0:T(8,128)S(1)} %get-tuple-element.33.mask_ref.refs_2_, ...), custom_call_target="tpu_custom_call" | custom-call | flops 268435456 | bytes 1048576 | tf_op jit(solution)/shard_map/own/pallas_call | solution.py:409
  6.7 0.6 %collective-permute-done.x_ref.refs_1_ = bf16[8,64,128]{2,1,0:T(8,128)(2,1)S(1)} collective-permute-done((bf16[8,64,128]{2,1,0:T(8,128)(2,1)}, bf16[8,64,128]{2,1,0:T(8,128)(2,1)S(1)}, u32[]{:S(2)}, u32[]{:S(2)}) %collective-permute-start) | collective-permute-done | bytes 131104 | tf_op jit(solution)/shard_map/ppermute | solution.py:423
  7.3 0.9 %score.1 = (f32[8,16,128]{2,1,0:T(8,128)S(1)}, f32[8,128]{1,0:T(8,128)S(1)}) custom-call(bf16[8,64,128]{2,1,0:T(8,128)(2,1)S(1)} %collective-permute-done.x_ref.refs_1_, f32[8,64,128]{2,1,0:T(8,128)S(1)} %get-tuple-element.36.first, f32[8,64,128]{2,1,0:T(8,128)S(1)} %get-tuple-element.37.second, f32[8,128]{1,0:T(8,128)S(1)} %get-tuple-element.38.bias_ref, ...), custom_call_target="tpu_custom_call" | custom-call | flops 268435456 | bytes 1048576 | tf_op jit(solution)/shard_map/score/pallas_call | solution.py:409
  8.2 2.1 %collective-permute-start.2 = (f32[8,128]{1,0:T(8,128)S(1)}, f32[8,128]{1,0:T(8,128)S(1)}, u32[]{:S(2)}, u32[]{:S(2)}) collective-permute-start(f32[8,128]{1,0:T(8,128)S(1)} %get-tuple-element.42.refs_5_), channel_id=1, source_target_pairs={{0,3},{1,2},{2,1},{3,0},{4,7},{5,6},{6,5},{7,4},{8,11},{9,10},{10,... | collective-permute-start | bytes 12296 | tf_op jit(solution)/shard_map/ppermute | solution.py:423
  10.3 0.0 collective-permute-done.1.refs_6_
  10.3 0.8 %back.1 = (f32[512,128]{1,0:T(8,128)S(1)}, f32[8,128]{1,0:T(8,128)S(1)}) custom-call(f32[8,16,128]{2,1,0:T(8,128)S(1)} %get-tuple-element.41.refs_0_, bf16[8,64,128]{2,1,0:T(8,128)(2,1)S(1)} %collective-permute-done.x_ref.refs_1_, s32[64,64]{1,0:T(8,128)S(1)} %get-tuple-element.33.mask_ref.refs_2_, bf16[128,2048]{1,0:T(8,128)(2,1)S(1)} %get-tuple-element.34.rows_ref.refs_3_, ...), custom_call_target="tpu_custom_call" | custom-call | flops 268435456 | bytes 1048576 | tf_op jit(solution)/shard_map/back/pallas_call | solution.py:409
  11.1 0.5 %collective-permute-done.2.refs_1_ = f32[8,128]{1,0:T(8,128)S(1)} collective-permute-done((f32[8,128]{1,0:T(8,128)S(1)}, f32[8,128]{1,0:T(8,128)S(1)}, u32[]{:S(2)}, u32[]{:S(2)}) %collective-permute-start.2) | collective-permute-done | bytes 4128 | tf_op jit(solution)/shard_map/ppermute | solution.py:423
  11.6 0.2 last_back.1
  11.8 0.4 %collective-permute-start.3 = (f32[264,128]{1,0:T(8,128)S(1)}, f32[264,128]{1,0:T(8,128)S(1)}, u32[]{:S(2)}, u32[]{:S(2)}) collective-permute-start(f32[264,128]{1,0:T(8,128)S(1)} %get-tuple-element.46), channel_id=1, source_target_pairs={{0,2},{2,0},{4,6},{6,4},{8,10},{10,8},{12,14},{14,12},{16,18},{18,... | collective-permute-start | bytes 405512 | tf_op jit(solution)/shard_map/ppermute | solution.py:494
  12.2 1.0 %collective-permute-done.3.got_ref = f32[264,128]{1,0:T(8,128)S(1)} collective-permute-done((f32[264,128]{1,0:T(8,128)S(1)}, f32[264,128]{1,0:T(8,128)S(1)}, u32[]{:S(2)}, u32[]{:S(2)}) %collective-permute-start.3) | collective-permute-done | bytes 135200 | tf_op jit(solution)/shard_map/ppermute | solution.py:494
  13.3 1.8 %collective-permute-start.4 = (bf16[80,128]{1,0:T(8,128)(2,1)S(1)}, bf16[80,128]{1,0:T(8,128)(2,1)S(1)}, u32[]{:S(2)}, u32[]{:S(2)}) collective-permute-start(bf16[80,128]{1,0:T(8,128)(2,1)S(1)} %get-tuple-element.50), channel_id=1, source_target_pairs={{0,6},{2,4},{4,2},{6,0},{8,14},{10,12},{12,10},{14,8},{16,22},{18,... | collective-permute-start | bytes 61448 | tf_op jit(solution)/shard_map/ppermute | solution.py:494
  15.1 1.5 %collective-permute-start.5 = (bf16[80,128]{1,0:T(8,128)(2,1)S(1)}, bf16[80,128]{1,0:T(8,128)(2,1)S(1)}, u32[]{:S(2)}, u32[]{:S(2)}) collective-permute-start(bf16[80,128]{1,0:T(8,128)(2,1)S(1)} %get-tuple-element.51), channel_id=1, source_target_pairs={{0,12},{2,14},{4,8},{6,10},{8,4},{10,6},{12,0},{14,2},{16,28},{18,... | collective-permute-start | bytes 61448 | tf_op jit(solution)/shard_map/ppermute | solution.py:494
  16.6 0.0 collective-permute-start.6
  16.6 0.0 collective-permute-done.4.refs_0_
  16.6 3.1 %collective-permute-done.5.refs_1_ = bf16[80,128]{1,0:T(8,128)(2,1)S(1)} collective-permute-done((bf16[80,128]{1,0:T(8,128)(2,1)S(1)}, bf16[80,128]{1,0:T(8,128)(2,1)S(1)}, u32[]{:S(2)}, u32[]{:S(2)}) %collective-permute-start.5) | collective-permute-done | bytes 20512 | tf_op jit(solution)/shard_map/ppermute | solution.py:494
  19.8 0.1 collective-permute-done.6.refs_2_
  19.8 2.4 %collective-permute-start.7 = (f32[40,128]{1,0:T(8,128)S(1)}, f32[40,128]{1,0:T(8,128)S(1)}, u32[]{:S(2)}, u32[]{:S(2)}) collective-permute-start(f32[40,128]{1,0:T(8,128)S(1)} %get-tuple-element.54), channel_id=1, source_target_pairs={{0,18},{2,16},{4,22},{6,20},{8,26},{10,24},{12,30},{14,28},{16,2},... | collective-permute-start | bytes 61448 | tf_op jit(solution)/shard_map/ppermute | solution.py:494
  22.2 1.8 %collective-permute-done.7.got_ref = f32[40,128]{1,0:T(8,128)S(1)} collective-permute-done((f32[40,128]{1,0:T(8,128)S(1)}, f32[40,128]{1,0:T(8,128)S(1)}, u32[]{:S(2)}, u32[]{:S(2)}) %collective-permute-start.7) | collective-permute-done | bytes 20512 | tf_op jit(solution)/shard_map/ppermute | solution.py:494
  24.0 0.6 %last.1 = (f32[8,4,128]{2,1,0:T(4,128)}, f32[8]{0:T(128)}, f32[8]{0:T(128)}) custom-call(f32[32,128]{1,0:T(8,128)S(1)} %get-tuple-element.53.keep_ref, f32[40,128]{1,0:T(8,128)S(1)} %collective-permute-done.7.got_ref, f32[8,128]{1,0:T(8,128)S(1)} %get-tuple-element.55.mass_in, f32[8,128]{1,0:T(8,128)S(1)} %get-tuple-element.56.loglik_in), custom_call_target="tpu_custom_call" | custom-call | bytes 1048576 | tf_op jit(solution)/shard_map/last/pallas_call | solution.py:409
  (2 shorter events, 0.0 us)
Async XLA Ops:
  0.6 6.6 %collective-permute-start = (bf16[8,64,128]{2,1,0:T(8,128)(2,1)}, bf16[8,64,128]{2,1,0:T(8,128)(2,1)S(1)}, u32[]{:S(2)}, u32[]{:S(2)}) collective-permute-start(bf16[8,64,128]{2,1,0:T(8,128)(2,1)} %refs_4_.1), channel_id=1, source_target_pairs={{0,3},{1,2},{2,1},{3,0},{4,7},{5,6},{6,5},{7,4},{8,11},{9,10},{10,... | collective-permute-start | bytes 393224 | tf_op jit(solution)/shard_map/ppermute | solution.py:423
  5.3 5.0 %collective-permute-start.1 = (f32[8,128]{1,0:T(8,128)S(1)}, f32[8,128]{1,0:T(8,128)S(1)}, u32[]{:S(2)}, u32[]{:S(2)}) collective-permute-start(f32[8,128]{1,0:T(8,128)S(1)} %get-tuple-element.31.lse_ref.refs_0_), channel_id=1, source_target_pairs={{0,3},{1,2},{2,1},{3,0},{4,7},{5,6},{6,5},{7,4},{8,11},{9,10},{10,... | collective-permute-start | bytes 12296 | tf_op jit(solution)/shard_map/ppermute | solution.py:423
  8.2 3.4 %collective-permute-start.2 = (f32[8,128]{1,0:T(8,128)S(1)}, f32[8,128]{1,0:T(8,128)S(1)}, u32[]{:S(2)}, u32[]{:S(2)}) collective-permute-start(f32[8,128]{1,0:T(8,128)S(1)} %get-tuple-element.42.refs_5_), channel_id=1, source_target_pairs={{0,3},{1,2},{2,1},{3,0},{4,7},{5,6},{6,5},{7,4},{8,11},{9,10},{10,... | collective-permute-start | bytes 12296 | tf_op jit(solution)/shard_map/ppermute | solution.py:423
  11.8 1.4 %collective-permute-start.3 = (f32[264,128]{1,0:T(8,128)S(1)}, f32[264,128]{1,0:T(8,128)S(1)}, u32[]{:S(2)}, u32[]{:S(2)}) collective-permute-start(f32[264,128]{1,0:T(8,128)S(1)} %get-tuple-element.46), channel_id=1, source_target_pairs={{0,2},{2,0},{4,6},{6,4},{8,10},{10,8},{12,14},{14,12},{16,18},{18,... | collective-permute-start | bytes 405512 | tf_op jit(solution)/shard_map/ppermute | solution.py:494
  13.3 3.3 %collective-permute-start.4 = (bf16[80,128]{1,0:T(8,128)(2,1)S(1)}, bf16[80,128]{1,0:T(8,128)(2,1)S(1)}, u32[]{:S(2)}, u32[]{:S(2)}) collective-permute-start(bf16[80,128]{1,0:T(8,128)(2,1)S(1)} %get-tuple-element.50), channel_id=1, source_target_pairs={{0,6},{2,4},{4,2},{6,0},{8,14},{10,12},{12,10},{14,8},{16,22},{18,... | collective-permute-start | bytes 61448 | tf_op jit(solution)/shard_map/ppermute | solution.py:494
  15.1 4.7 %collective-permute-start.5 = (bf16[80,128]{1,0:T(8,128)(2,1)S(1)}, bf16[80,128]{1,0:T(8,128)(2,1)S(1)}, u32[]{:S(2)}, u32[]{:S(2)}) collective-permute-start(bf16[80,128]{1,0:T(8,128)(2,1)S(1)} %get-tuple-element.51), channel_id=1, source_target_pairs={{0,12},{2,14},{4,8},{6,10},{8,4},{10,6},{12,0},{14,2},{16,28},{18,... | collective-permute-start | bytes 61448 | tf_op jit(solution)/shard_map/ppermute | solution.py:494
  16.6 3.2 %collective-permute-start.6 = (bf16[80,128]{1,0:T(8,128)(2,1)S(1)}, bf16[80,128]{1,0:T(8,128)(2,1)S(1)}, u32[]{:S(2)}, u32[]{:S(2)}) collective-permute-start(bf16[80,128]{1,0:T(8,128)(2,1)S(1)} %get-tuple-element.52), channel_id=1, source_target_pairs={{0,10},{2,8},{4,14},{6,12},{8,2},{10,0},{12,6},{14,4},{16,26},{18,... | collective-permute-start | bytes 61448 | tf_op jit(solution)/shard_map/ppermute | solution.py:494
  19.8 4.2 %collective-permute-start.7 = (f32[40,128]{1,0:T(8,128)S(1)}, f32[40,128]{1,0:T(8,128)S(1)}, u32[]{:S(2)}, u32[]{:S(2)}) collective-permute-start(f32[40,128]{1,0:T(8,128)S(1)} %get-tuple-element.54), channel_id=1, source_target_pairs={{0,18},{2,16},{4,22},{6,20},{8,26},{10,24},{12,30},{14,28},{16,2},... | collective-permute-start | bytes 61448 | tf_op jit(solution)/shard_map/ppermute | solution.py:494

commit v6 on v5

--- a/solution.py
+++ b/solution.py
@@ -316,15 +316,15 @@
     mass = to_lanes(jnp.sum(jnp.where(row == lane // TS, mass, 0.0), axis=1, keepdims=True))
     height = sum_ref.shape[0]
     half = height // 2
-    factors = [jnp.broadcast_to(factor[i : i + 1, :], (8, factor.shape[1])) for i in range(count)]
-    for at in range(0, height, 8):
-        total = sum_ref[at : at + 8]
+    factors = [jnp.broadcast_to(factor[i : i + 1, :], (16, factor.shape[1])) for i in range(count)]
+    for at in range(0, height, 16):
+        total = sum_ref[at : at + 16]
         for i in range(count):
-            total = total + own_ref[i * height + at : i * height + at + 8] * factors[i]
+            total = total + own_ref[i * height + at : i * height + at + 16] * factors[i]
         if at < half:
-            keep_ref[at : at + 8] = total
+            keep_ref[at : at + 16] = total
         else:
-            send_ref[at - half : at - half + 8] = total
+            send_ref[at - half : at - half + 16] = total.astype(send_ref.dtype)
     put_mass(send_ref, half, mass)
     loglik_ref[...] = jnp.broadcast_to(to_lanes(loglik[:, :1]), loglik_ref.shape)
     mass_ref[...] = jnp.broadcast_to(mass, mass_ref.shape)
@@ -465,7 +465,7 @@
     steps = bits(n_dom)
 
     def sent(step, height):
-        dtype = F32 if step in (0, steps - 1) else BF16
+        dtype = BF16
         return shape((height + (8 if dtype == F32 else 16), width), dtype)
 
     mass_shape = shape((8, lanes), F32)

time: 24.8 us -> 24.6 us (level)
  transfers between devices with their start and end apart: 8 -> 8, of which waited for: 6 -> 5; matrix products, arithmetic and copies ran while one was open for 0% -> 0% of each run, Pallas kernels for 21% -> 22%
where the time goes in v6:
time: 24.6 us; the launch traced here: 24.5 us
  starting transfers between devices  10.7 us (43%)
  waiting for transfers between devices  6.91 us (28%)
  Pallas kernels  6.17 us (25%)
  between operations  0.68 us (3%)
    pallas_call x8, Pallas kernels, call(): pl.pallas_call(kernel, out_shape=tuple(outs), in_specs=specs or [vmem] *...  6.17 us
    ppermute x5, starting transfers between devices, exchange(): return lax.ppermute(value, 'dom', [(i, i ^ step) for i in range(n_dom)])  6.08 us
    ppermute x5, waiting for transfers between devices, exchange(): return lax.ppermute(value, 'dom', [(i, i ^ step) for i in range(n_dom)])  5.83 us
    ppermute x3, starting transfers between devices, swap(): return lax.ppermute(value, ('dom', 'orient'), pairs)  4.63 us
    ppermute x3, waiting for transfers between devices, swap(): return lax.ppermute(value, ('dom', 'orient'), pairs)  1.08 us
  transfers between devices with their start and end apart: 8, of which 5 were waited for; matrix products, arithmetic and copies ran while one was open for 0% of the time, Pallas kernels for 22%

profile of v6, /device:TPU:0, one launch (start us, length us, event | category | flops | bytes accessed | tf_op | source)
XLA Modules:
  0.0 24.5 jit_solution(12336537099356566306)
XLA Ops:
  0.6 2.4 %collective-permute-start = (bf16[8,64,128]{2,1,0:T(8,128)(2,1)}, bf16[8,64,128]{2,1,0:T(8,128)(2,1)S(1)}, u32[]{:S(2)}, u32[]{:S(2)}) collective-permute-start(bf16[8,64,128]{2,1,0:T(8,128)(2,1)} %refs_4_.1), channel_id=1, source_target_pairs={{0,3},{1,2},{2,1},{3,0},{4,7},{5,6},{6,5},{7,4},{8,11},{9,10},{10,... | collective-permute-start | bytes 393224 | tf_op jit(solution)/shard_map/ppermute | solution.py:423
  3.1 2.3 %first.1 = (f32[8,16,128]{2,1,0:T(8,128)S(1)}, f32[8,128]{1,0:T(8,128)S(1)}, f32[8,64,128]{2,1,0:T(8,128)S(1)}, f32[8,64,128]{2,1,0:T(8,128)S(1)}, f32[8,128]{1,...) custom-call(s32[16]{0:T(128)} %refs_0_.1, ...), custom_call_target="tpu_custom_call" | custom-call | flops 268435456 | bytes 1048576 | tf_op jit(solution)/shard_map/first/pallas_call | solution.py:409
  5.3 0.1 collective-permute-start.1
  5.4 1.3 %own.1.own_ref = f32[4096,128]{1,0:T(8,128)S(1)} custom-call(f32[8,16,128]{2,1,0:T(8,128)S(1)} %get-tuple-element.30.logits_ref, f32[8,128]{1,0:T(8,128)S(1)} %get-tuple-element.31.lse_ref.refs_0_, bf16[8,64,128]{2,1,0:T(8,128)(2,1)S(1)} %get-tuple-element.32.x_ref, s32[64,64]{1,0:T(8,128)S(1)} %get-tuple-element.33.mask_ref.refs_2_, ...), custom_call_target="tpu_custom_call" | custom-call | flops 268435456 | bytes 1048576 | tf_op jit(solution)/shard_map/own/pallas_call | solution.py:409
  6.7 0.6 %collective-permute-done.x_ref.refs_1_ = bf16[8,64,128]{2,1,0:T(8,128)(2,1)S(1)} collective-permute-done((bf16[8,64,128]{2,1,0:T(8,128)(2,1)}, bf16[8,64,128]{2,1,0:T(8,128)(2,1)S(1)}, u32[]{:S(2)}, u32[]{:S(2)}) %collective-permute-start) | collective-permute-done | bytes 131104 | tf_op jit(solution)/shard_map/ppermute | solution.py:423
  7.3 0.9 %score.1 = (f32[8,16,128]{2,1,0:T(8,128)S(1)}, f32[8,128]{1,0:T(8,128)S(1)}) custom-call(bf16[8,64,128]{2,1,0:T(8,128)(2,1)S(1)} %collective-permute-done.x_ref.refs_1_, f32[8,64,128]{2,1,0:T(8,128)S(1)} %get-tuple-element.36.first, f32[8,64,128]{2,1,0:T(8,128)S(1)} %get-tuple-element.37.second, f32[8,128]{1,0:T(8,128)S(1)} %get-tuple-element.38.bias_ref, ...), custom_call_target="tpu_custom_call" | custom-call | flops 268435456 | bytes 1048576 | tf_op jit(solution)/shard_map/score/pallas_call | solution.py:409
  8.2 2.1 %collective-permute-start.2 = (f32[8,128]{1,0:T(8,128)S(1)}, f32[8,128]{1,0:T(8,128)S(1)}, u32[]{:S(2)}, u32[]{:S(2)}) collective-permute-start(f32[8,128]{1,0:T(8,128)S(1)} %get-tuple-element.42.refs_5_), channel_id=1, source_target_pairs={{0,3},{1,2},{2,1},{3,0},{4,7},{5,6},{6,5},{7,4},{8,11},{9,10},{10,... | collective-permute-start | bytes 12296 | tf_op jit(solution)/shard_map/ppermute | solution.py:423
  10.3 0.0 collective-permute-done.1.refs_6_
  10.3 0.8 %back.1 = (f32[512,128]{1,0:T(8,128)S(1)}, f32[8,128]{1,0:T(8,128)S(1)}) custom-call(f32[8,16,128]{2,1,0:T(8,128)S(1)} %get-tuple-element.41.refs_0_, bf16[8,64,128]{2,1,0:T(8,128)(2,1)S(1)} %collective-permute-done.x_ref.refs_1_, s32[64,64]{1,0:T(8,128)S(1)} %get-tuple-element.33.mask_ref.refs_2_, bf16[128,2048]{1,0:T(8,128)(2,1)S(1)} %get-tuple-element.34.rows_ref.refs_3_, ...), custom_call_target="tpu_custom_call" | custom-call | flops 268435456 | bytes 1048576 | tf_op jit(solution)/shard_map/back/pallas_call | solution.py:409
  11.1 0.5 %collective-permute-done.2.refs_1_ = f32[8,128]{1,0:T(8,128)S(1)} collective-permute-done((f32[8,128]{1,0:T(8,128)S(1)}, f32[8,128]{1,0:T(8,128)S(1)}, u32[]{:S(2)}, u32[]{:S(2)}) %collective-permute-start.2) | collective-permute-done | bytes 4128 | tf_op jit(solution)/shard_map/ppermute | solution.py:423
  11.7 0.2 last_back.1
  11.9 0.4 %collective-permute-start.3 = (bf16[272,128]{1,0:T(8,128)(2,1)S(1)}, bf16[272,128]{1,0:T(8,128)(2,1)S(1)}, u32[]{:S(2)}, u32[]{:S(2)}) collective-permute-start(bf16[272,128]{1,0:T(8,128)(2,1)S(1)} %get-tuple-element.46), channel_id=1, source_target_pairs={{0,2},{2,0},{4,6},{6,4},{8,10},{10,8},{12,14},{14,12},{16,18},{18,... | collective-permute-start | bytes 208904 | tf_op jit(solution)/shard_map/ppermute | solution.py:494
  12.3 0.9 %collective-permute-done.3.got_ref = bf16[272,128]{1,0:T(8,128)(2,1)S(1)} collective-permute-done((bf16[272,128]{1,0:T(8,128)(2,1)S(1)}, bf16[272,128]{1,0:T(8,128)(2,1)S(1)}, u32[]{:S(2)}, u32[]{:S(2)}) %collective-permute-start.3) | collective-permute-done | bytes 69664 | tf_op jit(solution)/shard_map/ppermute | solution.py:494
  13.2 1.8 %collective-permute-start.4 = (bf16[80,128]{1,0:T(8,128)(2,1)S(1)}, bf16[80,128]{1,0:T(8,128)(2,1)S(1)}, u32[]{:S(2)}, u32[]{:S(2)}) collective-permute-start(bf16[80,128]{1,0:T(8,128)(2,1)S(1)} %get-tuple-element.50), channel_id=1, source_target_pairs={{0,6},{2,4},{4,2},{6,0},{8,14},{10,12},{12,10},{14,8},{16,22},{18,... | collective-permute-start | bytes 61448 | tf_op jit(solution)/shard_map/ppermute | solution.py:494
  15.0 1.5 %collective-permute-start.5 = (bf16[80,128]{1,0:T(8,128)(2,1)S(1)}, bf16[80,128]{1,0:T(8,128)(2,1)S(1)}, u32[]{:S(2)}, u32[]{:S(2)}) collective-permute-start(bf16[80,128]{1,0:T(8,128)(2,1)S(1)} %get-tuple-element.51), channel_id=1, source_target_pairs={{0,12},{2,14},{4,8},{6,10},{8,4},{10,6},{12,0},{14,2},{16,28},{18,... | collective-permute-start | bytes 61448 | tf_op jit(solution)/shard_map/ppermute | solution.py:494
  16.5 0.0 collective-permute-start.6
  16.5 0.0 collective-permute-done.4.refs_0_
  16.5 3.1 %collective-permute-done.5.refs_1_ = bf16[80,128]{1,0:T(8,128)(2,1)S(1)} collective-permute-done((bf16[80,128]{1,0:T(8,128)(2,1)S(1)}, bf16[80,128]{1,0:T(8,128)(2,1)S(1)}, u32[]{:S(2)}, u32[]{:S(2)}) %collective-permute-start.5) | collective-permute-done | bytes 20512 | tf_op jit(solution)/shard_map/ppermute | solution.py:494
  19.7 0.0 collective-permute-done.6.refs_2_
  19.7 2.4 %collective-permute-start.7 = (bf16[48,128]{1,0:T(8,128)(2,1)S(1)}, bf16[48,128]{1,0:T(8,128)(2,1)S(1)}, u32[]{:S(2)}, u32[]{:S(2)}) collective-permute-start(bf16[48,128]{1,0:T(8,128)(2,1)S(1)} %get-tuple-element.54), channel_id=1, source_target_pairs={{0,18},{2,16},{4,22},{6,20},{8,26},{10,24},{12,30},{14,28},{16,2},... | collective-permute-start | bytes 36872 | tf_op jit(solution)/shard_map/ppermute | solution.py:494
  22.1 1.7 %collective-permute-done.7.got_ref = bf16[48,128]{1,0:T(8,128)(2,1)S(1)} collective-permute-done((bf16[48,128]{1,0:T(8,128)(2,1)S(1)}, bf16[48,128]{1,0:T(8,128)(2,1)S(1)}, u32[]{:S(2)}, u32[]{:S(2)}) %collective-permute-start.7) | collective-permute-done | bytes 12320 | tf_op jit(solution)/shard_map/ppermute | solution.py:494
  23.8 0.6 %last.1 = (f32[8,4,128]{2,1,0:T(4,128)}, f32[8]{0:T(128)}, f32[8]{0:T(128)}) custom-call(f32[32,128]{1,0:T(8,128)S(1)} %get-tuple-element.53.keep_ref, bf16[48,128]{1,0:T(8,128)(2,1)S(1)} %collective-permute-done.7.got_ref, f32[8,128]{1,0:T(8,128)S(1)} %get-tuple-element.55.mass_in, f32[8,128]{1,0:T(8,128)S(1)} %get-tuple-element.56.loglik_in), custom_call_target="tpu_custom_call" | custom-call | bytes 1048576 | tf_op jit(solution)/shard_map/last/pallas_call | solution.py:409
  (2 shorter events, 0.1 us)
Async XLA Ops:
  0.6 6.6 %collective-permute-start = (bf16[8,64,128]{2,1,0:T(8,128)(2,1)}, bf16[8,64,128]{2,1,0:T(8,128)(2,1)S(1)}, u32[]{:S(2)}, u32[]{:S(2)}) collective-permute-start(bf16[8,64,128]{2,1,0:T(8,128)(2,1)} %refs_4_.1), channel_id=1, source_target_pairs={{0,3},{1,2},{2,1},{3,0},{4,7},{5,6},{6,5},{7,4},{8,11},{9,10},{10,... | collective-permute-start | bytes 393224 | tf_op jit(solution)/shard_map/ppermute | solution.py:423
  5.3 5.0 %collective-permute-start.1 = (f32[8,128]{1,0:T(8,128)S(1)}, f32[8,128]{1,0:T(8,128)S(1)}, u32[]{:S(2)}, u32[]{:S(2)}) collective-permute-start(f32[8,128]{1,0:T(8,128)S(1)} %get-tuple-element.31.lse_ref.refs_0_), channel_id=1, source_target_pairs={{0,3},{1,2},{2,1},{3,0},{4,7},{5,6},{6,5},{7,4},{8,11},{9,10},{10,... | collective-permute-start | bytes 12296 | tf_op jit(solution)/shard_map/ppermute | solution.py:423
  8.2 3.4 %collective-permute-start.2 = (f32[8,128]{1,0:T(8,128)S(1)}, f32[8,128]{1,0:T(8,128)S(1)}, u32[]{:S(2)}, u32[]{:S(2)}) collective-permute-start(f32[8,128]{1,0:T(8,128)S(1)} %get-tuple-element.42.refs_5_), channel_id=1, source_target_pairs={{0,3},{1,2},{2,1},{3,0},{4,7},{5,6},{6,5},{7,4},{8,11},{9,10},{10,... | collective-permute-start | bytes 12296 | tf_op jit(solution)/shard_map/ppermute | solution.py:423
  11.9 1.3 %collective-permute-start.3 = (bf16[272,128]{1,0:T(8,128)(2,1)S(1)}, bf16[272,128]{1,0:T(8,128)(2,1)S(1)}, u32[]{:S(2)}, u32[]{:S(2)}) collective-permute-start(bf16[272,128]{1,0:T(8,128)(2,1)S(1)} %get-tuple-element.46), channel_id=1, source_target_pairs={{0,2},{2,0},{4,6},{6,4},{8,10},{10,8},{12,14},{14,12},{16,18},{18,... | collective-permute-start | bytes 208904 | tf_op jit(solution)/shard_map/ppermute | solution.py:494
  13.2 3.3 %collective-permute-start.4 = (bf16[80,128]{1,0:T(8,128)(2,1)S(1)}, bf16[80,128]{1,0:T(8,128)(2,1)S(1)}, u32[]{:S(2)}, u32[]{:S(2)}) collective-permute-start(bf16[80,128]{1,0:T(8,128)(2,1)S(1)} %get-tuple-element.50), channel_id=1, source_target_pairs={{0,6},{2,4},{4,2},{6,0},{8,14},{10,12},{12,10},{14,8},{16,22},{18,... | collective-permute-start | bytes 61448 | tf_op jit(solution)/shard_map/ppermute | solution.py:494
  15.0 4.7 %collective-permute-start.5 = (bf16[80,128]{1,0:T(8,128)(2,1)S(1)}, bf16[80,128]{1,0:T(8,128)(2,1)S(1)}, u32[]{:S(2)}, u32[]{:S(2)}) collective-permute-start(bf16[80,128]{1,0:T(8,128)(2,1)S(1)} %get-tuple-element.51), channel_id=1, source_target_pairs={{0,12},{2,14},{4,8},{6,10},{8,4},{10,6},{12,0},{14,2},{16,28},{18,... | collective-permute-start | bytes 61448 | tf_op jit(solution)/shard_map/ppermute | solution.py:494
  16.5 3.2 %collective-permute-start.6 = (bf16[80,128]{1,0:T(8,128)(2,1)S(1)}, bf16[80,128]{1,0:T(8,128)(2,1)S(1)}, u32[]{:S(2)}, u32[]{:S(2)}) collective-permute-start(bf16[80,128]{1,0:T(8,128)(2,1)S(1)} %get-tuple-element.52), channel_id=1, source_target_pairs={{0,10},{2,8},{4,14},{6,12},{8,2},{10,0},{12,6},{14,4},{16,26},{18,... | collective-permute-start | bytes 61448 | tf_op jit(solution)/shard_map/ppermute | solution.py:494
  19.7 4.1 %collective-permute-start.7 = (bf16[48,128]{1,0:T(8,128)(2,1)S(1)}, bf16[48,128]{1,0:T(8,128)(2,1)S(1)}, u32[]{:S(2)}, u32[]{:S(2)}) collective-permute-start(bf16[48,128]{1,0:T(8,128)(2,1)S(1)} %get-tuple-element.54), channel_id=1, source_target_pairs={{0,18},{2,16},{4,22},{6,20},{8,26},{10,24},{12,30},{14,28},{16,2},... | collective-permute-start | bytes 36872 | tf_op jit(solution)/shard_map/ppermute | solution.py:494

commit v7 on v5

--- a/solution.py
+++ b/solution.py
@@ -500,7 +500,7 @@
         [shape((height, width), F32)] + [sent(1, height)] * 3 + [shape((8, 128), F32)],
         (keep, got, mass), [], name="quarter",
     )
-    gots = [exchange(sends[turn - 1], turn << 1) for turn in (1, 3, 2)]
+    gots = [exchange(sends[turn - 1], turn << 1) for turn in (3, 2, 1)]
     for b in range(3, steps):
         height = keep.shape[0] // 2
         keep, send, mass = call(

time: 24.8 us -> 24.7 us (level)
  waiting for transfers between devices: 7.11 us -> 6.68 us
  starting transfers between devices: 10.7 us -> 11.1 us
    ppermute x5, waiting for transfers between devices: 6.02 us -> 5.59 us  [exchange(): return lax.ppermute(value, 'dom', [(i, i ^ step) for i in range(n_dom)])]
    ppermute x5, starting transfers between devices: 6.08 us -> 6.43 us  [exchange(): return lax.ppermute(value, 'dom', [(i, i ^ step) for i in range(n_dom)])]
where the time goes in v7:
time: 24.7 us; the launch traced here: 24.6 us
  starting transfers between devices  11.1 us (45%)
  waiting for transfers between devices  6.68 us (27%)
  Pallas kernels  6.14 us (25%)
  between operations  0.68 us (3%)
    ppermute x5, starting transfers between devices, exchange(): return lax.ppermute(value, 'dom', [(i, i ^ step) for i in range(n_dom)])  6.43 us
    pallas_call x8, Pallas kernels, call(): pl.pallas_call(kernel, out_shape=tuple(outs), in_specs=specs or [vmem] *...  6.14 us
    ppermute x5, waiting for transfers between devices, exchange(): return lax.ppermute(value, 'dom', [(i, i ^ step) for i in range(n_dom)])  5.59 us
    ppermute x3, starting transfers between devices, swap(): return lax.ppermute(value, ('dom', 'orient'), pairs)  4.64 us
    ppermute x3, waiting for transfers between devices, swap(): return lax.ppermute(value, ('dom', 'orient'), pairs)  1.09 us
  transfers between devices with their start and end apart: 8, of which 6 were waited for; matrix products, arithmetic and copies ran while one was open for 0% of the time, Pallas kernels for 21%

profile of v7, /device:TPU:0, one launch (start us, length us, event | category | flops | bytes accessed | tf_op | source)
XLA Modules:
  0.0 24.6 jit_solution(4645971139323013064)
XLA Ops:
  0.6 2.4 %collective-permute-start = (bf16[8,64,128]{2,1,0:T(8,128)(2,1)}, bf16[8,64,128]{2,1,0:T(8,128)(2,1)S(1)}, u32[]{:S(2)}, u32[]{:S(2)}) collective-permute-start(bf16[8,64,128]{2,1,0:T(8,128)(2,1)} %refs_4_.1), channel_id=1, source_target_pairs={{0,3},{1,2},{2,1},{3,0},{4,7},{5,6},{6,5},{7,4},{8,11},{9,10},{10,... | collective-permute-start | bytes 393224 | tf_op jit(solution)/shard_map/ppermute | solution.py:423
  3.1 2.2 %first.1 = (f32[8,16,128]{2,1,0:T(8,128)S(1)}, f32[8,128]{1,0:T(8,128)S(1)}, f32[8,64,128]{2,1,0:T(8,128)S(1)}, f32[8,64,128]{2,1,0:T(8,128)S(1)}, f32[8,128]{1,...) custom-call(s32[16]{0:T(128)} %refs_0_.1, ...), custom_call_target="tpu_custom_call" | custom-call | flops 268435456 | bytes 1048576 | tf_op jit(solution)/shard_map/first/pallas_call | solution.py:409
  5.3 0.1 collective-permute-start.1
  5.4 1.3 %own.1.own_ref = f32[4096,128]{1,0:T(8,128)S(1)} custom-call(f32[8,16,128]{2,1,0:T(8,128)S(1)} %get-tuple-element.30.logits_ref, f32[8,128]{1,0:T(8,128)S(1)} %get-tuple-element.31.lse_ref.refs_0_, bf16[8,64,128]{2,1,0:T(8,128)(2,1)S(1)} %get-tuple-element.32.x_ref, s32[64,64]{1,0:T(8,128)S(1)} %get-tuple-element.33.mask_ref.refs_2_, ...), custom_call_target="tpu_custom_call" | custom-call | flops 268435456 | bytes 1048576 | tf_op jit(solution)/shard_map/own/pallas_call | solution.py:409
  6.7 0.6 %collective-permute-done.x_ref.refs_1_ = bf16[8,64,128]{2,1,0:T(8,128)(2,1)S(1)} collective-permute-done((bf16[8,64,128]{2,1,0:T(8,128)(2,1)}, bf16[8,64,128]{2,1,0:T(8,128)(2,1)S(1)}, u32[]{:S(2)}, u32[]{:S(2)}) %collective-permute-start) | collective-permute-done | bytes 131104 | tf_op jit(solution)/shard_map/ppermute | solution.py:423
  7.3 0.9 %score.1 = (f32[8,16,128]{2,1,0:T(8,128)S(1)}, f32[8,128]{1,0:T(8,128)S(1)}) custom-call(bf16[8,64,128]{2,1,0:T(8,128)(2,1)S(1)} %collective-permute-done.x_ref.refs_1_, f32[8,64,128]{2,1,0:T(8,128)S(1)} %get-tuple-element.36.first, f32[8,64,128]{2,1,0:T(8,128)S(1)} %get-tuple-element.37.second, f32[8,128]{1,0:T(8,128)S(1)} %get-tuple-element.38.bias_ref, ...), custom_call_target="tpu_custom_call" | custom-call | flops 268435456 | bytes 1048576 | tf_op jit(solution)/shard_map/score/pallas_call | solution.py:409
  8.2 2.1 %collective-permute-start.2 = (f32[8,128]{1,0:T(8,128)S(1)}, f32[8,128]{1,0:T(8,128)S(1)}, u32[]{:S(2)}, u32[]{:S(2)}) collective-permute-start(f32[8,128]{1,0:T(8,128)S(1)} %get-tuple-element.42.refs_5_), channel_id=1, source_target_pairs={{0,3},{1,2},{2,1},{3,0},{4,7},{5,6},{6,5},{7,4},{8,11},{9,10},{10,... | collective-permute-start | bytes 12296 | tf_op jit(solution)/shard_map/ppermute | solution.py:423
  10.3 0.0 collective-permute-done.1.refs_6_
  10.3 0.8 %back.1 = (f32[512,128]{1,0:T(8,128)S(1)}, f32[8,128]{1,0:T(8,128)S(1)}) custom-call(f32[8,16,128]{2,1,0:T(8,128)S(1)} %get-tuple-element.41.refs_0_, bf16[8,64,128]{2,1,0:T(8,128)(2,1)S(1)} %collective-permute-done.x_ref.refs_1_, s32[64,64]{1,0:T(8,128)S(1)} %get-tuple-element.33.mask_ref.refs_2_, bf16[128,2048]{1,0:T(8,128)(2,1)S(1)} %get-tuple-element.34.rows_ref.refs_3_, ...), custom_call_target="tpu_custom_call" | custom-call | flops 268435456 | bytes 1048576 | tf_op jit(solution)/shard_map/back/pallas_call | solution.py:409
  11.1 0.5 %collective-permute-done.2.refs_1_ = f32[8,128]{1,0:T(8,128)S(1)} collective-permute-done((f32[8,128]{1,0:T(8,128)S(1)}, f32[8,128]{1,0:T(8,128)S(1)}, u32[]{:S(2)}, u32[]{:S(2)}) %collective-permute-start.2) | collective-permute-done | bytes 4128 | tf_op jit(solution)/shard_map/ppermute | solution.py:423
  11.6 0.2 last_back.1
  11.8 0.4 %collective-permute-start.3 = (f32[264,128]{1,0:T(8,128)S(1)}, f32[264,128]{1,0:T(8,128)S(1)}, u32[]{:S(2)}, u32[]{:S(2)}) collective-permute-start(f32[264,128]{1,0:T(8,128)S(1)} %get-tuple-element.46), channel_id=1, source_target_pairs={{0,2},{2,0},{4,6},{6,4},{8,10},{10,8},{12,14},{14,12},{16,18},{18,... | collective-permute-start | bytes 405512 | tf_op jit(solution)/shard_map/ppermute | solution.py:494
  12.2 1.0 %collective-permute-done.3.got_ref = f32[264,128]{1,0:T(8,128)S(1)} collective-permute-done((f32[264,128]{1,0:T(8,128)S(1)}, f32[264,128]{1,0:T(8,128)S(1)}, u32[]{:S(2)}, u32[]{:S(2)}) %collective-permute-start.3) | collective-permute-done | bytes 135200 | tf_op jit(solution)/shard_map/ppermute | solution.py:494
  13.3 3.0 %collective-permute-start.4 = (bf16[80,128]{1,0:T(8,128)(2,1)S(1)}, bf16[80,128]{1,0:T(8,128)(2,1)S(1)}, u32[]{:S(2)}, u32[]{:S(2)}) collective-permute-start(bf16[80,128]{1,0:T(8,128)(2,1)S(1)} %get-tuple-element.50), channel_id=1, source_target_pairs={{0,12},{2,14},{4,8},{6,10},{8,4},{10,6},{12,0},{14,2},{16,28},{18,... | collective-permute-start | bytes 61448 | tf_op jit(solution)/shard_map/ppermute | solution.py:494
  16.3 0.0 collective-permute-start.5
  16.3 0.4 %collective-permute-start.6 = (bf16[80,128]{1,0:T(8,128)(2,1)S(1)}, bf16[80,128]{1,0:T(8,128)(2,1)S(1)}, u32[]{:S(2)}, u32[]{:S(2)}) collective-permute-start(bf16[80,128]{1,0:T(8,128)(2,1)S(1)} %get-tuple-element.52), channel_id=1, source_target_pairs={{0,6},{2,4},{4,2},{6,0},{8,14},{10,12},{12,10},{14,8},{16,22},{18,... | collective-permute-start | bytes 61448 | tf_op jit(solution)/shard_map/ppermute | solution.py:494
  16.7 1.4 %collective-permute-done.4.refs_0_ = bf16[80,128]{1,0:T(8,128)(2,1)S(1)} collective-permute-done((bf16[80,128]{1,0:T(8,128)(2,1)S(1)}, bf16[80,128]{1,0:T(8,128)(2,1)S(1)}, u32[]{:S(2)}, u32[]{:S(2)}) %collective-permute-start.4) | collective-permute-done | bytes 20512 | tf_op jit(solution)/shard_map/ppermute | solution.py:494
  18.1 1.6 %collective-permute-done.5.refs_1_ = bf16[80,128]{1,0:T(8,128)(2,1)S(1)} collective-permute-done((bf16[80,128]{1,0:T(8,128)(2,1)S(1)}, bf16[80,128]{1,0:T(8,128)(2,1)S(1)}, u32[]{:S(2)}, u32[]{:S(2)}) %collective-permute-start.5) | collective-permute-done | bytes 20512 | tf_op jit(solution)/shard_map/ppermute | solution.py:494
  19.7 0.0 collective-permute-done.6.refs_2_
  19.7 2.7 %collective-permute-start.7 = (f32[40,128]{1,0:T(8,128)S(1)}, f32[40,128]{1,0:T(8,128)S(1)}, u32[]{:S(2)}, u32[]{:S(2)}) collective-permute-start(f32[40,128]{1,0:T(8,128)S(1)} %get-tuple-element.54), channel_id=1, source_target_pairs={{0,18},{2,16},{4,22},{6,20},{8,26},{10,24},{12,30},{14,28},{16,2},... | collective-permute-start | bytes 61448 | tf_op jit(solution)/shard_map/ppermute | solution.py:494
  22.4 1.5 %collective-permute-done.7.got_ref = f32[40,128]{1,0:T(8,128)S(1)} collective-permute-done((f32[40,128]{1,0:T(8,128)S(1)}, f32[40,128]{1,0:T(8,128)S(1)}, u32[]{:S(2)}, u32[]{:S(2)}) %collective-permute-start.7) | collective-permute-done | bytes 20512 | tf_op jit(solution)/shard_map/ppermute | solution.py:494
  23.9 0.6 %last.1 = (f32[8,4,128]{2,1,0:T(4,128)}, f32[8]{0:T(128)}, f32[8]{0:T(128)}) custom-call(f32[32,128]{1,0:T(8,128)S(1)} %get-tuple-element.53.keep_ref, f32[40,128]{1,0:T(8,128)S(1)} %collective-permute-done.7.got_ref, f32[8,128]{1,0:T(8,128)S(1)} %get-tuple-element.55.mass_in, f32[8,128]{1,0:T(8,128)S(1)} %get-tuple-element.56.loglik_in), custom_call_target="tpu_custom_call" | custom-call | bytes 1048576 | tf_op jit(solution)/shard_map/last/pallas_call | solution.py:409
  (2 shorter events, 0.0 us)
Async XLA Ops:
  0.6 6.6 %collective-permute-start = (bf16[8,64,128]{2,1,0:T(8,128)(2,1)}, bf16[8,64,128]{2,1,0:T(8,128)(2,1)S(1)}, u32[]{:S(2)}, u32[]{:S(2)}) collective-permute-start(bf16[8,64,128]{2,1,0:T(8,128)(2,1)} %refs_4_.1), channel_id=1, source_target_pairs={{0,3},{1,2},{2,1},{3,0},{4,7},{5,6},{6,5},{7,4},{8,11},{9,10},{10,... | collective-permute-start | bytes 393224 | tf_op jit(solution)/shard_map/ppermute | solution.py:423
  5.3 5.0 %collective-permute-start.1 = (f32[8,128]{1,0:T(8,128)S(1)}, f32[8,128]{1,0:T(8,128)S(1)}, u32[]{:S(2)}, u32[]{:S(2)}) collective-permute-start(f32[8,128]{1,0:T(8,128)S(1)} %get-tuple-element.31.lse_ref.refs_0_), channel_id=1, source_target_pairs={{0,3},{1,2},{2,1},{3,0},{4,7},{5,6},{6,5},{7,4},{8,11},{9,10},{10,... | collective-permute-start | bytes 12296 | tf_op jit(solution)/shard_map/ppermute | solution.py:423
  8.2 3.4 %collective-permute-start.2 = (f32[8,128]{1,0:T(8,128)S(1)}, f32[8,128]{1,0:T(8,128)S(1)}, u32[]{:S(2)}, u32[]{:S(2)}) collective-permute-start(f32[8,128]{1,0:T(8,128)S(1)} %get-tuple-element.42.refs_5_), channel_id=1, source_target_pairs={{0,3},{1,2},{2,1},{3,0},{4,7},{5,6},{6,5},{7,4},{8,11},{9,10},{10,... | collective-permute-start | bytes 12296 | tf_op jit(solution)/shard_map/ppermute | solution.py:423
  11.8 1.4 %collective-permute-start.3 = (f32[264,128]{1,0:T(8,128)S(1)}, f32[264,128]{1,0:T(8,128)S(1)}, u32[]{:S(2)}, u32[]{:S(2)}) collective-permute-start(f32[264,128]{1,0:T(8,128)S(1)} %get-tuple-element.46), channel_id=1, source_target_pairs={{0,2},{2,0},{4,6},{6,4},{8,10},{10,8},{12,14},{14,12},{16,18},{18,... | collective-permute-start | bytes 405512 | tf_op jit(solution)/shard_map/ppermute | solution.py:494
  13.3 4.8 %collective-permute-start.4 = (bf16[80,128]{1,0:T(8,128)(2,1)S(1)}, bf16[80,128]{1,0:T(8,128)(2,1)S(1)}, u32[]{:S(2)}, u32[]{:S(2)}) collective-permute-start(bf16[80,128]{1,0:T(8,128)(2,1)S(1)} %get-tuple-element.50), channel_id=1, source_target_pairs={{0,12},{2,14},{4,8},{6,10},{8,4},{10,6},{12,0},{14,2},{16,28},{18,... | collective-permute-start | bytes 61448 | tf_op jit(solution)/shard_map/ppermute | solution.py:494
  16.3 3.4 %collective-permute-start.5 = (bf16[80,128]{1,0:T(8,128)(2,1)S(1)}, bf16[80,128]{1,0:T(8,128)(2,1)S(1)}, u32[]{:S(2)}, u32[]{:S(2)}) collective-permute-start(bf16[80,128]{1,0:T(8,128)(2,1)S(1)} %get-tuple-element.51), channel_id=1, source_target_pairs={{0,10},{2,8},{4,14},{6,12},{8,2},{10,0},{12,6},{14,4},{16,26},{18,... | collective-permute-start | bytes 61448 | tf_op jit(solution)/shard_map/ppermute | solution.py:494
  16.3 3.4 %collective-permute-start.6 = (bf16[80,128]{1,0:T(8,128)(2,1)S(1)}, bf16[80,128]{1,0:T(8,128)(2,1)S(1)}, u32[]{:S(2)}, u32[]{:S(2)}) collective-permute-start(bf16[80,128]{1,0:T(8,128)(2,1)S(1)} %get-tuple-element.52), channel_id=1, source_target_pairs={{0,6},{2,4},{4,2},{6,0},{8,14},{10,12},{12,10},{14,8},{16,22},{18,... | collective-permute-start | bytes 61448 | tf_op jit(solution)/shard_map/ppermute | solution.py:494
  19.7 4.2 %collective-permute-start.7 = (f32[40,128]{1,0:T(8,128)S(1)}, f32[40,128]{1,0:T(8,128)S(1)}, u32[]{:S(2)}, u32[]{:S(2)}) collective-permute-start(f32[40,128]{1,0:T(8,128)S(1)} %get-tuple-element.54), channel_id=1, source_target_pairs={{0,18},{2,16},{4,22},{6,20},{8,26},{10,24},{12,30},{14,28},{16,2},... | collective-permute-start | bytes 61448 | tf_op jit(solution)/shard_map/ppermute | solution.py:494
